TPU v7x, 32 devices: a whole 2x2x4 slice. The times are simulated.
32 devices in a mesh: wide: 16 (over z, y, x), narrow: 2 (over core).
Axes of the slice: x: 2, y: 2, z: 4, core: 2. Of those that a mesh axis runs over, the one named last changes fastest.
Arguments:
- tokens: bfloat16 [65536, 768], P(('wide', 'narrow')), may hold values from -6 to 6
- cotangent: bfloat16 [65536, 768], P(('wide', 'narrow')), may hold values from -6 to 6
- size_tags: int32 [16], P('wide'), may hold values from 1024 to 4096, as said below
- timesteps: int32 [64], P(('wide', 'narrow')), may hold values from 0 to 999, as said below
- labels: int32 [64], P(('wide', 'narrow')), may hold values from 0 to 999, as said below
- modulator: bfloat16 [768, 4608], replicated, may hold values from -0.21875 to 0.21875
- class_table: bfloat16 [768, 1000], replicated, may hold values from -6 to 6
- mix_kernel: bfloat16 [768, 9], replicated, may hold values from -2 to 2
- heads_in: bfloat16 [768, 2304], P(None, 'narrow'), may hold values from -0.21875 to 0.21875
- heads_out: bfloat16 [768, 768], P('narrow'), may hold values from -1.25 to 1.25
- up_weight: bfloat16 [768, 3072], P(None, 'narrow'), may hold values from -0.21875 to 0.21875
- hidden_kernel: bfloat16 [3072, 9], P('narrow'), may hold values from -2 to 2
- down_weight: bfloat16 [3072, 768], P('narrow'), may hold values from -0.109375 to 0.109375
- modulator_master: float32 [768, 4608], P(('wide', 'narrow')), may hold values from -0.21875 to 0.21875
- modulator_first: float32 [768, 4608], P(('wide', 'narrow')), may hold values from -6 to 6
- modulator_second: float32 [768, 4608], P(('wide', 'narrow')), may hold values from 1 to 4
- class_table_master: float32 [768, 1000], P(('wide', 'narrow')), may hold values from -6 to 6
- class_table_first: float32 [768, 1000], P(('wide', 'narrow')), may hold values from -0.625 to 0.625
- class_table_second: float32 [768, 1000], P(('wide', 'narrow')), may hold values from 0.05 to 0.2
- mix_kernel_master: float32 [768, 9], P(('wide', 'narrow')), may hold values from -2 to 2
- mix_kernel_first: float32 [768, 9], P(('wide', 'narrow')), may hold values from -6 to 6
- mix_kernel_second: float32 [768, 9], P(('wide', 'narrow')), may hold values from 1 to 4
- heads_in_master: float32 [768, 2304], P('wide', 'narrow'), may hold values from -0.21875 to 0.21875
- heads_in_first: float32 [768, 2304], P('wide', 'narrow'), may hold values from -6 to 6
- heads_in_second: float32 [768, 2304], P('wide', 'narrow'), may hold values from 1 to 4
- heads_out_master: float32 [768, 768], P(('narrow', 'wide')), may hold values from -1.25 to 1.25
- heads_out_first: float32 [768, 768], P(('narrow', 'wide')), may hold values from -6 to 6
- heads_out_second: float32 [768, 768], P(('narrow', 'wide')), may hold values from 1 to 4
- up_weight_master: float32 [768, 3072], P('wide', 'narrow'), may hold values from -0.21875 to 0.21875
- up_weight_first: float32 [768, 3072], P('wide', 'narrow'), may hold values from -6 to 6
- up_weight_second: float32 [768, 3072], P('wide', 'narrow'), may hold values from 0.1 to 0.4
- hidden_kernel_master: float32 [3072, 9], P(('narrow', 'wide')), may hold values from -2 to 2
- hidden_kernel_first: float32 [3072, 9], P(('narrow', 'wide')), may hold values from -6 to 6
- hidden_kernel_second: float32 [3072, 9], P(('narrow', 'wide')), may hold values from 0.05 to 0.2
- down_weight_master: float32 [3072, 768], P(('narrow', 'wide')), may hold values from -0.109375 to 0.109375
- down_weight_first: float32 [3072, 768], P(('narrow', 'wide')), may hold values from -6 to 6
- down_weight_second: float32 [3072, 768], P(('narrow', 'wide')), may hold values from 1 to 4
Outputs:
- output: bfloat16 [65536, 768], P(('wide', 'narrow'))
- input_grad: bfloat16 [65536, 768], P(('wide', 'narrow'))
- grad_norm: float32 [], replicated
- modulator_first_new: float32 [768, 4608], P(('wide', 'narrow'))
- modulator_second_new: float32 [768, 4608], P(('wide', 'narrow'))
- modulator_master_new: float32 [768, 4608], P(('wide', 'narrow'))
- modulator_copy: bfloat16 [768, 4608], P(('wide', 'narrow'))
- class_table_first_new: float32 [768, 1000], P(('wide', 'narrow'))
- class_table_second_new: float32 [768, 1000], P(('wide', 'narrow'))
- class_table_master_new: float32 [768, 1000], P(('wide', 'narrow'))
- class_table_copy: bfloat16 [768, 1000], P(('wide', 'narrow'))
- mix_kernel_first_new: float32 [768, 9], P(('wide', 'narrow'))
- mix_kernel_second_new: float32 [768, 9], P(('wide', 'narrow'))
- mix_kernel_master_new: float32 [768, 9], P(('wide', 'narrow'))
- mix_kernel_copy: bfloat16 [768, 9], P(('wide', 'narrow'))
- heads_in_first_new: float32 [768, 2304], P('wide', 'narrow')
- heads_in_second_new: float32 [768, 2304], P('wide', 'narrow')
- heads_in_master_new: float32 [768, 2304], P('wide', 'narrow')
- heads_in_copy: bfloat16 [768, 2304], P('wide', 'narrow')
- heads_out_first_new: float32 [768, 768], P(('narrow', 'wide'))
- heads_out_second_new: float32 [768, 768], P(('narrow', 'wide'))
- heads_out_master_new: float32 [768, 768], P(('narrow', 'wide'))
- heads_out_copy: bfloat16 [768, 768], P(('narrow', 'wide'))
- up_weight_first_new: float32 [768, 3072], P('wide', 'narrow')
- up_weight_second_new: float32 [768, 3072], P('wide', 'narrow')
- up_weight_master_new: float32 [768, 3072], P('wide', 'narrow')
- up_weight_copy: bfloat16 [768, 3072], P('wide', 'narrow')
- hidden_kernel_first_new: float32 [3072, 9], P(('narrow', 'wide'))
- hidden_kernel_second_new: float32 [3072, 9], P(('narrow', 'wide'))
- hidden_kernel_master_new: float32 [3072, 9], P(('narrow', 'wide'))
- hidden_kernel_copy: bfloat16 [3072, 9], P(('narrow', 'wide'))
- down_weight_first_new: float32 [3072, 768], P(('narrow', 'wide'))
- down_weight_second_new: float32 [3072, 768], P(('narrow', 'wide'))
- down_weight_master_new: float32 [3072, 768], P(('narrow', 'wide'))
- down_weight_copy: bfloat16 [3072, 768], P(('narrow', 'wide'))
- modulation_two_grad: float32 [64, 1536], P(('wide', 'narrow'))
Inputs may be any that keep to these rules, and one draw needn't show every extreme that they name: `size_tags`: each tag is 1024 or 4096; both occur in every draw. `timesteps`: the four frames of a quad tagged 4 * 32 * 32 carry the same timestep. `labels`: the four frames of a quad tagged 4 * 32 * 32 carry the same label.
All inputs are finite; a program needn't handle non-finite values.
Results may differ from a plain program's by a relative error of at most 0.03.
Values may be sent and summed in bfloat16 or wider, within the bound.
A program may use at most 576 MiB of HBM per device.

v0:
```python
import jax
import jax.numpy as jnp
from jax import lax
from jax.sharding import PartitionSpec as P

D = 768
HS = 64
FF = 3072
SIDE = 32
STEP = 10
PARAMS = 11419392


NORM_EPS = 1e-06
BETA_ONE = 0.5
BETA_TWO = 0.5
ADAM_EPS = 1e-08
WEIGHT_DECAY = 0.01
HIGHEST_PRECISION = lax.Precision.HIGHEST


def timestep_code(stamps, channels):
    half_dim = channels // 2
    scales = jnp.exp(-jnp.log(10000.0) * jnp.arange(half_dim, dtype=jnp.float32) / half_dim)
    angles = stamps.astype(jnp.float32)[:, None] * scales[None, :]
    return jnp.concatenate([jnp.cos(angles), jnp.sin(angles)], axis=1)


def layer_norm(fields):
    center = fields - jnp.mean(fields, -1, keepdims=True)
    inverse = lax.rsqrt(jnp.mean(center * center, -1, keepdims=True) + NORM_EPS)
    return (center * inverse, inverse)


def norm_back(grad_hat, normed, inverse):
    return inverse * (
        grad_hat
        - jnp.mean(grad_hat, -1, keepdims=True)
        - normed * jnp.mean(grad_hat * normed, -1, keepdims=True)
    )


def as_images(fields, big_flag, grid_side):
    channels = fields.shape[-1]
    if big_flag:
        return fields.reshape(1, 2 * grid_side, 2 * grid_side, channels)
    return fields.reshape(4, grid_side, grid_side, channels)


def conv_image(images, kernel):
    padded = jnp.pad(images, ((0, 0), (1, 1), (1, 1), (0, 0)))
    row_count, col_count = (images.shape[1], images.shape[2])
    result = jnp.zeros_like(images)
    for offset in range(9):
        result = (
            result
            + padded[
                :, offset // 3 : offset // 3 + row_count, offset % 3 : offset % 3 + col_count, :
            ]
            * kernel[:, offset]
        )
    return result


def conv_taps(images, gradients):
    padded = jnp.pad(images, ((0, 0), (1, 1), (1, 1), (0, 0)))
    row_count, col_count = (images.shape[1], images.shape[2])
    columns = [
        jnp.sum(
            padded[:, offset // 3 : offset // 3 + row_count, offset % 3 : offset % 3 + col_count, :]
            * gradients,
            axis=(0, 1, 2),
        )
        for offset in range(9)
    ]
    return jnp.stack(columns, axis=1)


def quad_conv(fields, kernel, big_flag, grid_side):

    def branch(static_flag):

        def run_branch(inputs):
            return conv_image(as_images(inputs, static_flag, grid_side), kernel).reshape(
                inputs.shape
            )

        return run_branch

    return lax.cond(big_flag, branch(True), branch(False), fields)


def quad_taps(fields, gradients, big_flag, grid_side):

    def branch(static_flag):

        def run_branch(operands):
            return conv_taps(
                as_images(operands[0], static_flag, grid_side),
                as_images(operands[1], static_flag, grid_side),
            )

        return run_branch

    return lax.cond(big_flag, branch(True), branch(False), (fields, gradients))


def to_groups(fields, big_flag, grid_side):
    channels = fields.shape[-1]
    half_side = grid_side // 2

    def to_large_case(inputs):
        return (
            inputs.reshape(grid_side, 2, grid_side, 2, channels)
            .transpose(1, 3, 0, 2, 4)
            .reshape(4, grid_side * grid_side, channels)
        )

    def to_small_case(inputs):
        return (
            inputs.reshape(4, half_side, 2, half_side, 2, channels)
            .transpose(2, 4, 0, 1, 3, 5)
            .reshape(4, grid_side * grid_side, channels)
        )

    return lax.cond(big_flag, to_large_case, to_small_case, fields)


def from_groups(blocks, big_flag, grid_side):
    channels = blocks.shape[-1]
    half_side = grid_side // 2

    def from_large_case(inputs):
        return (
            inputs.reshape(2, 2, grid_side, grid_side, channels)
            .transpose(2, 0, 3, 1, 4)
            .reshape(-1, channels)
        )

    def from_small_case(inputs):
        return (
            inputs.reshape(2, 2, 4, half_side, half_side, channels)
            .transpose(2, 3, 0, 4, 1, 5)
            .reshape(-1, channels)
        )

    return lax.cond(big_flag, from_large_case, from_small_case, blocks)


def attend(queries, key_rows, values, factor):
    scores = (
        jnp.einsum("blhe,bmhe->bhlm", queries, key_rows, preferred_element_type=jnp.float32)
        * factor
    )
    highest = jnp.max(scores, -1, keepdims=True)
    weights = jnp.exp(scores - highest)
    totals = jnp.sum(weights, -1, keepdims=True)
    shares = (weights / totals).astype(jnp.bfloat16)
    mixture = jnp.einsum("bhlm,bmhe->blhe", shares, values, preferred_element_type=jnp.float32)
    return (mixture, (highest + jnp.log(totals))[..., 0])


def attend_back(queries, key_rows, values, grad_mixture, log_sums, factor):
    scores = (
        jnp.einsum("blhe,bmhe->bhlm", queries, key_rows, preferred_element_type=jnp.float32)
        * factor
    )
    shares = jnp.exp(scores - log_sums[..., None])
    grad_values = jnp.einsum(
        "bhlm,blhe->bmhe",
        shares.astype(jnp.bfloat16),
        grad_mixture,
        preferred_element_type=jnp.float32,
    )
    grad_shares = jnp.einsum(
        "blhe,bmhe->bhlm", grad_mixture, values, preferred_element_type=jnp.float32
    )
    inner_sum = jnp.sum(shares * grad_shares, -1, keepdims=True)
    grad_scores = (shares * (grad_shares - inner_sum)).astype(jnp.bfloat16)
    grad_queries = (
        jnp.einsum("bhlm,bmhe->blhe", grad_scores, key_rows, preferred_element_type=jnp.float32)
        * factor
    )
    grad_keys = (
        jnp.einsum("bhlm,blhe->bmhe", grad_scores, queries, preferred_element_type=jnp.float32)
        * factor
    )
    return (grad_queries, grad_keys, grad_values)


def group_forward(group_rows, big_flag, head_size):
    row_count = group_rows.shape[0]
    divided = group_rows.reshape(row_count, -1, 3, head_size)
    head_count = divided.shape[1]
    factor = head_size ** (-0.5)

    def branch(pieces):

        def run_branch(members):
            shaped = [
                member.reshape(pieces, row_count // pieces, head_count, head_size)
                for member in members
            ]
            mixture, log_sums = attend(shaped[0], shaped[1], shaped[2], factor)
            return (mixture.reshape(row_count, head_count * head_size), log_sums.reshape(-1))

        return run_branch

    return lax.cond(
        big_flag, branch(1), branch(4), (divided[:, :, 0], divided[:, :, 1], divided[:, :, 2])
    )


def group_back(group_rows, log_sums, grad_mixture, big_flag, head_size):
    row_count = group_rows.shape[0]
    divided = group_rows.reshape(row_count, -1, 3, head_size)
    head_count = divided.shape[1]
    factor = head_size ** (-0.5)

    def branch(pieces):

        def run_branch(members):
            shaped = [
                member.reshape(pieces, row_count // pieces, head_count, head_size)
                for member in members[:4]
            ]
            sums_here = members[4].reshape(pieces, head_count, row_count // pieces)
            grad_triple = attend_back(shaped[0], shaped[1], shaped[2], shaped[3], sums_here, factor)
            stacked = jnp.stack(
                [member.reshape(row_count, head_count, head_size) for member in grad_triple], axis=2
            )
            return stacked.reshape(row_count, -1).astype(jnp.bfloat16)

        return run_branch

    operands = (
        divided[:, :, 0],
        divided[:, :, 1],
        divided[:, :, 2],
        grad_mixture.reshape(row_count, head_count, head_size),
        log_sums,
    )
    return lax.cond(big_flag, branch(1), branch(4), operands)


def own_rows(full_grad, block_index, block_total):
    row_count = full_grad.shape[0] // block_total
    return lax.dynamic_slice_in_dim(full_grad, block_index * row_count, row_count, 0)


def square_sum(arrays):
    total_square = jnp.float32(0.0)
    for member in arrays:
        total_square = total_square + jnp.sum(member * member)
    return total_square


def adamw_update(gradient, master, first_old, second, step_rate, factor):
    scaled = gradient * factor
    first_new = BETA_ONE * first_old + (1.0 - BETA_ONE) * scaled
    second_new = BETA_TWO * second + (1.0 - BETA_TWO) * scaled * scaled
    step_ratio = (
        first_new
        / (1.0 - BETA_ONE**STEP)
        / (jnp.sqrt(second_new / (1.0 - BETA_TWO**STEP)) + ADAM_EPS)
    )
    master_new = master - step_rate * (step_ratio + WEIGHT_DECAY * master)
    return (first_new, second_new, master_new, master_new.astype(jnp.bfloat16))


def per_device(
    tokens,
    cotangent,
    size_tags,
    timesteps,
    labels,
    modulator,
    class_table,
    mix_kernel,
    heads_in,
    heads_out,
    up_weight,
    hidden_kernel,
    down_weight,
    modulator_master,
    modulator_first,
    modulator_second,
    class_table_master,
    class_table_first,
    class_table_second,
    mix_kernel_master,
    mix_kernel_first,
    mix_kernel_second,
    heads_in_master,
    heads_in_first,
    heads_in_second,
    heads_out_master,
    heads_out_first,
    heads_out_second,
    up_weight_master,
    up_weight_first,
    up_weight_second,
    hidden_kernel_master,
    hidden_kernel_first,
    hidden_kernel_second,
    down_weight_master,
    down_weight_first,
    down_weight_second,
):
    channels = tokens.shape[1]
    head_size = HS
    grid_side = SIDE
    frame_len = grid_side * grid_side
    quad_len = 4 * frame_len
    frame_count = timesteps.shape[0]
    half_rows = tokens.shape[0]
    is_big = size_tags > frame_len
    class_count = class_table.shape[1]
    class_onehot = (labels[:, None] == jnp.arange(class_count, dtype=jnp.int32)[None, :]).astype(
        jnp.bfloat16
    )
    embedded = timestep_code(timesteps, channels) + jnp.einsum(
        "fc,dc->fd", class_onehot, class_table, preferred_element_type=jnp.float32
    )
    cond_low = jax.nn.silu(embedded).astype(jnp.bfloat16)
    modulation = jnp.dot(cond_low, modulator, preferred_element_type=jnp.float32).reshape(
        frame_count, 6, 1, channels
    )
    shift_one = modulation[:, 0]
    scale_one = modulation[:, 1]
    gate_one = modulation[:, 2]
    shift_two = modulation[:, 3]
    scale_two = modulation[:, 4]
    gate_two = modulation[:, 5]
    inputs = tokens.astype(jnp.float32).reshape(frame_count, frame_len, channels)
    normed_one, inverse_one = layer_norm(inputs)
    norm_low = (
        (normed_one * (1.0 + scale_one) + shift_one)
        .astype(jnp.bfloat16)
        .reshape(half_rows, channels)
    )
    norm_full = lax.all_gather(norm_low, "narrow", axis=0, tiled=True)
    quad_count = norm_full.shape[0] // quad_len
    mix_values = mix_kernel.astype(jnp.float32)

    def mix_quad(operands):
        return quad_conv(
            operands[0].astype(jnp.float32), mix_values, operands[1], grid_side
        ).astype(jnp.bfloat16)

    mixed_low = lax.map(
        mix_quad, (norm_full.reshape(quad_count, quad_len, channels), is_big)
    ).reshape(-1, channels)
    triples = jnp.dot(mixed_low, heads_in, preferred_element_type=jnp.float32).astype(jnp.bfloat16)

    def attend_quad(operands):
        grouped = to_groups(operands[0], operands[1], grid_side)
        mixture, log_sums = lax.map(
            lambda pieces: group_forward(pieces[0], pieces[1], head_size),
            (grouped, jnp.broadcast_to(operands[1], (4,))),
        )
        return (from_groups(mixture, operands[1], grid_side).astype(jnp.bfloat16), log_sums)

    attended, quad_sums = lax.map(attend_quad, (triples.reshape(quad_count, quad_len, -1), is_big))
    attended = attended.reshape(-1, attended.shape[-1])
    attn_half = (
        lax.psum_scatter(
            jnp.dot(attended, heads_out, preferred_element_type=jnp.float32).astype(jnp.bfloat16),
            "narrow",
            scatter_dimension=0,
            tiled=True,
        )
        .astype(jnp.float32)
        .reshape(frame_count, frame_len, channels)
    )
    residual = inputs + gate_one * attn_half
    normed_two, inverse_two = layer_norm(residual)
    ffn_low = (
        (normed_two * (1.0 + scale_two) + shift_two)
        .astype(jnp.bfloat16)
        .reshape(half_rows, channels)
    )
    ffn_full = lax.all_gather(ffn_low, "narrow", axis=0, tiled=True)
    hidden = jnp.dot(ffn_full, up_weight, preferred_element_type=jnp.float32)
    kernel_values = hidden_kernel.astype(jnp.float32)

    def hidden_quad(operands):
        return quad_conv(operands[0], kernel_values, operands[1], grid_side)

    convolved = lax.map(hidden_quad, (hidden.reshape(quad_count, quad_len, -1), is_big)).reshape(
        hidden.shape
    )
    activated = jax.nn.gelu(convolved).astype(jnp.bfloat16)
    ffn_half = (
        lax.psum_scatter(
            jnp.dot(activated, down_weight, preferred_element_type=jnp.float32).astype(
                jnp.bfloat16
            ),
            "narrow",
            scatter_dimension=0,
            tiled=True,
        )
        .astype(jnp.float32)
        .reshape(frame_count, frame_len, channels)
    )
    output = (residual + gate_two * ffn_half).reshape(half_rows, channels).astype(jnp.bfloat16)
    grad_out = cotangent.astype(jnp.float32).reshape(frame_count, frame_len, channels)
    grad_gate_two = jnp.sum(grad_out * ffn_half, axis=1)
    grad_ffn_low = (grad_out * gate_two).astype(jnp.bfloat16).reshape(half_rows, channels)
    grad_ffn_full = lax.all_gather(grad_ffn_low, "narrow", axis=0, tiled=True)
    down_grad = jnp.einsum(
        "tf,td->fd", activated, grad_ffn_full, preferred_element_type=jnp.float32
    )
    grad_active = jnp.einsum(
        "td,fd->tf", grad_ffn_full, down_weight, preferred_element_type=jnp.float32
    )
    gelu_values, gelu_pullback = jax.vjp(jax.nn.gelu, convolved)
    grad_conv = gelu_pullback(grad_active)[0]
    kernel_flipped = kernel_values[:, ::-1]

    def hidden_back(operands):
        return (
            quad_conv(operands[1], kernel_flipped, operands[2], grid_side),
            quad_taps(operands[0], operands[1], operands[2], grid_side),
        )

    grad_hidden, hidden_taps = lax.map(
        hidden_back,
        (
            hidden.reshape(quad_count, quad_len, -1),
            grad_conv.reshape(quad_count, quad_len, -1),
            is_big,
        ),
    )
    grad_hidden = grad_hidden.reshape(hidden.shape).astype(jnp.bfloat16)
    hidden_kernel_grad = jnp.sum(hidden_taps, axis=0)
    up_grad = jnp.einsum("td,tf->df", ffn_full, grad_hidden, preferred_element_type=jnp.float32)
    grad_norm_two = (
        lax.psum_scatter(
            jnp.einsum(
                "tf,df->td", grad_hidden, up_weight, preferred_element_type=jnp.float32
            ).astype(jnp.bfloat16),
            "narrow",
            scatter_dimension=0,
            tiled=True,
        )
        .astype(jnp.float32)
        .reshape(frame_count, frame_len, channels)
    )
    grad_shift_two = jnp.sum(grad_norm_two, axis=1)
    grad_scale_two = jnp.sum(grad_norm_two * normed_two, axis=1)
    modulation_two_grad = jnp.concatenate([grad_shift_two, grad_scale_two], axis=1)
    grad_residual = grad_out + norm_back(grad_norm_two * (1.0 + scale_two), normed_two, inverse_two)
    grad_gate_one = jnp.sum(grad_residual * attn_half, axis=1)
    grad_attn_low = (grad_residual * gate_one).astype(jnp.bfloat16).reshape(half_rows, channels)
    grad_attn_full = lax.all_gather(grad_attn_low, "narrow", axis=0, tiled=True)
    heads_out_grad = jnp.einsum(
        "te,td->ed", attended, grad_attn_full, preferred_element_type=jnp.float32
    )
    grad_attended = jnp.einsum(
        "td,ed->te", grad_attn_full, heads_out, preferred_element_type=jnp.float32
    ).astype(jnp.bfloat16)

    def attend_back_quad(operands):
        grouped = to_groups(operands[0], operands[3], grid_side)
        grad_groups = to_groups(operands[2], operands[3], grid_side)
        result = lax.map(
            lambda pieces: group_back(pieces[0], pieces[1], pieces[2], pieces[3], head_size),
            (grouped, operands[1], grad_groups, jnp.broadcast_to(operands[3], (4,))),
        )
        return from_groups(result, operands[3], grid_side)

    grad_triples = lax.map(
        attend_back_quad,
        (
            triples.reshape(quad_count, quad_len, -1),
            quad_sums,
            grad_attended.reshape(quad_count, quad_len, -1),
            is_big,
        ),
    ).reshape(triples.shape)
    heads_in_grad = jnp.einsum(
        "td,tk->dk", mixed_low, grad_triples, preferred_element_type=jnp.float32
    )
    grad_mixture = jnp.einsum(
        "tk,dk->td", grad_triples, heads_in, preferred_element_type=jnp.float32
    )
    mix_flipped = mix_values[:, ::-1]

    def mix_back(operands):
        return (
            quad_conv(operands[1], mix_flipped, operands[2], grid_side),
            quad_taps(operands[0].astype(jnp.float32), operands[1], operands[2], grid_side),
        )

    grad_norm_part, mix_taps = lax.map(
        mix_back,
        (
            norm_full.reshape(quad_count, quad_len, channels),
            grad_mixture.reshape(quad_count, quad_len, channels),
            is_big,
        ),
    )
    mix_kernel_grad = jnp.sum(mix_taps, axis=0)
    grad_norm_one = (
        lax.psum_scatter(
            grad_norm_part.reshape(-1, channels).astype(jnp.bfloat16),
            "narrow",
            scatter_dimension=0,
            tiled=True,
        )
        .astype(jnp.float32)
        .reshape(frame_count, frame_len, channels)
    )
    grad_shift_one = jnp.sum(grad_norm_one, axis=1)
    grad_scale_one = jnp.sum(grad_norm_one * normed_one, axis=1)
    grad_input = grad_residual + norm_back(
        grad_norm_one * (1.0 + scale_one), normed_one, inverse_one
    )
    input_grad = grad_input.reshape(half_rows, channels).astype(jnp.bfloat16)
    grad_modulation = (
        jnp.stack(
            [
                grad_shift_one,
                grad_scale_one,
                grad_gate_one,
                grad_shift_two,
                grad_scale_two,
                grad_gate_two,
            ],
            axis=1,
        )
        .reshape(frame_count, 6 * channels)
        .astype(jnp.bfloat16)
    )
    grad_cond = jnp.einsum(
        "fk,dk->fd", grad_modulation, modulator, preferred_element_type=jnp.float32
    )
    silu_values, silu_pullback = jax.vjp(jax.nn.silu, embedded)
    grad_embedded = silu_pullback(grad_cond)[0]
    wide_count = lax.axis_size("wide")
    cell_count = wide_count * lax.axis_size("narrow")
    wide_index = lax.axis_index("wide")
    cell_index = wide_index * lax.axis_size("narrow") + lax.axis_index("narrow")
    modulator_grad = jnp.einsum(
        "fd,fk->dk", cond_low, grad_modulation, preferred_element_type=jnp.float32
    )
    class_grad = jnp.dot(
        grad_embedded.T,
        class_onehot.astype(jnp.float32),
        precision=HIGHEST_PRECISION,
        preferred_element_type=jnp.float32,
    )
    local_part = ()
    shared_grads = (modulator_grad, class_grad, mix_kernel_grad)
    split_grads = (heads_in_grad, heads_out_grad, up_grad, hidden_kernel_grad, down_grad)
    summed = lax.psum(shared_grads + (square_sum(local_part),), ("wide", "narrow"))
    shared_full = summed[:-1]
    split_full = lax.psum(
        (split_grads[0], split_grads[1], split_grads[2], split_grads[3], split_grads[4]), "wide"
    )
    split_square = lax.psum(square_sum(split_full), "narrow")
    total_square = split_square + square_sum(shared_full) + summed[-1]
    shared_shards = local_part + tuple(
        (own_rows(member, cell_index, cell_count) for member in shared_full)
    )
    split_shards = tuple((own_rows(member, wide_index, wide_count) for member in split_full))
    grad_norm = jnp.sqrt(total_square)
    clip_limit = PARAMS**0.5
    factor = clip_limit / jnp.maximum(grad_norm, clip_limit)
    step_rates = (
        D ** (-0.5),
        1.0,
        1.0 / 3.0,
        D ** (-0.5),
        (D // 32) ** (-0.5),
        D ** (-0.5),
        1.0 / 3.0,
        FF ** (-0.5),
    )
    states = (
        (modulator_master, modulator_first, modulator_second),
        (class_table_master, class_table_first, class_table_second),
        (mix_kernel_master, mix_kernel_first, mix_kernel_second),
        (heads_in_master, heads_in_first, heads_in_second),
        (heads_out_master, heads_out_first, heads_out_second),
        (up_weight_master, up_weight_first, up_weight_second),
        (hidden_kernel_master, hidden_kernel_first, hidden_kernel_second),
        (down_weight_master, down_weight_first, down_weight_second),
    )
    shards = tuple(shared_shards) + tuple(split_shards)
    updated = [
        adamw_update(gradient, state_set[0], state_set[1], state_set[2], step_rate, factor)
        for gradient, state_set, step_rate in zip(shards, states, step_rates)
    ]
    return (
        output,
        input_grad,
        grad_norm,
        updated[0][0],
        updated[0][1],
        updated[0][2],
        updated[0][3],
        updated[1][0],
        updated[1][1],
        updated[1][2],
        updated[1][3],
        updated[2][0],
        updated[2][1],
        updated[2][2],
        updated[2][3],
        updated[3][0],
        updated[3][1],
        updated[3][2],
        updated[3][3],
        updated[4][0],
        updated[4][1],
        updated[4][2],
        updated[4][3],
        updated[5][0],
        updated[5][1],
        updated[5][2],
        updated[5][3],
        updated[6][0],
        updated[6][1],
        updated[6][2],
        updated[6][3],
        updated[7][0],
        updated[7][1],
        updated[7][2],
        updated[7][3],
        modulation_two_grad,
    )


def solution(mesh):
    in_specs = (
        P(("wide", "narrow"), None),
        P(("wide", "narrow"), None),
        P("wide"),
        P(("wide", "narrow")),
        P(("wide", "narrow")),
        P(),
        P(),
        P(),
        P(None, "narrow"),
        P("narrow", None),
        P(None, "narrow"),
        P("narrow", None),
        P("narrow", None),
        P(("wide", "narrow"), None),
        P(("wide", "narrow"), None),
        P(("wide", "narrow"), None),
        P(("wide", "narrow"), None),
        P(("wide", "narrow"), None),
        P(("wide", "narrow"), None),
        P(("wide", "narrow"), None),
        P(("wide", "narrow"), None),
        P(("wide", "narrow"), None),
        P("wide", "narrow"),
        P("wide", "narrow"),
        P("wide", "narrow"),
        P(("narrow", "wide"), None),
        P(("narrow", "wide"), None),
        P(("narrow", "wide"), None),
        P("wide", "narrow"),
        P("wide", "narrow"),
        P("wide", "narrow"),
        P(("narrow", "wide"), None),
        P(("narrow", "wide"), None),
        P(("narrow", "wide"), None),
        P(("narrow", "wide"), None),
        P(("narrow", "wide"), None),
        P(("narrow", "wide"), None),
    )
    out_specs = (
        P(("wide", "narrow"), None),
        P(("wide", "narrow"), None),
        P(),
        P(("wide", "narrow"), None),
        P(("wide", "narrow"), None),
        P(("wide", "narrow"), None),
        P(("wide", "narrow"), None),
        P(("wide", "narrow"), None),
        P(("wide", "narrow"), None),
        P(("wide", "narrow"), None),
        P(("wide", "narrow"), None),
        P(("wide", "narrow"), None),
        P(("wide", "narrow"), None),
        P(("wide", "narrow"), None),
        P(("wide", "narrow"), None),
        P("wide", "narrow"),
        P("wide", "narrow"),
        P("wide", "narrow"),
        P("wide", "narrow"),
        P(("narrow", "wide"), None),
        P(("narrow", "wide"), None),
        P(("narrow", "wide"), None),
        P(("narrow", "wide"), None),
        P("wide", "narrow"),
        P("wide", "narrow"),
        P("wide", "narrow"),
        P("wide", "narrow"),
        P(("narrow", "wide"), None),
        P(("narrow", "wide"), None),
        P(("narrow", "wide"), None),
        P(("narrow", "wide"), None),
        P(("narrow", "wide"), None),
        P(("narrow", "wide"), None),
        P(("narrow", "wide"), None),
        P(("narrow", "wide"), None),
        P(("wide", "narrow"), None),
    )
    return jax.shard_map(
        per_device, mesh=mesh, in_specs=in_specs, out_specs=out_specs, check_vma=False
    )
```

profile of v0, /device:TPU:0, one launch (start us, length us, event | category | flops | bytes accessed | tf_op | source)
XLA Modules:
  0.0 1999.4 jit_solution(2191708204572553516)
XLA Ops:
  25.9 18.9 all-gather.5.cloned.1.call-done
  53.1 40.9 %conditional.30 = (bf16[4096,768]{1,0:T(8,128)(2,1)}) conditional(s32[]{:T(128)} %convert_element_type.239, (f32[4096,768]{1,0:T(8,128)}, f32[768,9]{0,1:T(8,128)S(1)}) %tuple.167, (f32[4096,768]{1,0:T(8,128)}, f32[768,9]{0,1:T(8,128)S(1)}) %tuple.167), branch_computations={%region_2.3_spmd, %region_3.4_spmd} | conditional | flops 56623104 | bytes 18957320
  53.1 40.6 %fusion.106 = bf16[1,64,64,768]{3,2,1,0:T(8,128)(2,1)} fusion(f32[1,64,64,768]{3,2,1,0:T(8,128)} %bitcast.2, f32[768]{0:T(1024)S(1)} %get-tuple-element.642, f32[768]{0:T(1024)S(1)} %get-tuple-element.643, f32[768]{0:T(1024)S(1)} %get-tuple-element.644, f32[768]{0:T(1024)S(1)} %get-tuple-element.645, f32[768]{0:T(1024)S(1)} %get-tuple-element.646, ...), kind=kLoop, calls=%fused_computation.184 | loop fusion | flops 56623104 | bytes 18902016 | tf_op jit(solution)/shard_map/while/body/eval_jaxpr/cond/branch_1_fun/add | solution.py:56
  107.1 40.8 %conditional.31 = (bf16[4,1024,1152]{1,2,0:T(8,128)(2,1)}) conditional(s32[]{:T(128)} %convert_element_type.239, bf16[4096,1152]{1,0:T(8,128)(2,1)} %convolution_convert_fusion, bf16[4096,1152]{1,0:T(8,128)(2,1)} %convolution_convert_fusion), branch_computations={%region_4.5_spmd, %region_5.6_spmd} | conditional | bytes 56623112 | solution.py:126
  107.1 19.1 reshape.829
  147.9 162.9 %while.35 = (s32[]{:T(128)}, bf16[4,1024,384]{1,2,0:T(8,128)(2,1)}, f32[4,6144]{1,0:T(4,128)S(1)}, pred[4]{0:T(512)(128)(4,1)S(1)}, bf16[4,1024,1152]{1,2,0:T(8,128)(2,1)}, /*index=5*/s32[]{:T(128)}, s32[]{:T(128)}) while((s32[]{:T(128)}, bf16[4,1024,384]{1,2,0:T(8,128)(2,1)}, f32[4,6144]{1,0:T(4,128)S(1)}, pred[4]{0:T(512)(128)(4,1)S(1)}, ...), condition=%wide.region_13.14_spmd, body=%wide.region_6.13_spmd.sunk | while | flops 1667229696 | bytes 85229680 | solution.py:358
  152.9 34.7 %conditional.42 = (bf16[1,1024,384]{1,2,0:T(8,128)(2,1)S(1)}, f32[1,6144]{1,0:T(1,128)S(1)}) conditional(s32[]{:T(128)} %bitcast.366, bf16[1024,6,3,64]{0,3,2,1:T(8,128)(2,1)} %bitcast.367, bf16[1024,6,3,64]{0,3,2,1:T(8,128)(2,1)} %bitcast.367), branch_computations={%region_7.9_spmd, %region_10.12_spmd} | conditional | flops 1667229696 | bytes 78888976 | solution.py:209
  193.4 34.7 %conditional.42 = (bf16[1,1024,384]{1,2,0:T(8,128)(2,1)S(1)}, f32[1,6144]{1,0:T(1,128)S(1)}) conditional(s32[]{:T(128)} %bitcast.366, bf16[1024,6,3,64]{0,3,2,1:T(8,128)(2,1)} %bitcast.367, bf16[1024,6,3,64]{0,3,2,1:T(8,128)(2,1)} %bitcast.367), branch_computations={%region_7.9_spmd, %region_10.12_spmd} | conditional | flops 1667229696 | bytes 78888976 | solution.py:209
  234.0 34.7 %conditional.42 = (bf16[1,1024,384]{1,2,0:T(8,128)(2,1)S(1)}, f32[1,6144]{1,0:T(1,128)S(1)}) conditional(s32[]{:T(128)} %bitcast.366, bf16[1024,6,3,64]{0,3,2,1:T(8,128)(2,1)} %bitcast.367, bf16[1024,6,3,64]{0,3,2,1:T(8,128)(2,1)} %bitcast.367), branch_computations={%region_7.9_spmd, %region_10.12_spmd} | conditional | flops 1667229696 | bytes 78888976 | solution.py:209
  274.6 34.7 %conditional.42 = (bf16[1,1024,384]{1,2,0:T(8,128)(2,1)S(1)}, f32[1,6144]{1,0:T(1,128)S(1)}) conditional(s32[]{:T(128)} %bitcast.366, bf16[1024,6,3,64]{0,3,2,1:T(8,128)(2,1)} %bitcast.367, bf16[1024,6,3,64]{0,3,2,1:T(8,128)(2,1)} %bitcast.367), branch_computations={%region_7.9_spmd, %region_10.12_spmd} | conditional | flops 1667229696 | bytes 78888976 | solution.py:209
  311.4 19.2 conditional.32
  383.9 17.9 fusion.306
  401.7 96.6 %conditional.33 = (f32[4096,1536]{1,0:T(8,128)}, f32[4096,1536]{1,0:T(8,128)}) conditional(s32[]{:T(128)} %convert_element_type.239, (f32[4096,1536]{1,0:T(8,128)}, f32[1536,9]{0,1:T(8,128)S(1)}) %tuple.169, (f32[4096,1536]{1,0:T(8,128)}, f32[1536,9]{0,1:T(8,128)S(1)}) %tuple.169), branch_computations={%region_19.20_spmd, %region_20.21_spmd} | conditional | flops 113246208 | bytes 100829200 | solution.py:90
  402.3 78.3 %fusion.138 = f32[1,64,64,1536]{3,2,1,0:T(8,128)} fusion(f32[1,64,64,1536]{3,2,1,0:T(8,128)} %bitcast.371, f32[1536]{0:T(1024)S(1)} %get-tuple-element.660, f32[1536]{0:T(1024)S(1)} %get-tuple-element.661, f32[1536]{0:T(1024)S(1)} %get-tuple-element.662, f32[1536]{0:T(1024)S(1)} %get-tuple-element.663, f32[1536]{0:T(1024)S(1)} %get-tuple-element.664, ...), kind=kLoop, calls=%fused_computation.250 | loop fusion | flops 106954752 | bytes 50386944 | tf_op jit(solution)/shard_map/while/body/eval_jaxpr/cond/branch_1_fun/add | solution.py:56
  480.6 17.6 bitcast_multiply_fusion.11
  498.3 37.0 %multiply_add_fusion = f32[4096,1536]{1,0:T(8,128)} fusion(f32[4096,1536]{1,0:T(8,128)} %get-tuple-element.475, f32[4096,1536]{1,0:T(8,128)} %get-tuple-element.474, bf16[4096,768]{1,0:T(8,128)(2,1)} %all-gather.9.cloned.1.call-done, bf16[1536,768]{1,0:T(8,128)(2,1)} %param.77), kind=kOutput, calls=%fused_computation.441 | convolution fusion | flops 9776922624 | bytes 84148224 | tf_op jit(solution)/shard_map/td,fd->tf/dot_general | solution.py:414
  535.3 74.2 %conditional.34 = (bf16[4096,1536]{1,0:T(8,128)(2,1)}) conditional(s32[]{:T(128)} %convert_element_type.239, (f32[4096,1536]{1,0:T(8,128)}, f32[1536,9]{0,1:T(8,128)S(1)}) %tuple.170, (f32[4096,1536]{1,0:T(8,128)}, f32[1536,9]{0,1:T(8,128)S(1)}) %tuple.170), branch_computations={%region_22.23_spmd, %region_23.24_spmd} | conditional | flops 113246208 | bytes 37914632
  535.7 73.9 %fusion.170 = bf16[1,64,64,1536]{3,2,1,0:T(8,128)(2,1)} fusion(f32[1,64,64,1536]{3,2,1,0:T(8,128)} %bitcast.375, f32[1536]{0:T(1024)S(1)} %get-tuple-element.678, f32[1536]{0:T(1024)S(1)} %get-tuple-element.679, f32[1536]{0:T(1024)S(1)} %get-tuple-element.680, f32[1536]{0:T(1024)S(1)} %get-tuple-element.681, f32[1536]{0:T(1024)S(1)} %get-tuple-element.682, ...), kind=kLoop, calls=%fused_computation.316 | loop fusion | flops 113246208 | bytes 37804032 | tf_op jit(solution)/shard_map/while/body/eval_jaxpr/cond/branch_1_fun/add | solution.py:56
  624.3 20.4 %multiply_convert_fusion.2 = bf16[4096,1536]{1,0:T(8,128)(2,1)S(1)} fusion(f32[4096,1536]{1,0:T(8,128)} %get-tuple-element.474, f32[4096,1536]{1,0:T(8,128)} %get-tuple-element.475), kind=kLoop, calls=%fused_computation.442 | loop fusion | flops 50331648 | bytes 62914560 | tf_op jit(solution)/shard_map/convert_element_type | solution.py:393
  731.0 381.2 %while.36 = (s32[]{:T(128)}, bf16[4,1024,1152]{1,2,0:T(8,128)(2,1)}, pred[4]{0:T(512)(128)(4,1)S(1)}, bf16[4,1024,1152]{1,2,0:T(8,128)(2,1)}, f32[4,6144]{1,0:T(...) while((s32[]{:T(128)}, bf16[4,1024,1152]{1,2,0:T(8,128)(2,1)}, pred[4]{0:T(512)(128)(4,1)S(1)}, ...), condition=%wide.region_34.35_spmd, body=%wide.region_29.34_spmd.sunk | while | flops 4105955328 | bytes 223576816 | solution.py:467
  752.3 82.0 %conditional.43 = (bf16[1,1024,1152]{1,2,0:T(8,128)(2,1)}) conditional(s32[]{:T(128)} %bitcast.368, (bf16[1024,6,3,64]{0,3,2,1:T(8,128)(2,1)S(1)}, f32[4,6144]{1,0:T(4,128)S(1)}, s32[]{:T(128)}, bf16[4,1024,384]{1,2,0:T(8,128)(2,1)}) %tuple.403, (bf16[1024,6,3,64]{0,3,2,1:T(8,128)(2,1)S(1)}, f32[4,6144]{1,0:T(4,128)S(1)}, s32[]{:T(128)}, ...), branch_computations={%region_30.31_spmd, %region_32.33_spmd} | conditional | flops 4105955328 | bytes 214138944
  775.1 19.8 multiply_reduce_fusion.7
  794.9 21.0 %multiply_convert_fusion.1 = bf16[6,1024,1024]{1,2,0:T(8,128)(2,1)} fusion(f32[6,1024,1024]{1,2,0:T(8,128)} %get-tuple-element.791, f32[6,1024,1024]{1,2,0:T(8,128)} %fusion.235, f32[6,1024]{1,0:T(8,128)S(1)} %get-tuple-element.790, f32[6,1024]{1,0:T(8,128)S(1)} %sub.135), kind=kLoop, calls=%fused_computation.422 | loop fusion | flops 31457280 | bytes 62963712 | tf_op jit(solution)/shard_map/while/body/eval_jaxpr/while/body/eval_jaxpr/cond/branch_1_fun/convert_element_type | solution.py:179
  840.7 82.0 %conditional.43 = (bf16[1,1024,1152]{1,2,0:T(8,128)(2,1)}) conditional(s32[]{:T(128)} %bitcast.368, (bf16[1024,6,3,64]{0,3,2,1:T(8,128)(2,1)S(1)}, f32[4,6144]{1,0:T(4,128)S(1)}, s32[]{:T(128)}, bf16[4,1024,384]{1,2,0:T(8,128)(2,1)}) %tuple.403, (bf16[1024,6,3,64]{0,3,2,1:T(8,128)(2,1)S(1)}, f32[4,6144]{1,0:T(4,128)S(1)}, s32[]{:T(128)}, ...), branch_computations={%region_30.31_spmd, %region_32.33_spmd} | conditional | flops 4105955328 | bytes 214138944
  863.5 19.8 multiply_reduce_fusion.7
  883.3 21.0 %multiply_convert_fusion.1 = bf16[6,1024,1024]{1,2,0:T(8,128)(2,1)} fusion(f32[6,1024,1024]{1,2,0:T(8,128)} %get-tuple-element.791, f32[6,1024,1024]{1,2,0:T(8,128)} %fusion.235, f32[6,1024]{1,0:T(8,128)S(1)} %get-tuple-element.790, f32[6,1024]{1,0:T(8,128)S(1)} %sub.135), kind=kLoop, calls=%fused_computation.422 | loop fusion | flops 31457280 | bytes 62963712 | tf_op jit(solution)/shard_map/while/body/eval_jaxpr/while/body/eval_jaxpr/cond/branch_1_fun/convert_element_type | solution.py:179
  929.1 82.0 %conditional.43 = (bf16[1,1024,1152]{1,2,0:T(8,128)(2,1)}) conditional(s32[]{:T(128)} %bitcast.368, (bf16[1024,6,3,64]{0,3,2,1:T(8,128)(2,1)S(1)}, f32[4,6144]{1,0:T(4,128)S(1)}, s32[]{:T(128)}, bf16[4,1024,384]{1,2,0:T(8,128)(2,1)}) %tuple.403, (bf16[1024,6,3,64]{0,3,2,1:T(8,128)(2,1)S(1)}, f32[4,6144]{1,0:T(4,128)S(1)}, s32[]{:T(128)}, ...), branch_computations={%region_30.31_spmd, %region_32.33_spmd} | conditional | flops 4105955328 | bytes 214138944
  951.9 19.8 multiply_reduce_fusion.7
  971.6 21.0 %multiply_convert_fusion.1 = bf16[6,1024,1024]{1,2,0:T(8,128)(2,1)} fusion(f32[6,1024,1024]{1,2,0:T(8,128)} %get-tuple-element.791, f32[6,1024,1024]{1,2,0:T(8,128)} %fusion.235, f32[6,1024]{1,0:T(8,128)S(1)} %get-tuple-element.790, f32[6,1024]{1,0:T(8,128)S(1)} %sub.135), kind=kLoop, calls=%fused_computation.422 | loop fusion | flops 31457280 | bytes 62963712 | tf_op jit(solution)/shard_map/while/body/eval_jaxpr/while/body/eval_jaxpr/cond/branch_1_fun/convert_element_type | solution.py:179
  1017.5 82.0 %conditional.43 = (bf16[1,1024,1152]{1,2,0:T(8,128)(2,1)}) conditional(s32[]{:T(128)} %bitcast.368, (bf16[1024,6,3,64]{0,3,2,1:T(8,128)(2,1)S(1)}, f32[4,6144]{1,0:T(4,128)S(1)}, s32[]{:T(128)}, bf16[4,1024,384]{1,2,0:T(8,128)(2,1)}) %tuple.403, (bf16[1024,6,3,64]{0,3,2,1:T(8,128)(2,1)S(1)}, f32[4,6144]{1,0:T(4,128)S(1)}, s32[]{:T(128)}, ...), branch_computations={%region_30.31_spmd, %region_32.33_spmd} | conditional | flops 4105955328 | bytes 214138944
  1040.3 19.8 multiply_reduce_fusion.7
  1060.1 21.0 %multiply_convert_fusion.1 = bf16[6,1024,1024]{1,2,0:T(8,128)(2,1)} fusion(f32[6,1024,1024]{1,2,0:T(8,128)} %get-tuple-element.791, f32[6,1024,1024]{1,2,0:T(8,128)} %fusion.235, f32[6,1024]{1,0:T(8,128)S(1)} %get-tuple-element.790, f32[6,1024]{1,0:T(8,128)S(1)} %sub.135), kind=kLoop, calls=%fused_computation.422 | loop fusion | flops 31457280 | bytes 62963712 | tf_op jit(solution)/shard_map/while/body/eval_jaxpr/while/body/eval_jaxpr/cond/branch_1_fun/convert_element_type | solution.py:179
  1112.2 50.9 %conditional.36 = (bf16[4096,1152]{1,0:T(8,128)(2,1)}) conditional(s32[]{:T(128)} %convert_element_type.239, bf16[4,1024,1152]{1,2,0:T(8,128)(2,1)} %get-tuple-element.477, bf16[4,1024,1152]{1,2,0:T(8,128)(2,1)} %get-tuple-element.477), branch_computations={%region_35.36_spmd, %region_36.37_spmd} | conditional | bytes 56623112 | solution.py:147
  1125.1 18.2 copy.283
  1143.3 19.9 reshape.868
  1176.8 42.0 %conditional.37 = (bf16[4096,768]{1,0:T(8,128)(2,1)}) conditional(s32[]{:T(128)} %convert_element_type.239, (f32[4096,768]{1,0:T(8,128)}, f32[768,9]{0,1:T(8,128)S(1)}) %tuple.407, (f32[4096,768]{1,0:T(8,128)}, f32[768,9]{0,1:T(8,128)S(1)}) %tuple.408), branch_computations={%region_37.38_spmd, %region_38.39_spmd} | conditional | flops 56623104 | bytes 18957320 | solution.py:90
  1176.9 41.7 %fusion.202 = bf16[1,64,64,768]{3,2,1,0:T(8,128)(2,1)} fusion(f32[1,64,64,768]{3,2,1,0:T(8,128)} %bitcast.62, f32[768]{0:T(1024)S(1)} %get-tuple-element.696, f32[768]{0:T(1024)S(1)} %get-tuple-element.697, f32[768]{0:T(1024)S(1)} %get-tuple-element.698, f32[768]{0:T(1024)S(1)} %get-tuple-element.699, f32[768]{0:T(1024)S(1)} %get-tuple-element.700, ...), kind=kLoop, calls=%fused_computation.382 | loop fusion | flops 56623104 | bytes 18902016 | tf_op jit(solution)/shard_map/while/body/eval_jaxpr/cond/branch_1_fun/add | solution.py:56
  1218.9 16.5 fusion.308
  1235.4 16.8 fusion.310
  1294.0 91.6 %conditional.38 = (f32[1536,9]{0,1:T(8,128)S(1)}) conditional(s32[]{:T(128)} %convert_element_type.239, (f32[4096,1536]{1,0:T(8,128)}, f32[4096,1536]{1,0:T(8,128)}) %tuple.173, (f32[4096,1536]{1,0:T(8,128)}, f32[4096,1536]{1,0:T(8,128)}) %tuple.173), branch_computations={%region_48.58_spmd, %region_58.68_spmd} | conditional | flops 113232384 | bytes 100939784 | solution.py:105
  1294.0 17.2 multiply_reduce_fusion.3
  1311.2 74.1 %fusion.49 = (f32[1536]{0:T(1024)S(1)}, f32[1536]{0:T(1024)S(1)}, f32[1536]{0:T(1024)S(1)}, f32[1536]{0:T(1024)S(1)}, f32[1536]{0:T(1024)S(1)}, /*index=5*/f32[1536]{0:T(1024)S(1)}, f32[1536]{0:T(1024)S(1)}, f32[1536]{0:T(1024)S(1)}) fusion(f32[1,64,64,1536]{3,2,1,0:T(8,128)} %bitcast.373, f32[4096,1536]{1,0:T(8,128)} %get-tuple-element.427), kind=kLoop, calls=%fused_computation.83 | loop fusion | flops 100651008 | bytes 50380800 | tf_op jit(solution)/shard_map/while/body/eval_jaxpr/cond/branch_1_fun/reduce_sum | solution.py:69
  1385.6 81.1 %psum.73 = f32[1536,9]{0,1:T(8,128)S(1)} all-reduce(f32[1536,9]{0,1:T(8,128)S(1)} %get-tuple-element.942), channel_id=1, replica_groups=mesh['wide'=16,'narrow'=2] {'wide'}, use_global_device_ids=true, to_apply=%region_68.69 | all-reduce | flops 13824 | bytes 110592 | tf_op jit(solution)/shard_map/psum | solution.py:559
  1467.4 48.5 %conditional.39 = (f32[768,9]{0,1:T(8,128)S(1)}) conditional(s32[]{:T(128)} %convert_element_type.239, (f32[4096,768]{1,0:T(8,128)}, f32[4096,768]{1,0:T(8,128)}) %tuple.174, (f32[4096,768]{1,0:T(8,128)}, f32[4096,768]{1,0:T(8,128)}) %tuple.174), branch_computations={%region_83.93_spmd, %region_93.103_spmd} | conditional | flops 56616192 | bytes 50469896 | solution.py:105
  1477.2 38.5 %fusion.81 = (f32[768]{0:T(1024)S(1)}, f32[768]{0:T(1024)S(1)}, f32[768]{0:T(1024)S(1)}, f32[768]{0:T(1024)S(1)}, f32[768]{0:T(1024)S(1)}, /*index=5*/f32[768]{0:T(1024)S(1)}, f32[768]{0:T(1024)S(1)}, f32[768]{0:T(1024)S(1)}) fusion(f32[1,64,64,768]{3,2,1,0:T(8,128)} %bitcast.70, f32[4096,768]{1,0:T(8,128)} %get-tuple-element.431), kind=kLoop, calls=%fused_computation.133 | loop fusion | flops 50325504 | bytes 25190400 | tf_op jit(solution)/shard_map/while/body/eval_jaxpr/cond/branch_1_fun/reduce_sum | solution.py:69
  1515.9 38.1 %all-reduce.12 = (f32[768,9]{0,1:T(8,128)S(1)}, f32[]{:T(128)}) all-reduce(f32[768,9]{0,1:T(8,128)S(1)} %get-tuple-element.943, f32[]{:T(128)} %constant.204.clone.1), channel_id=1, replica_groups=mesh['wide'=16,'narrow'=2] {'wide','narrow'}, use_global_device_ids=true, to_apply=%region_103.104 | all-reduce | flops 6913 | bytes 55304 | tf_op jit(solution)/shard_map/psum | solution.py:557
  1559.4 109.2 %all-reduce.20.cloned.1.call-done = (f32[768,1152]{1,0:T(8,128)}, f32[384,768]{1,0:T(8,128)}, f32[768,1536]{1,0:T(8,128)}, f32[1536,768]{1,0:T(8,128)}) async-done(((f32[768,1152]{1,0:T(8,128)}, f32[384,768]{1,0:T(8,128)}, f32[768,1536]{1,0:T(8,128)}, f32[1536,768]{1,0:T(8,128)}), (f32[768,1152]{1,0:T(8,128)}, f32[384,768]{1,0:T(8,128)}, f32[768,1536]{1,0:T(8,128)}, ...) | async-done | bytes 14155792 | tf_op jit(solution)/shard_map/psum | solution.py:559
  1696.6 262.6 %all-reduce.18.cloned.1.call-done = (f32[768,4608]{1,0:T(8,128)}, f32[768,1000]{1,0:T(8,128)}) async-done(((f32[768,4608]{1,0:T(8,128)}, f32[768,1000]{1,0:T(8,128)}), (f32[768,4608]{1,0:T(8,128)}, f32[768,1000]{1,0:T(8,128)})) %all-reduce.18.cloned.1.call-update) | async-done | bytes 17227792 | tf_op jit(solution)/shard_map/psum | solution.py:557
  (372 shorter events, 735.2 us)
Async XLA Ops:
  7.2 376.7 %copy-start = (bf16[768,1536]{1,0:T(8,128)(2,1)S(1)}, bf16[768,1536]{1,0:T(8,128)(2,1)}, u32[]{:S(2)}) copy-start(bf16[768,1536]{1,0:T(8,128)(2,1)} %param.75) | copy-start | bytes 7077892
  7.2 18.6 copy-start.40
  7.2 37.5 %all-gather.5.cloned.1.call-start = ((), (), s32[]{:S(2)}) async-start(), calls=%async_computation.4 | async-start | bytes 9437184 | tf_op jit(solution)/shard_map/all_gather | solution.py:342
  10.5 42.6 %copy-start.21 = (f32[2048]{0:T(1024)}, f32[2048]{0:T(1024)S(1)}, u32[]{:S(2)}) copy-start(f32[2048]{0:T(1024)S(1)} %broadcast_multiply_fusion.5) | copy-start | bytes 24580
  25.1 329.3 %reduce-scatter.5.cloned.1.call-start = ((), (), s32[]{:S(2)}) async-start(), calls=%async_computation.5 | async-start | bytes 9437184 | tf_op jit(solution)/shard_map/reduce_scatter | solution.py:367
  310.8 19.9 copy-start.60
  338.6 45.3 %all-gather.7.cloned.1.call-start = ((), (), s32[]{:S(2)}) async-start(), calls=%async_computation.6 | async-start | bytes 9437184 | tf_op jit(solution)/shard_map/all_gather | solution.py:383
  338.6 27.1 %copy-start.18 = (f32[2,1,1,768]{3,0,1,2:T(2,128)}, f32[2,1,1,768]{3,0,1,2:T(2,128)S(1)}, u32[]{:S(2)}) copy-start(f32[2,1,1,768]{3,0,1,2:T(2,128)S(1)} %copy.285) | copy-start | bytes 18436
  338.7 27.1 %copy-start.33 = (f32[2,768]{1,0:T(2,128)}, f32[2,768]{1,0:T(2,128)S(1)}, u32[]{:S(2)}) copy-start(f32[2,768]{1,0:T(2,128)S(1)} %get-tuple-element.802) | copy-start | bytes 18436
  365.8 132.5 %all-gather.9.cloned.1.call-start = ((), (), s32[]{:S(2)}) async-start(), calls=%async_computation.8 | async-start | bytes 9437184 | tf_op jit(solution)/shard_map/all_gather | solution.py:410
  370.7 290.9 %reduce-scatter.9.cloned.1.call-start = ((), (), s32[]{:S(2)}) async-start(), calls=%async_computation.9 | async-start | bytes 9437184 | tf_op jit(solution)/shard_map/reduce_scatter | solution.py:439
  624.3 54.5 %reduce-scatter.7.cloned.1.call-start = ((), (), s32[]{:S(2)}) async-start(), calls=%async_computation.7 | async-start | bytes 9437184 | tf_op jit(solution)/shard_map/reduce_scatter | solution.py:395
  624.3 24.9 %copy-start.58 = (bf16[1536,768]{1,0:T(8,128)(2,1)S(1)}, bf16[1536,768]{1,0:T(8,128)(2,1)}, u32[]{:S(2)}) copy-start(bf16[1536,768]{1,0:T(8,128)(2,1)} %param.77) | copy-start | bytes 7077892
  661.1 17.6 copy-start.50
  661.1 45.9 %all-gather.11.cloned.1.call-start = ((), (), s32[]{:S(2)}) async-start(), calls=%async_computation.10 | async-start | bytes 9437184 | tf_op jit(solution)/shard_map/all_gather | solution.py:456
  666.8 22.1 %copy-start.44 = (f32[2048]{0:T(1024)}, f32[2048]{0:T(1024)S(1)}, u32[]{:S(2)}) copy-start(f32[2048]{0:T(1024)S(1)} %broadcast_multiply_fusion.3) | copy-start | bytes 24580
  666.8 22.1 %copy-start.46 = (f32[2048]{0:T(1024)}, f32[2048]{0:T(1024)S(1)}, u32[]{:S(2)}) copy-start(f32[2048]{0:T(1024)S(1)} %broadcast_multiply_fusion.2) | copy-start | bytes 24580
  666.8 22.2 %copy-start.41 = (bf16[768,9]{0,1:T(8,128)(2,1)S(1)}, bf16[768,9]{0,1:T(8,128)(2,1)}, u32[]{:S(2)}) copy-start(bf16[768,9]{0,1:T(8,128)(2,1)} %param.72) | copy-start | bytes 41476
  666.8 40.2 %copy-start.61 = (bf16[384,768]{1,0:T(8,128)(2,1)S(1)}, bf16[384,768]{1,0:T(8,128)(2,1)}, u32[]{:S(2)}) copy-start(bf16[384,768]{1,0:T(8,128)(2,1)} %param.74) | copy-start | bytes 1769476
  688.9 578.4 %reduce-scatter.11.cloned.1.call-start = ((), (), s32[]{:S(2)}) async-start(), calls=%async_computation.11 | async-start | bytes 9437184 | tf_op jit(solution)/shard_map/reduce_scatter | solution.py:506
  714.9 16.1 copy-start.15
  714.9 16.1 copy-start.63
  815.9 16.4 copy-start.6
  904.3 16.4 copy-start.6
  992.7 16.4 copy-start.6
  1081.1 16.4 copy-start.6
  1112.2 50.9 %copy-start.59 = (bf16[768,1152]{1,0:T(8,128)(2,1)S(1)}, bf16[768,1152]{1,0:T(8,128)(2,1)}, u32[]{:S(2)}) copy-start(bf16[768,1152]{1,0:T(8,128)(2,1)} %param.73) | copy-start | bytes 5308420
  1218.8 449.9 %all-reduce.20.cloned.1.call-start = ((), (), s32[]{:S(2)}) async-start(), calls=%async_computation.13 | async-start | bytes 28311552 | tf_op jit(solution)/shard_map/psum | solution.py:559
  1218.8 33.4 %slice-start = ((s8[6291456]{0:T(1024)(128)(4,1)}), s8[4194304]{0:T(1024)(128)(4,1)S(1)}, s32[]{:S(2)}) async-start(s8[6291456]{0:T(1024)(128)(4,1)} %bitcast.391), calls=%async_computation.14 | async-start | bytes 8388608
  1218.8 37.1 %slice-start.2 = ((s8[9437184]{0:T(1024)(128)(4,1)}), s8[4194304]{0:T(1024)(128)(4,1)S(1)}, s32[]{:S(2)}) async-start(s8[9437184]{0:T(1024)(128)(4,1)} %bitcast.401), calls=%async_computation.16 | async-start | bytes 8388608
  1218.8 37.1 %slice-start.3 = ((s8[9437184]{0:T(1024)(128)(4,1)}), s8[4194304]{0:T(1024)(128)(4,1)S(1)}, s32[]{:S(2)}) async-start(s8[9437184]{0:T(1024)(128)(4,1)} %bitcast.401), calls=%async_computation.17 | async-start | bytes 8388608
  1218.9 37.1 %slice-start.5 = ((s8[6291456]{0:T(1024)(128)(4,1)}), s8[4194304]{0:T(1024)(128)(4,1)S(1)}, s32[]{:S(2)}) async-start(s8[6291456]{0:T(1024)(128)(4,1)} %bitcast.405), calls=%async_computation.19 | async-start | bytes 8388608
  1235.3 16.9 copy-start.10
  1235.3 16.9 slice-start.1
  1235.3 20.6 %slice-start.4 = ((s8[9437184]{0:T(1024)(128)(4,1)}), s8[1048576]{0:T(1024)(128)(4,1)S(1)}, s32[]{:S(2)}) async-start(s8[9437184]{0:T(1024)(128)(4,1)} %bitcast.401), calls=%async_computation.18 | async-start | bytes 2097152
  1235.3 20.6 %slice-start.6 = ((s8[6291456]{0:T(1024)(128)(4,1)}), s8[2097152]{0:T(1024)(128)(4,1)S(1)}, s32[]{:S(2)}) async-start(s8[6291456]{0:T(1024)(128)(4,1)} %bitcast.405), calls=%async_computation.20 | async-start | bytes 4194304
  1266.5 692.7 %all-reduce.18.cloned.1.call-start = ((), (), s32[]{:S(2)}) async-start(), calls=%async_computation.12 | async-start | bytes 34603008 | tf_op jit(solution)/shard_map/psum | solution.py:557
  1267.3 16.4 copy-start.37
  1267.3 16.4 copy-start.57
  1467.4 87.2 %copy-start.39 = (f32[2,768]{1,0:T(2,128)S(1)}, f32[2,768]{1,0:T(2,128)}, u32[]{:S(2)}) copy-start(f32[2,768]{1,0:T(2,128)} %copy-done.38) | copy-start | bytes 18436
  1554.0 132.0 %copy-start.48 = (f32[768,9]{0,1:T(8,128)}, f32[768,9]{0,1:T(8,128)S(1)}, u32[]{:S(2)}) copy-start(f32[768,9]{0,1:T(8,128)S(1)} %get-tuple-element.736) | copy-start | bytes 82948
  1693.2 282.1 %copy-start.16 = (f32[24,4608]{1,0:T(8,128)S(1)}, f32[24,4608]{1,0:T(8,128)}, u32[]{:S(2)}) copy-start(f32[24,4608]{1,0:T(8,128)} %param.78) | copy-start | bytes 1327108
  1693.2 282.1 %copy-start.17 = (f32[24,4608]{1,0:T(8,128)S(1)}, f32[24,4608]{1,0:T(8,128)}, u32[]{:S(2)}) copy-start(f32[24,4608]{1,0:T(8,128)} %param.80) | copy-start | bytes 1327108
  1693.2 284.6 %copy-start.42 = (f32[24,1000]{1,0:T(8,128)S(1)}, f32[24,1000]{1,0:T(8,128)}, u32[]{:S(2)}) copy-start(f32[24,1000]{1,0:T(8,128)} %param.81) | copy-start | bytes 288004
  1693.2 284.6 %copy-start.43 = (f32[24,1000]{1,0:T(8,128)S(1)}, f32[24,1000]{1,0:T(8,128)}, u32[]{:S(2)}) copy-start(f32[24,1000]{1,0:T(8,128)} %param.83) | copy-start | bytes 288004
  1959.2 31.8 %copy-start.1 = (bf16[768,1536]{1,0:T(8,128)(2,1)S(1)}, bf16[768,1536]{1,0:T(8,128)(2,1)}, u32[]{:S(2)}) copy-start(bf16[768,1536]{1,0:T(8,128)(2,1)} %param.75) | copy-start | bytes 7077892
  1962.7 23.8 %copy-start.55 = (f32[96,9]{0,1:T(8,128)S(1)}, f32[96,9]{0,1:T(8,128)}, u32[]{:S(2)}) copy-start(f32[96,9]{0,1:T(8,128)} %param.96) | copy-start | bytes 10372
  1962.7 23.8 %copy-start.56 = (f32[96,9]{0,1:T(8,128)S(1)}, f32[96,9]{0,1:T(8,128)}, u32[]{:S(2)}) copy-start(f32[96,9]{0,1:T(8,128)} %param.98) | copy-start | bytes 10372
  (33 other events, 182.3 us)
Sparse Core Ops, SparseCore 0:
  25.3 19.4 all-gather.4
  338.7 15.6 reduce-scatter.4
  365.9 17.9 all-gather.6
  385.9 17.9 all-gather.8
  624.4 17.4 reduce-scatter.8
  661.3 17.4 reduce-scatter.6
  689.0 17.9 all-gather.10
  1218.9 15.6 reduce-scatter.10
  1266.7 401.9 all-reduce.19
  1675.0 284.2 all-reduce.17
where the time goes:
time: 2010 us; the launch traced here: 2000 us
  other arithmetic  656 us (33%)
  matrix products  519 us (26%)
  waiting for transfers between devices  447 us (22%)
  local copies, waits for them, and re-layouts  194 us (10%)
  blocking collectives  123 us (6%)
  loops' own time  35.6 us (2%)
  between operations  23.9 us (1%)
    psum x1, waiting for transfers between devices, per_device(): lax.psum(shared_grads + (square_sum(local_part),), ('wide', 'narrow'))  263 us
    add x4, other arithmetic, conv_image(): result + padded[:, offset // 3:offset // 3 + row_count, offset % 3:offset...  234 us
    reduce_sum x4, other arithmetic, conv_taps(): jnp.sum(padded[:, offset // 3:offset // 3 + row_count, offset % 3:offset...  139 us
    psum x1, waiting for transfers between devices, per_device(): lax.psum((split_grads[0], split_grads[1], split_grads[2], split_grads[3],...  109 us
    convert_element_type x4, other arithmetic, attend_back(): grad_scores = (shares * (grad_shares - inner_sum)).astype(jnp.bfloat16)  84.2 us
    psum x1, blocking collectives, per_device(): lax.psum((split_grads[0], split_grads[1], split_grads[2], split_grads[3],...  81.1 us
    dot_general x4, matrix products, attend_back(): jnp.einsum('blhe,bmhe->bhlm', grad_mixture, values, preferred_element_typ...  79 us
    dot_general x4, matrix products, attend(): jnp.einsum('blhe,bmhe->bhlm', queries, key_rows, preferred_element_type=j...  52.6 us
  transfers between devices with their start and end apart: 10, of which 7 were waited for; matrix products, arithmetic and copies ran while one was open for 20% of the time, Pallas kernels for 0%

commit v1 on v0

v1 whole, which is shorter than its diff:
```python
import functools

import jax
import jax.numpy as jnp
from jax import lax
from jax.experimental import pallas as pl
from jax.experimental.pallas import tpu as pltpu
from jax.sharding import PartitionSpec as P

D = 768
HS = 64
FF = 3072
SIDE = 32
STEP = 10
PARAMS = 11419392

NORM_EPS = 1e-06
BETA_ONE = 0.5
BETA_TWO = 0.5
ADAM_EPS = 1e-08
WEIGHT_DECAY = 0.01

F32 = jnp.float32
BF16 = jnp.bfloat16

BODY = 512
HALF = 256
EDGE = 32
PLANE = 592
CHUNK = 256
VMEM_BYTES = 60 * 1024 * 1024


def params(*semantics):
    return pltpu.CompilerParams(
        dimension_semantics=semantics or None, vmem_limit_bytes=VMEM_BYTES
    )


def nn(left, right):
    return lax.dot_general(left, right, (((1,), (0,)), ((), ())), preferred_element_type=F32)


def nt(left, right):
    return lax.dot_general(left, right, (((1,), (1,)), ((), ())), preferred_element_type=F32)


def tn(left, right):
    return lax.dot_general(left, right, (((0,), (0,)), ((), ())), preferred_element_type=F32)


def whole(shape):
    return pl.BlockSpec(shape, lambda *_: (0,) * len(shape), pipeline_mode=pl.Buffered(1))


def scalars():
    return pl.BlockSpec(memory_space=pltpu.SMEM)


def geometry(scal_ref):
    return scal_ref[0], scal_ref[1], scal_ref[2] == 1, scal_ref[3]


def body_offset(half, gap):
    return pl.multiple_of(EDGE + half * (HALF + gap), 16)


def edge_offset(place):
    return pl.multiple_of(jnp.where(place == 0, EDGE + BODY, 0), 16)


def normalize(fields):
    center = fields - jnp.mean(fields, -1, keepdims=True)
    inverse = lax.rsqrt(jnp.mean(center * center, -1, keepdims=True) + NORM_EPS)
    return center * inverse, inverse


def norm_back(grad_hat, normed, inverse):
    return inverse * (
        grad_hat
        - jnp.mean(grad_hat, -1, keepdims=True)
        - normed * jnp.mean(grad_hat * normed, -1, keepdims=True)
    )


def variants(base, shifted, offset, width, rows, lanes):
    up = pl.multiple_of(offset - width, 16)
    down = pl.multiple_of(offset + width, 16)
    found = {}
    for part, shift, where in ((0, 0, offset), (0, 1, down), (1, 0, offset), (1, -1, up)):
        for column in (0, 1):
            at = (2 * part + column, pl.ds(where, rows), lanes)
            found[part, shift, column, 0] = base[at]
            found[part, shift, column, 1] = shifted[at]
    return found


def tap(found, p, q, a, b):
    part, shift = ((1, -1), (0, 0), (1, 0))[a + 1] if p == 0 else ((0, 0), (1, 0), (0, 1))[a + 1]
    column, moved = ((1, 1), (0, 0), (1, 0))[b + 1] if q == 0 else ((0, 0), (1, 0), (0, 1))[b + 1]
    return found[part, shift, column, moved]


def conv_at(found, kernel, p, q, flip=False):
    total = None
    for a in (-1, 0, 1):
        for b in (-1, 0, 1):
            index = 3 * (a + 1) + (b + 1)
            term = tap(found, p, q, a, b) * kernel[8 - index if flip else index]
            total = term if total is None else total + term
    return total


def kernel_rows(kernel_ref, lanes, rows):
    return [
        jnp.broadcast_to(kernel_ref[index : index + 1, lanes], (rows, lanes.size)) for index in range(9)
    ]


def clear_borders(plane, wide_gap=True):
    zeros = jnp.zeros((4, EDGE, plane.shape[2]), plane.dtype)
    plane[:, 0:EDGE, :] = zeros
    plane[:, EDGE + HALF : EDGE + HALF + EDGE, :] = zeros
    plane[:, EDGE + BODY : EDGE + BODY + EDGE, :] = zeros
    plane[:, PLANE - EDGE : PLANE, :] = zeros


def shift_planes(base, shifted, shift_ref, gap, long_latent, place, lanes=slice(None)):
    for column in (0, 1):

        @pl.loop(0, 4)
        def _(step, column=column):
            group = 2 * (step // 2) + column
            at = (group, pl.ds(body_offset(step % 2, gap), HALF), lanes)
            shifted[at] = nn(shift_ref[column], base[at]).astype(BF16)

        @pl.when(long_latent)
        def _(column=column):
            for part in (0, 1):
                at = (2 * part + column, pl.ds(edge_offset(place), EDGE), lanes)
                shifted[at] = nn(shift_ref[column, 0:EDGE, 0:EDGE], base[at]).astype(BF16)


def front_kernel(
    scal_ref, x_ref, edge_ref, perm_ref, edge_perm_ref, shift_ref, mod_ref, taps_ref, weight_ref,
    x_out, mixed_out, base_out, shifted_out, q_out, kv_out,
):
    width, gap, long_latent, place = geometry(scal_ref)
    step = pl.program_id(0)

    @pl.when(step == 0)
    def _():
        clear_borders(base_out)
        clear_borders(shifted_out)

        @pl.loop(0, 8)
        def _(block):
            half = block // 4
            rows = x_ref[pl.ds(pl.multiple_of(block * 256, 256), 256), :]
            shift = mod_ref[half, 0:1, :]
            scale = mod_ref[half, 1:2, :]
            place_in = pl.ds(pl.multiple_of(block * 64, 64), 64)
            place_out = pl.ds(pl.multiple_of(body_offset(half, gap) + (block % 4) * 64, 16), 64)
            for group in range(4):
                picked = nn(perm_ref[64 * group : 64 * group + 64, :], rows)
                x_out[group, place_in, :] = picked.astype(BF16)
                normed = normalize(picked)[0]
                base_out[group, place_out, :] = (normed * (1.0 + scale) + shift).astype(BF16)

        @pl.when(long_latent)
        def _():
            for group in range(4):
                picked = nn(edge_perm_ref[32 * group : 32 * group + 32, :], edge_ref[...])
                normed = normalize(picked)[0]
                value = normed * (1.0 + mod_ref[0, 1:2, :]) + mod_ref[0, 0:1, :]
                base_out[group, pl.ds(edge_offset(place), EDGE), :] = value.astype(BF16)

        shift_planes(base_out, shifted_out, shift_ref, gap, long_latent, place)

        for lane in range(D // 128):
            lanes = pl.ds(lane * 128, 128)
            kernel = kernel_rows(taps_ref, lanes, 16)

            @pl.loop(0, 32)
            def _(tile, lanes=lanes, kernel=kernel):
                offset = body_offset(tile // 16, gap) + (tile % 16) * 16
                found = variants(base_out, shifted_out, pl.multiple_of(offset, 16), width, 16, lanes)
                for p in (0, 1):
                    for q in (0, 1):
                        at = (2 * p + q, pl.ds(pl.multiple_of(tile * 16, 16), 16), lanes)
                        mixed_out[at] = conv_at(found, kernel, p, q)

    for group in range(4):
        triple = nn(mixed_out[group], weight_ref[0])
        q_out[0, group] = (triple[:, 0:128] * (HS**-0.5)).astype(BF16)
        kv_out[0, 0, group] = triple[:, 128:256].astype(BF16)
        kv_out[0, 1, group] = triple[:, 256:384].astype(BF16)


def front(scal, x, edge, perm, edge_perm, shifts, mod, taps, weight):
    pairs = weight.shape[0]
    plane = jax.ShapeDtypeStruct((4, PLANE, D), BF16)
    body = jax.ShapeDtypeStruct((4, BODY, D), BF16)
    return pl.pallas_call(
        front_kernel,
        grid=(pairs,),
        out_shape=(
            body, body, plane, plane,
            jax.ShapeDtypeStruct((pairs, 4, BODY, 128), BF16),
            jax.ShapeDtypeStruct((pairs, 2, 4, BODY, 128), BF16),
        ),
        in_specs=[
            scalars(), whole(x.shape), whole(edge.shape), whole(perm.shape), whole(edge_perm.shape),
            whole(shifts.shape), whole(mod.shape), whole(taps.shape),
            pl.BlockSpec((1, D, 384), lambda i: (i, 0, 0)),
        ],
        out_specs=(
            whole(body.shape), whole(body.shape), whole(plane.shape), whole(plane.shape),
            pl.BlockSpec((1, 4, BODY, 128), lambda i: (i, 0, 0, 0)),
            pl.BlockSpec((1, 2, 4, BODY, 128), lambda i: (i, 0, 0, 0, 0)),
        ),
        compiler_params=params("arbitrary"),
        name="front",
    )(scal, x, edge, perm, edge_perm, shifts, mod, taps, weight)


def head_mask(rows, head):
    lane = lax.broadcasted_iota(jnp.int32, (rows, 128), 1)
    return (lane < HS) if head == 0 else (lane >= HS)


def pieces(first, second, rows):
    lane = lax.broadcasted_iota(jnp.int32, (rows, 128), 1)
    value = jnp.where(lane < HS, first, second)
    one = value.astype(BF16).astype(F32)
    two = (value - one).astype(BF16).astype(F32)
    three = value - one - two
    turn = lane % HS
    picked = jnp.where(turn == 0, one, jnp.where(turn == 1, two, jnp.where(turn == 2, three, 0.0)))
    return picked.astype(BF16)


def unit_pieces(rows):
    lane = lax.broadcasted_iota(jnp.int32, (rows, 128), 1)
    return jnp.where(lane % HS < 3, 1.0, 0.0).astype(BF16)


def attend_kernel(scal_ref, q_ref, own_ref, other_ref, out_ref, log_ref):
    long_latent = scal_ref[2] == 1

    def attend(query, keys, values, rows):
        mixes, logs = [], []
        for head in (0, 1):
            masked = jnp.where(head_mask(rows, head), query, jnp.zeros_like(query))
            scores = [nt(masked, key) for key in keys]
            highest = jnp.max(scores[0], -1, keepdims=True)
            for other in scores[1:]:
                highest = jnp.maximum(highest, jnp.max(other, -1, keepdims=True))
            mix = None
            for score, value in zip(scores, values):
                share = jnp.exp(score - highest).astype(BF16)
                part = nn(share, value)
                mix = part if mix is None else mix + part
            total = mix[:, 128:256]
            mixes.append(mix[:, 0:128] / total)
            logs.append(highest + jnp.log(total))
        mix = jnp.where(head_mask(rows, 0), mixes[0], mixes[1])
        return mix.astype(BF16), pieces(-logs[0], -logs[1], rows)

    def with_ones(value):
        return jnp.concatenate([value, jnp.ones_like(value)], axis=1)

    @pl.when(long_latent)
    def _():
        for tile in range(2):
            at = pl.ds(tile * 256, 256)
            out_ref[0, at, :], log_ref[0, 0, at, :] = attend(
                q_ref[0, 0, at, :],
                [own_ref[0, 0, 0], other_ref[0, 0, 0]],
                [with_ones(own_ref[0, 1, 0]), with_ones(other_ref[0, 1, 0])],
                256,
            )

    @pl.when(jnp.logical_not(long_latent))
    def _():
        for tile in range(2):
            at = pl.ds(tile * 256, 256)
            out_ref[0, at, :], log_ref[0, 0, at, :] = attend(
                q_ref[0, 0, at, :],
                [own_ref[0, 0, 0, at, :]],
                [with_ones(own_ref[0, 1, 0, at, :])],
                256,
            )


def attention(scal, q, own, other):
    pairs = q.shape[0]
    pair_spec = pl.BlockSpec((1, 1, BODY, 128), lambda p, g: (p, g, 0, 0))
    kv_spec = pl.BlockSpec((1, 2, 1, BODY, 128), lambda p, g: (p, 0, g, 0, 0))
    other_spec = pl.BlockSpec((1, 2, 1, BODY, 128), lambda p, g: ((p + pairs // 2) % pairs, 0, g, 0, 0))
    return pl.pallas_call(
        attend_kernel,
        grid=(pairs, 4),
        out_shape=(
            jax.ShapeDtypeStruct((4, BODY, 128 * pairs), BF16),
            jax.ShapeDtypeStruct((pairs, 4, BODY, 128), BF16),
        ),
        in_specs=[scalars(), pair_spec, kv_spec, other_spec],
        out_specs=(pl.BlockSpec((1, BODY, 128), lambda p, g: (g, 0, p)), pair_spec),
        compiler_params=params("arbitrary", "arbitrary"),
        name="attention",
    )(scal, q, own, other)


def attend_back_kernel(
    scal_ref, q_ref, own_ref, other_ref, mix_ref, grad_ref, log_ref, gq_ref, gown_ref, gother_ref
):
    long_latent = scal_ref[2] == 1

    def side(query, mix, grad, log):
        rows = query.shape[0]
        product = mix.astype(F32) * grad.astype(F32)
        deltas = [
            jnp.sum(jnp.where(head_mask(rows, head), product, 0.0), -1, keepdims=True) for head in (0, 1)
        ]
        delta = pieces(-deltas[0], -deltas[1], rows)
        result = []
        for head in (0, 1):
            mask = head_mask(rows, head)
            zero = jnp.zeros_like(query)
            q_head = jnp.where(mask, query, zero)
            g_head = jnp.where(mask, grad, zero)
            q_more = jnp.concatenate([q_head, jnp.where(mask, log, zero)], axis=1)
            g_more = jnp.concatenate([g_head, jnp.where(mask, delta, zero)], axis=1)
            result.append((q_head, g_head, q_more, g_more))
        return result

    def keys_part(heads, key, value):
        rows = key.shape[0]
        ones = unit_pieces(rows)
        key_more = jnp.concatenate([key, ones], axis=1)
        value_more = jnp.concatenate([value, ones], axis=1)
        key_turned = key.astype(F32).T.astype(BF16)
        gk = gv = None
        turned = []
        for q_head, g_head, q_more, g_more in heads:
            share = jnp.exp(nt(key_more, q_more))
            slope = (share * nt(value_more, g_more)).astype(BF16)
            share = share.astype(BF16)
            gv_part = nn(share, g_head)
            gk_part = nn(slope, q_head)
            gv = gv_part if gv is None else gv + gv_part
            gk = gk_part if gk is None else gk + gk_part
            turned.append(nn(key_turned, slope))
        return gk, gv, turned

    def query_grad(turned):
        row = lax.broadcasted_iota(jnp.int32, turned[0].shape, 0)
        both = jnp.where(row < HS, turned[0], turned[1]) * (HS**-0.5)
        return both.T.astype(BF16)

    @pl.when(long_latent)
    def _():
        heads = side(q_ref[0, 0], mix_ref[0], grad_ref[0], log_ref[0, 0])
        totals = None
        for source, target in ((own_ref, gown_ref), (other_ref, gother_ref)):
            for tile in range(2):
                at = pl.ds(tile * 256, 256)
                gk, gv, turned = keys_part(heads, source[0, 0, 0, at, :], source[0, 1, 0, at, :])
                target[0, 0, 0, at, :] = gk.astype(BF16)
                target[0, 1, 0, at, :] = gv.astype(BF16)
                totals = turned if totals is None else [a + b for a, b in zip(totals, turned)]
        gq_ref[0, 0] = query_grad(totals)

    @pl.when(jnp.logical_not(long_latent))
    def _():
        for tile in range(2):
            at = pl.ds(tile * 256, 256)
            heads = side(q_ref[0, 0, at, :], mix_ref[0, at, :], grad_ref[0, at, :], log_ref[0, 0, at, :])
            gk, gv, turned = keys_part(heads, own_ref[0, 0, 0, at, :], own_ref[0, 1, 0, at, :])
            gown_ref[0, 0, 0, at, :] = gk.astype(BF16)
            gown_ref[0, 1, 0, at, :] = gv.astype(BF16)
            gq_ref[0, 0, at, :] = query_grad(turned)
        gother_ref[...] = jnp.zeros_like(gother_ref)


def attention_back(scal, q, own, other, mix, grad, log):
    pairs = q.shape[0]
    pair_spec = pl.BlockSpec((1, 1, BODY, 128), lambda p, g: (p, g, 0, 0))
    kv_spec = pl.BlockSpec((1, 2, 1, BODY, 128), lambda p, g: (p, 0, g, 0, 0))
    other_spec = pl.BlockSpec((1, 2, 1, BODY, 128), lambda p, g: ((p + pairs // 2) % pairs, 0, g, 0, 0))
    lane_spec = pl.BlockSpec((1, BODY, 128), lambda p, g: (g, 0, p))
    return pl.pallas_call(
        attend_back_kernel,
        grid=(pairs, 4),
        out_shape=(
            jax.ShapeDtypeStruct(q.shape, BF16),
            jax.ShapeDtypeStruct(own.shape, BF16),
            jax.ShapeDtypeStruct(own.shape, BF16),
        ),
        in_specs=[scalars(), pair_spec, kv_spec, other_spec, lane_spec, lane_spec, pair_spec],
        out_specs=(pair_spec, kv_spec, other_spec),
        compiler_params=params("arbitrary", "arbitrary"),
        name="attention_back",
    )(scal, q, own, other, mix, grad, log)


def middle_kernel(
    x_ref, mix_ref, cot_ref, perm_ref, mod_ref, weight_ref, attn_out, norm_out, cot_out, grad_out
):
    gate_one = mod_ref[0, 2:3, :]
    shift = mod_ref[0, 3:4, :]
    scale = mod_ref[0, 4:5, :]
    gate_two = mod_ref[0, 5:6, :]
    for group in range(4):
        attn = nn(mix_ref[group], weight_ref[...])
        attn_low = attn.astype(BF16)
        attn_out[group] = attn_low
        residual = x_ref[group].astype(F32) + gate_one * attn_low.astype(F32)
        norm_out[group] = (normalize(residual)[0] * (1.0 + scale) + shift).astype(BF16)
        cot = nn(perm_ref[64 * group : 64 * group + 64, :], cot_ref[...])
        cot_out[group] = cot.astype(BF16)
        grad_out[group] = (cot * gate_two).astype(BF16)


def middle(x, mix, cot, perm, mod, weight):
    block = pl.BlockSpec((4, 64, D), lambda i: (0, i, 0))
    body = jax.ShapeDtypeStruct((4, BODY, D), BF16)
    return pl.pallas_call(
        middle_kernel,
        grid=(8,),
        out_shape=(body,) * 4,
        in_specs=[
            block, block, pl.BlockSpec((256, D), lambda i: (i, 0)), whole(perm.shape),
            pl.BlockSpec((1, 8, D), lambda i: (i // 4, 0, 0)), whole(weight.shape),
        ],
        out_specs=(block,) * 4,
        compiler_params=params("arbitrary"),
        name="middle",
    )(x, mix, cot, perm, mod, weight)


def gelu_both(value):
    root = 0.7978845608028654
    square = value * value
    angle = value * (root + (root * 0.044715) * square)
    bent = jnp.tanh(angle)
    half = 0.5 + 0.5 * bent
    inner = (0.5 * root) + (1.5 * root * 0.044715) * square
    return value * half, half + value * (1.0 - bent * bent) * inner


def ffn_kernel(
    scal_ref, taps_own, taps_other, norm_ref, norm_edge, grad_ref, grad_edge, shift_ref,
    up_own, up_other, down_own, down_other,
    ffn_out, back_out, up_grad, down_grad, taps_grad,
    hid, hid_moved, gc, gc_moved, act, gh, da, da_edge, ffn_sum, back_sum, up, down, taps, norm_turned, grad_turned,
):
    width, gap, long_latent, place = geometry(scal_ref)
    step = pl.program_id(0)
    steps = pl.num_programs(0)

    @pl.when(step < steps // 2)
    def _():
        up[...] = up_own[...]
        down[...] = down_own[...]
        taps[...] = taps_own[...]

    @pl.when(step >= steps // 2)
    def _():
        up[...] = up_other[...]
        down[...] = down_other[...]
        taps[...] = taps_other[...]

    @pl.when(step == 0)
    def _():
        for plane in (hid, hid_moved, gc, gc_moved):
            clear_borders(plane)

        @pl.loop(0, 8)
        def _(tile):
            rows = pl.ds(pl.multiple_of((tile % 2) * HALF, HALF), HALF)
            cols = pl.ds(pl.multiple_of(tile * HALF, HALF), HALF)
            norm_turned[:, cols] = norm_ref[tile // 2, rows, :].T
            grad_turned[:, cols] = grad_ref[tile // 2, rows, :].T
            ffn_sum[tile // 2, rows, :] = jnp.zeros((HALF, D), F32)
            back_sum[tile // 2, rows, :] = jnp.zeros((HALF, D), F32)

    turn = lax.broadcasted_iota(jnp.int32, (BODY, CHUNK), 0) & (width - 1)
    keep = (turn != width - 1, turn != 0)
    for group in range(4):
        value = nn(norm_ref[group], up[...])
        moved = jnp.where(keep[group % 2], pltpu.roll(value, BODY - 1 if group % 2 == 0 else 1, 0), 0.0)
        for half in (0, 1):
            at = (group, pl.ds(body_offset(half, gap), HALF), slice(None))
            hid[at] = value[half * HALF : (half + 1) * HALF].astype(BF16)
            hid_moved[at] = moved[half * HALF : (half + 1) * HALF].astype(BF16)
        da[group] = nt(grad_ref[group], down[...]).astype(BF16)

    @pl.when(long_latent)
    def _():
        for group in range(4):
            at = (group, pl.ds(edge_offset(place), EDGE), slice(None))
            value = nn(norm_edge[group], up[...]).astype(BF16)
            hid[at] = value
            hid_moved[at] = nn(shift_ref[group % 2, 0:EDGE, 0:EDGE], value).astype(BF16)
            da_edge[group] = nt(grad_edge[group], down[...]).astype(BF16)

    for lane in range(CHUNK // 128):
        lanes = pl.ds(lane * 128, 128)
        kernel = kernel_rows(taps, lanes, 16)

        @pl.loop(0, 32, unroll=4)
        def _(tile, lanes=lanes, kernel=kernel):
            offset = pl.multiple_of(body_offset(tile // 16, gap) + (tile % 16) * 16, 16)
            found = variants(hid, hid_moved, offset, width, 16, lanes)
            rows = pl.ds(pl.multiple_of(tile * 16, 16), 16)
            for p in (0, 1):
                for q in (0, 1):
                    group = 2 * p + q
                    value, slope = gelu_both(conv_at(found, kernel, p, q).astype(F32))
                    act[group, rows, lanes] = value.astype(BF16)
                    gc[group, pl.ds(offset, 16), lanes] = (slope * da[group, rows, lanes].astype(F32)).astype(BF16)

        for side in (0, 1):

            @pl.when(jnp.logical_and(long_latent, place == side))
            def _(lanes=lanes, kernel=kernel, side=side):
                for tile in (0, 1):
                    offset = (EDGE + BODY if side == 0 else 0) + 16 * tile
                    low = max(offset - EDGE, 0)
                    found = {}
                    for part, shift, where in ((0, 0, offset), (0, 1, offset + EDGE), (1, 0, offset), (1, -1, low)):
                        if where + 16 > PLANE:
                            continue
                        for column in (0, 1):
                            at = (2 * part + column, slice(where, where + 16), lanes)
                            found[part, shift, column, 0] = hid[at]
                            found[part, shift, column, 1] = hid_moved[at]
                    for q in (0, 1):
                        group = 2 * side + q
                        slope = gelu_both(conv_at(found, kernel, side, q).astype(F32))[1]
                        grad = da_edge[group, 16 * tile : 16 * tile + 16, lanes].astype(F32)
                        gc[group, offset : offset + 16, lanes] = (slope * grad).astype(BF16)

    for group in range(4):
        for half in (0, 1):
            at = (group, pl.ds(body_offset(half, gap), HALF), slice(None))
            value = gc[at].astype(F32)
            moved = pltpu.roll(value, HALF - 1 if group % 2 == 0 else 1, 0)
            gc_moved[at] = jnp.where(keep[group % 2][:HALF], moved, 0.0).astype(BF16)
        @pl.when(long_latent)
        def _(group=group):
            at = (group, pl.ds(edge_offset(place), EDGE), slice(None))
            gc_moved[at] = nn(shift_ref[group % 2, 0:EDGE, 0:EDGE], gc[at]).astype(BF16)

    for lane in range(CHUNK // 128):
        lanes = pl.ds(lane * 128, 128)
        kernel = kernel_rows(taps, lanes, 16)

        def back_tile(tile, sums, lanes=lanes, kernel=kernel):
            offset = pl.multiple_of(body_offset(tile // 16, gap) + (tile % 16) * 16, 16)
            rows = pl.ds(pl.multiple_of(tile * 16, 16), 16)
            found = variants(gc, gc_moved, offset, width, 16, lanes)
            for p in (0, 1):
                for q in (0, 1):
                    gh[2 * p + q, rows, lanes] = conv_at(found, kernel, p, q, flip=True)
            return taps_at(found, variants(hid, hid_moved, offset, width, 16, lanes), sums)

        sums = lax.fori_loop(0, 32, back_tile, (jnp.zeros((16, 128), F32),) * 9,unroll=4)
        for index in range(9):
            taps_grad[0, index : index + 1, lanes] = jnp.sum(sums[index], 0, keepdims=True)

    for group in range(4):
        ffn_sum[group] += nn(act[group], down[...])
        back_sum[group] += nt(gh[group], up[...])

    flat_gh = gh[...].reshape(4 * BODY, CHUNK)
    flat_act = act[...].reshape(4 * BODY, CHUNK)
    up_grad[0] = nn(norm_turned[...], flat_gh).astype(BF16)
    down_grad[...] = nn(grad_turned[...], flat_act).T.astype(BF16)

    @pl.when(step == steps - 1)
    def _():
        ffn_out[...] = ffn_sum[...].astype(BF16)
        back_out[...] = back_sum[...].astype(BF16)


def taps_at(grads, fields, sums):
    sums = list(sums)
    for a in (-1, 0, 1):
        for b in (-1, 0, 1):
            index = 3 * (a + 1) + (b + 1)
            total = None
            for p in (0, 1):
                for q in (0, 1):
                    term = grads[p, 0, q, 0] * tap(fields, p, q, a, b)
                    total = term if total is None else total + term
            sums[index] = sums[index] + total.astype(F32)
    return tuple(sums)


def feed_forward(scal, taps_own, taps_other, norm, norm_edge, grad, grad_edge, shifts, up_own, up_other, down_own, down_other):
    half = up_own.shape[1] // CHUNK
    steps = 2 * half
    body = jax.ShapeDtypeStruct((4, BODY, D), BF16)

    def own(i):
        return jnp.minimum(i, half - 1)

    def other(i):
        return jnp.maximum(i - half, 0)

    per = D // CHUNK
    plane = pltpu.VMEM((4, PLANE, CHUNK), BF16)
    small = pltpu.VMEM((4, BODY, CHUNK), BF16)
    return pl.pallas_call(
        ffn_kernel,
        grid=(steps,),
        out_shape=(
            body, body,
            jax.ShapeDtypeStruct((steps // per, D, D), BF16),
            jax.ShapeDtypeStruct((steps * CHUNK, D), BF16),
            jax.ShapeDtypeStruct((steps, 16, CHUNK), F32),
        ),
        in_specs=[
            scalars(),
            pl.BlockSpec((16, CHUNK), lambda i: (0, own(i))),
            pl.BlockSpec((16, CHUNK), lambda i: (0, other(i))),
            whole(norm.shape), whole(norm_edge.shape), whole(grad.shape), whole(grad_edge.shape), whole(shifts.shape),
            pl.BlockSpec((D, CHUNK), lambda i: (0, own(i))),
            pl.BlockSpec((D, CHUNK), lambda i: (0, other(i))),
            pl.BlockSpec((CHUNK, D), lambda i: (own(i), 0)),
            pl.BlockSpec((CHUNK, D), lambda i: (other(i), 0)),
        ],
        out_specs=(
            whole(body.shape), whole(body.shape),
            pl.BlockSpec((1, D, CHUNK), lambda i: (i // per, 0, i % per)),
            pl.BlockSpec((CHUNK, D), lambda i: (i, 0)),
            pl.BlockSpec((1, 16, CHUNK), lambda i: (i, 0, 0)),
        ),
        scratch_shapes=[
            plane, plane, plane, plane, small, small, small, pltpu.VMEM((4, EDGE, CHUNK), BF16),
            pltpu.VMEM((4, BODY, D), F32), pltpu.VMEM((4, BODY, D), F32),
            pltpu.VMEM((D, CHUNK), BF16), pltpu.VMEM((CHUNK, D), BF16), pltpu.VMEM((16, CHUNK), BF16),
            pltpu.VMEM((D, 4 * BODY), BF16), pltpu.VMEM((D, 4 * BODY), BF16),
        ],
        compiler_params=params("arbitrary"),
        name="feed_forward",
    )(scal, taps_own, taps_other, norm, norm_edge, grad, grad_edge, shifts, up_own, up_other, down_own, down_other)


def turn_kernel(
    x_ref, attn_ref, ffn_ref, cot_ref, back_ref, mix_ref, perm_ref, mod_ref, weight_ref,
    out_ref, grad_ref, gmix_ref, sums_ref, wgrad_ref,
    wsum,
):
    step = pl.program_id(0)
    gate_one = mod_ref[0, 2:3, :]
    scale = mod_ref[0, 4:5, :]
    gate_two = mod_ref[0, 5:6, :]

    @pl.when(step % 4 == 0)
    def _():
        sums_ref[...] = jnp.zeros_like(sums_ref)

    @pl.when(step == 0)
    def _():
        wsum[...] = jnp.zeros_like(wsum)

    result = None
    for group in range(4):
        attn = attn_ref[group].astype(F32)
        ffn = ffn_ref[group].astype(F32)
        cot = cot_ref[group].astype(F32)
        back = back_ref[group].astype(F32)
        residual = x_ref[group].astype(F32) + gate_one * attn
        low = (residual + gate_two * ffn).astype(BF16)
        part = nn(perm_ref[:, 64 * group : 64 * group + 64], low)
        result = part if result is None else result + part
        normed, inverse = normalize(residual)
        grad = cot + norm_back(back * (1.0 + scale), normed, inverse)
        grad_ref[group] = grad.astype(BF16)
        for row, value in ((0, grad * attn), (1, back), (2, back * normed), (3, cot * ffn)):
            sums_ref[0, row : row + 1, :] += jnp.sum(value, 0, keepdims=True)
        gattn = (grad * gate_one).astype(BF16)
        gmix_ref[group] = nt(gattn, weight_ref[...]).astype(BF16)
        wsum[...] += tn(mix_ref[group], gattn)
    out_ref[...] = result.astype(BF16)

    @pl.when(step == 7)
    def _():
        wgrad_ref[...] = wsum[...].astype(BF16)


def turn(x, attn, ffn, cot, back, mix, perm, mod, weight):
    block = pl.BlockSpec((4, 64, D), lambda i: (0, i, 0))
    body = jax.ShapeDtypeStruct((4, BODY, D), BF16)
    return pl.pallas_call(
        turn_kernel,
        grid=(8,),
        out_shape=(
            jax.ShapeDtypeStruct((2048, D), BF16), body, body,
            jax.ShapeDtypeStruct((2, 8, D), F32), jax.ShapeDtypeStruct((D, D), BF16),
        ),
        in_specs=[block] * 6 + [
            whole(perm.shape), pl.BlockSpec((1, 8, D), lambda i: (i // 4, 0, 0)), whole(weight.shape),
        ],
        out_specs=(
            pl.BlockSpec((256, D), lambda i: (i, 0)), block, block,
            pl.BlockSpec((1, 8, D), lambda i: (i // 4, 0, 0)), whole((D, D)),
        ),
        scratch_shapes=[pltpu.VMEM((D, D), F32)],
        compiler_params=params("arbitrary"),
        name="turn",
    )(x, attn, ffn, cot, back, mix, perm, mod, weight)


def project_back_kernel(gq_ref, gown_ref, gother_ref, mixed_ref, weight_ref, gmixed_ref, wgrad_ref, gsum, turned):
    step = pl.program_id(0)

    @pl.when(step == 0)
    def _():
        gsum[...] = jnp.zeros_like(gsum)

        @pl.loop(0, 8)
        def _(tile):
            rows = pl.ds(pl.multiple_of((tile % 2) * HALF, HALF), HALF)
            cols = pl.ds(pl.multiple_of(tile * HALF, HALF), HALF)
            turned[:, cols] = mixed_ref[tile // 2, rows, :].T

    wsum = None
    for group in range(4):
        gk = (gown_ref[0, 0, group].astype(F32) + gother_ref[0, 0, group].astype(F32)).astype(BF16)
        gv = (gown_ref[0, 1, group].astype(F32) + gother_ref[0, 1, group].astype(F32)).astype(BF16)
        triple = jnp.concatenate([gq_ref[0, group], gk, gv], axis=1)
        gsum[group] += nt(triple, weight_ref[0])
        part = nn(turned[:, BODY * group : BODY * (group + 1)], triple)
        wsum = part if wsum is None else wsum + part
    wgrad_ref[0] = wsum.astype(BF16)

    @pl.when(step == pl.num_programs(0) - 1)
    def _():
        gmixed_ref[...] = gsum[...].astype(BF16)


def project_back(gq, gown, gother, mixed, weight):
    pairs = gq.shape[0]
    kv_spec = pl.BlockSpec((1, 2, 4, BODY, 128), lambda i: (i, 0, 0, 0, 0))
    return pl.pallas_call(
        project_back_kernel,
        grid=(pairs,),
        out_shape=(jax.ShapeDtypeStruct((4, BODY, D), BF16), jax.ShapeDtypeStruct((pairs, D, 384), BF16)),
        in_specs=[
            pl.BlockSpec((1, 4, BODY, 128), lambda i: (i, 0, 0, 0)), kv_spec, kv_spec,
            whole(mixed.shape), pl.BlockSpec((1, D, 384), lambda i: (i, 0, 0)),
        ],
        out_specs=(whole((4, BODY, D)), pl.BlockSpec((1, D, 384), lambda i: (i, 0, 0))),
        scratch_shapes=[pltpu.VMEM((4, BODY, D), F32), pltpu.VMEM((D, 4 * BODY), BF16)],
        compiler_params=params("arbitrary"),
        name="project_back",
    )(gq, gown, gother, mixed, weight)


def back_kernel(
    scal_ref, x_ref, gmixed_ref, gedge_ref, base_ref, shifted_ref, gres_ref, perm_ref, shift_ref, mod_ref, taps_ref,
    out_ref, sums_ref, taps_grad,
    gm, gm_moved, gnorm,
):
    width, gap, long_latent, place = geometry(scal_ref)
    clear_borders(gm)
    clear_borders(gm_moved)
    for group in range(4):
        for half in (0, 1):
            gm[group, pl.ds(body_offset(half, gap), HALF), :] = gmixed_ref[group, half * HALF : (half + 1) * HALF, :]

    @pl.when(long_latent)
    def _():
        for group in range(4):
            gm[group, pl.ds(edge_offset(place), EDGE), :] = gedge_ref[group]

    shift_planes(gm, gm_moved, shift_ref, gap, long_latent, place)

    for lane in range(D // 128):
        lanes = pl.ds(lane * 128, 128)
        kernel = kernel_rows(taps_ref, lanes, 16)

        def back_tile(tile, sums, lanes=lanes, kernel=kernel):
            offset = pl.multiple_of(body_offset(tile // 16, gap) + (tile % 16) * 16, 16)
            rows = pl.ds(pl.multiple_of(tile * 16, 16), 16)
            found = variants(gm, gm_moved, offset, width, 16, lanes)
            for p in (0, 1):
                for q in (0, 1):
                    gnorm[2 * p + q, rows, lanes] = conv_at(found, kernel, p, q, flip=True)
            return taps_at(found, variants(base_ref, shifted_ref, offset, width, 16, lanes), sums)

        sums = lax.fori_loop(0, 32, back_tile, (jnp.zeros((16, 128), F32),) * 9)
        for index in range(9):
            taps_grad[index : index + 1, lanes] = jnp.sum(sums[index], 0, keepdims=True)

    sums_ref[...] = jnp.zeros_like(sums_ref)

    @pl.loop(0, 8)
    def _(block):
        half = block // 4
        scale = mod_ref[half, 1:2, :]
        rows = pl.ds(pl.multiple_of(block * 64, 64), 64)
        result = None
        for group in range(4):
            normed, inverse = normalize(x_ref[group, rows, :].astype(F32))
            back = gnorm[group, rows, :].astype(F32)
            grad = gres_ref[group, rows, :].astype(F32) + norm_back(back * (1.0 + scale), normed, inverse)
            sums_ref[half, 0:1, :] += jnp.sum(back, 0, keepdims=True)
            sums_ref[half, 1:2, :] += jnp.sum(back * normed, 0, keepdims=True)
            part = nn(perm_ref[:, 64 * group : 64 * group + 64], grad.astype(BF16))
            result = part if result is None else result + part
        out_ref[pl.ds(pl.multiple_of(block * 256, 256), 256), :] = result.astype(BF16)


def back(scal, x, gmixed, gedge, base, shifted, gres, perm, shifts, mod, taps):
    arrays = (x, gmixed, gedge, base, shifted, gres, perm, shifts, mod, taps)
    plane = pltpu.VMEM((4, PLANE, D), BF16)
    return pl.pallas_call(
        back_kernel,
        out_shape=(
            jax.ShapeDtypeStruct((2048, D), BF16),
            jax.ShapeDtypeStruct((2, 8, D), F32),
            jax.ShapeDtypeStruct((16, D), F32),
        ),
        in_specs=[scalars()] + [pl.BlockSpec(memory_space=pltpu.VMEM)] * len(arrays),
        out_specs=(pl.BlockSpec(memory_space=pltpu.VMEM),) * 3,
        scratch_shapes=[plane, plane, pltpu.VMEM((4, BODY, D), BF16)],
        compiler_params=params(),
        name="back",
    )(scal, *arrays)


MESH = pl.DeviceIdType.MESH


def chip_grid(count):
    return {16: (4, 2, 2), 64: (4, 4, 4)}.get(count, (count, 1, 1))


def reduce_gather_kernel(grid, parts_ref, sent_ref, sum_ref, all_ref, *scratch):
    (first, work, r1a, r1b, w1a, w1b, r2a, r2b, w2, r3, gz, gx, gy) = scratch[:13]
    sends, recvs = scratch[13:]
    deep, tall, broad = grid
    low = deep // 2
    wide = lax.axis_index("wide")
    place = lax.axis_index("narrow")
    z, y, x = wide // (tall * broad), (wide // broad) % tall, wide % broad

    def chip(zz, yy, xx):
        return {"wide": (zz * tall + yy) * broad + xx, "narrow": place}

    def along_x(step):
        return chip(z, y, (x + step) % broad)

    def along_y(step):
        return chip(z, (y + step) % tall, x)

    def along_z(step):
        return chip((z + step) % deep, y, x)

    sibling = {"wide": wide, "narrow": 1 - place}
    partners = (
        [sibling]
        + [along_x(step) for step in range(1, broad)]
        + [along_y(step) for step in range(1, tall)]
        + [along_z(step) for step in range(1, deep)]
    )
    barrier = pltpu.get_barrier_semaphore()
    for partner in partners:
        pl.semaphore_signal(barrier, inc=1, device_id=partner, device_id_type=MESH)
    pl.semaphore_wait(barrier, len(partners))

    count = [0]

    def send(source, target, partner):
        copy = pltpu.make_async_remote_copy(
            src_ref=source, dst_ref=target, send_sem=sends.at[count[0]], recv_sem=recvs.at[count[0]],
            device_id=partner, device_id_type=MESH,
        )
        count[0] += 1
        copy.start()
        return copy

    def wait(copies):
        for copy in copies:
            copy.wait()

    def add(target, *sources):
        total = sources[0].astype(F32)
        for source in sources[1:]:
            total = total + source.astype(F32)
        return total.astype(target.dtype)

    gz[z] = sent_ref[...]
    halves = ((0, low), (low, deep))
    swaps = [send(parts_ref.at[1, start:stop], first.at[start:stop], sibling) for start, stop in halves]
    gathers = [send(sent_ref, gz.at[z], along_z(step)) for step in range(1, deep)]

    def add_first(start, stop):
        for zz in range(start, stop):

            @pl.loop(0, tall * broad)
            def _(at, zz=zz):
                yy, xx = at // broad, at % broad
                work[zz, yy, xx] = add(work, parts_ref[0, zz, yy, xx], first[zz, yy, xx])

    swaps[0].wait()
    add_first(0, low)
    one_a = [send(work.at[0:low, :, (x + s) % broad], r1a.at[s - 1], along_x(s)) for s in range(1, broad)]
    swaps[1].wait()
    add_first(low, deep)
    one_b = [send(work.at[low:deep, (y + s) % tall], r1b.at[s - 1], along_y(s)) for s in range(1, tall)]
    wait(gathers)
    gx[x] = gz[...]
    gathers = [send(gz, gx.at[x], along_x(step)) for step in range(1, broad)]

    wait(one_a)
    for zz in range(low):
        for yy in range(tall):
            w1a[zz, yy] = add(w1a, work[zz, yy, x], *[r1a[s, zz, yy] for s in range(broad - 1)])
    two_a = [send(w1a.at[:, (y + s) % tall], r2a.at[s - 1], along_y(s)) for s in range(1, tall)]
    wait(one_b)
    for zz in range(deep - low):
        for xx in range(broad):
            w1b[zz, xx] = add(w1b, work[low + zz, y, xx], *[r1b[s, zz, xx] for s in range(tall - 1)])
    two_b = [send(w1b.at[:, (x + s) % broad], r2b.at[s - 1], along_x(s)) for s in range(1, broad)]
    wait(gathers)
    gy[y] = gx[...]
    gathers = [send(gx, gy.at[y], along_y(step)) for step in range(1, tall)]

    wait(two_a)
    for zz in range(low):
        w2[zz] = add(w2, w1a[zz, y], *[r2a[s, zz] for s in range(tall - 1)])
    wait(two_b)
    for zz in range(deep - low):
        w2[low + zz] = add(w2, w1b[zz, x], *[r2b[s, zz] for s in range(broad - 1)])
    three = [send(w2.at[(z + s) % deep], r3.at[s - 1], along_z(s)) for s in range(1, deep)]
    wait(gathers)
    all_ref[place] = gy[...]
    gathers = [send(gy, all_ref.at[place], sibling)]
    wait(three)
    sum_ref[...] = add(sum_ref, w2[z], *[r3[s] for s in range(deep - 1)])
    wait(gathers)


def reduce_gather(parts, sent):
    wide_count, rows, lanes = parts.shape[1:]
    deep, tall, broad = grid = chip_grid(wide_count)
    low = deep // 2
    unit = (rows, lanes)
    copies = 2 + 2 * (broad - 1 + tall - 1) + (deep - 1) + (deep - 1) + (broad - 1) + (tall - 1) + 1

    def slots(count, *shape):
        return pltpu.VMEM((max(count, 1), *shape, *unit), BF16)

    row = sent.shape
    result = pl.pallas_call(
        functools.partial(reduce_gather_kernel, grid),
        out_shape=(
            jax.ShapeDtypeStruct(unit, F32),
            jax.ShapeDtypeStruct((2, tall, broad, deep, *row), BF16),
        ),
        in_specs=[pl.BlockSpec(memory_space=pltpu.VMEM)] * 2,
        out_specs=(pl.BlockSpec(memory_space=pltpu.VMEM),) * 2,
        scratch_shapes=[
            pltpu.VMEM((*grid, *unit), BF16), pltpu.VMEM((*grid, *unit), BF16),
            slots(broad - 1, low, tall), slots(tall - 1, deep - low, broad),
            pltpu.VMEM((low, tall, *unit), BF16), pltpu.VMEM((deep - low, broad, *unit), BF16),
            slots(tall - 1, low), slots(broad - 1, deep - low),
            pltpu.VMEM((deep, *unit), BF16), slots(deep - 1),
            pltpu.VMEM((deep, *row), BF16), pltpu.VMEM((broad, deep, *row), BF16),
            pltpu.VMEM((tall, broad, deep, *row), BF16),
            pltpu.SemaphoreType.DMA((copies,)), pltpu.SemaphoreType.DMA((copies,)),
        ],
        compiler_params=pltpu.CompilerParams(
            collective_id=1, has_side_effects=True, vmem_limit_bytes=VMEM_BYTES
        ),
        name="reduce_gather",
    )(parts.reshape(2, *grid, *unit), sent)
    return result[0], result[1].reshape(-1, *row)


def square_sum_kernel(grid, *refs):
    count = len(refs) - 6
    grads = refs[:count]
    out_ref, mine, near, far, sends, recvs = refs[count:]
    deep, tall, broad = grid
    wide = lax.axis_index("wide")
    place = lax.axis_index("narrow")
    z, across = wide // (tall * broad), wide % (tall * broad)
    line = z * 2 + place

    def near_device(step):
        other = (line + step) % (2 * deep)
        return {"wide": (other // 2) * (tall * broad) + across, "narrow": other % 2}

    def far_device(step):
        return {"wide": z * (tall * broad) + (across + step) % (tall * broad), "narrow": place}

    nears = [near_device(step) for step in range(1, 2 * deep)]
    fars = [far_device(step) for step in range(1, tall * broad)]
    barrier = pltpu.get_barrier_semaphore()
    for partner in nears + fars:
        pl.semaphore_signal(barrier, inc=1, device_id=partner, device_id_type=MESH)

    total = jnp.zeros((), F32)
    for grad in grads:
        total = total + jnp.sum(grad[...] * grad[...])
    mine[...] = jnp.full((8, 128), total, F32)
    pl.semaphore_wait(barrier, len(nears + fars))

    def exchange(slots, partners, first):
        copies = []
        for step, partner in enumerate(partners):
            copy = pltpu.make_async_remote_copy(
                src_ref=mine, dst_ref=slots.at[step], send_sem=sends.at[first + step],
                recv_sem=recvs.at[first + step], device_id=partner, device_id_type=MESH,
            )
            copy.start()
            copies.append(copy)
        for copy in copies:
            copy.wait()
        value = mine[...]
        for step in range(len(partners)):
            value = value + slots[step]
        return value

    mine[...] = exchange(near, nears, 0)
    out_ref[...] = exchange(far, fars, len(nears))


def square_sum(wide_count, grads):
    deep, tall, broad = grid = chip_grid(wide_count)
    near, far = 2 * deep - 1, tall * broad - 1
    return pl.pallas_call(
        functools.partial(square_sum_kernel, grid),
        out_shape=jax.ShapeDtypeStruct((8, 128), F32),
        in_specs=[pl.BlockSpec(memory_space=pltpu.VMEM)] * len(grads),
        out_specs=pl.BlockSpec(memory_space=pltpu.VMEM),
        scratch_shapes=[
            pltpu.VMEM((8, 128), F32), pltpu.VMEM((near, 8, 128), F32), pltpu.VMEM((max(far, 1), 8, 128), F32),
            pltpu.SemaphoreType.DMA((near + far,)), pltpu.SemaphoreType.DMA((near + far,)),
        ],
        compiler_params=pltpu.CompilerParams(
            collective_id=2, has_side_effects=True, vmem_limit_bytes=VMEM_BYTES
        ),
        name="square_sum",
    )(*grads)


def adamw_kernel(rates, square_ref, *refs):
    clip_limit = PARAMS**0.5
    norm = jnp.sqrt(square_ref[0:1, 0:1])
    factor = clip_limit / jnp.maximum(norm, clip_limit)
    count = len(rates)
    ins, outs = refs[: 4 * count], refs[4 * count :]
    for index, rate in enumerate(rates):
        grad, master, first, second = ins[4 * index : 4 * index + 4]
        scaled = grad[...] * factor
        first_new = BETA_ONE * first[...] + (1.0 - BETA_ONE) * scaled
        second_new = BETA_TWO * second[...] + (1.0 - BETA_TWO) * scaled * scaled
        ratio = (first_new * (1.0 / (1.0 - BETA_ONE**STEP))) / (
            jnp.sqrt(second_new * (1.0 / (1.0 - BETA_TWO**STEP))) + ADAM_EPS
        )
        master_new = master[...] - rate * (ratio + WEIGHT_DECAY * master[...])
        first_out, second_out, master_out, copy_out = outs[4 * index : 4 * index + 4]
        first_out[...] = first_new
        second_out[...] = second_new
        master_out[...] = master_new
        copy_out[...] = master_new.astype(BF16)


def adamw(square, grads, states, rates):
    arrays = [array for grad, state in zip(grads, states) for array in (grad, *state)]
    shapes = [
        jax.ShapeDtypeStruct(grad.shape, dtype) for grad in grads for dtype in (F32, F32, F32, BF16)
    ]
    space = pl.BlockSpec(memory_space=pltpu.VMEM)
    return pl.pallas_call(
        functools.partial(adamw_kernel, rates),
        out_shape=shapes,
        in_specs=[space] * (1 + len(arrays)),
        out_specs=[space] * len(shapes),
        compiler_params=params(),
        name="adamw",
    )(square, *arrays)


def timestep_code(stamps, channels):
    half_dim = channels // 2
    scales = jnp.exp(-jnp.log(10000.0) * jnp.arange(half_dim, dtype=F32) / half_dim)
    angles = stamps.astype(F32)[:, None] * scales[None, :]
    return jnp.concatenate([jnp.cos(angles), jnp.sin(angles)], axis=1)


def one_hot_rows(source, columns, valid=None):
    hit = source[:, None] == jnp.arange(columns, dtype=jnp.int32)[None, :]
    if valid is not None:
        hit = jnp.logical_and(hit, valid[:, None])
    return hit.astype(BF16)


def permutation(long_latent):
    row = jnp.arange(256, dtype=jnp.int32)
    p, q, s = row // 128, (row // 64) % 2, row % 64
    big = (2 * (s // 32) + p) * 64 + 2 * (s % 32) + q
    small = (2 * (s // 16) + p) * 32 + 2 * (s % 16) + q
    return one_hot_rows(jnp.where(long_latent, big, small), 256)


def edge_permutation():
    row = jnp.arange(128, dtype=jnp.int32)
    return one_hot_rows((row // 64) * 64 + 2 * (row % 32) + (row // 32) % 2, 128)


def shift_matrices(width):
    row = jnp.arange(256, dtype=jnp.int32)
    column = row % width
    return jnp.stack([one_hot_rows(row + 1, 256, column != width - 1), one_hot_rows(row - 1, 256, column != 0)])


def pair_columns(weight):
    split = weight.reshape(weight.shape[0], -1, 2, 3, HS)
    return split.transpose(1, 0, 3, 2, 4).reshape(-1, weight.shape[0], 6 * HS)


def head_columns(paired):
    split = paired.reshape(paired.shape[0], paired.shape[1], 3, 2, HS)
    return split.transpose(1, 0, 3, 2, 4).reshape(paired.shape[1], -1)


def tap_rows(kernel):
    return jnp.pad(kernel.T, ((0, 7), (0, 0)))


def per_device(tokens, cotangent, size_tags, timesteps, labels, *weights_and_states):
    modulator, class_table, mix_kernel, heads_in, heads_out, up_weight, hidden_kernel, down_weight = weights_and_states[:8]
    states = [weights_and_states[8 + 3 * i : 11 + 3 * i] for i in range(8)]
    wide_count = lax.axis_size("wide")
    wide = lax.axis_index("wide")
    place = lax.axis_index("narrow")
    cell = wide * 2 + place
    cells = wide_count * 2

    def swap(value):
        return lax.ppermute(value, "narrow", [(0, 1), (1, 0)])

    def boundary(body):
        return jnp.where(place == 0, body[:, BODY - EDGE :], body[:, :EDGE])

    edge = swap(jnp.where(place == 0, tokens[-4 * EDGE :], tokens[: 4 * EDGE]))
    hin_own = pair_columns(heads_in)
    hin = jnp.concatenate([hin_own, swap(hin_own)], axis=0)
    hout = jnp.concatenate([heads_out, swap(heads_out)], axis=0)
    up_other = swap(up_weight)
    down_other = swap(down_weight)
    taps_own = tap_rows(hidden_kernel)
    taps_other = swap(taps_own)
    mix_taps = tap_rows(mix_kernel)

    long_latent = size_tags[0] > SIDE * SIDE
    width = jnp.where(long_latent, SIDE, SIDE // 2)
    gap = jnp.where(long_latent, 0, 16)
    scal = jnp.stack([width, gap, long_latent.astype(jnp.int32), place]).astype(jnp.int32)
    perm = permutation(long_latent)
    perm_back = perm.T
    shifts = shift_matrices(width)
    embedded = timestep_code(timesteps, D) + class_table[:, labels].astype(F32).T
    cond_low = jax.nn.silu(embedded).astype(BF16)
    modulation = jnp.dot(cond_low, modulator, preferred_element_type=F32).reshape(-1, 6, D)
    mod = jnp.pad(modulation, ((0, 0), (0, 2), (0, 0)))

    x, mixed, base, shifted, q, kv = front(
        scal, tokens, edge, perm, edge_permutation(), shifts, mod, mix_taps, hin
    )
    kv_other = swap(kv)
    attended, logs = attention(scal, q, kv, kv_other)
    attn, norm, cot, grad_ffn = middle(x, attended, cotangent, perm, mod, hout)
    norm_edge, grad_edge = swap((boundary(norm), boundary(grad_ffn)))
    ffn, back_norm, up_grad, down_grad, taps_grad = feed_forward(
        scal, taps_own, taps_other, norm, norm_edge, grad_ffn, grad_edge, shifts, up_weight, up_other, down_weight, down_other
    )

    output, grad_residual, grad_attended, sums_two, hout_grad = turn(
        x, attn, ffn, cot, back_norm, attended, perm_back, mod, hout
    )
    rows = D // wide_count
    half = FF // 2
    up_sum = up_grad[:2].astype(F32) + swap(up_grad[2:]).astype(F32)
    down_sum = down_grad[:half].astype(F32) + swap(down_grad[half:]).astype(F32)
    hout_sum = hout_grad[: D // 2].astype(F32) + swap(hout_grad[D // 2 :]).astype(F32)
    tap_half = taps_grad.shape[0] // 2
    taps_sum = taps_grad[:tap_half, :9] + swap(taps_grad[tap_half:, :9])
    tap_part = taps_sum.transpose(0, 2, 1).reshape(wide_count, -1)
    tap_part = jnp.pad(tap_part, ((0, 0), (0, -tap_part.shape[1] % D)))
    grads = jnp.concatenate(
        [
            up_sum.reshape(2, wide_count, rows, D).transpose(1, 0, 2, 3).reshape(wide_count, 2 * rows, D),
            down_sum.reshape(wide_count, -1, D),
            hout_sum.reshape(wide_count, -1, D),
            tap_part.reshape(wide_count, -1, D),
        ],
        axis=1,
    )
    pad = -grads.shape[1] % 16
    grads = jnp.pad(grads, ((0, 0), (0, pad), (0, 0))).astype(BF16)
    grads, grad_attended = lax.optimization_barrier((grads, grad_attended))
    mine = lax.psum_scatter(grads, "wide", scatter_dimension=0, tiled=False)

    gq, gkv, gkv_other = attention_back(scal, q, kv, kv_other, attended, grad_attended, logs)
    gmixed, hin_grad = project_back(gq, gkv, swap(gkv_other), mixed, hin)
    gmixed_edge = swap(boundary(gmixed))
    input_grad, sums_one, mix_grad = back(
        scal, x, gmixed, gmixed_edge, base, shifted, grad_residual, perm_back, shifts, mod, mix_taps
    )

    modulation_two_grad = sums_two[:, 1:3].reshape(-1, 2 * D)
    own = D // cells
    hin_rows = 3 * rows
    hin_parts = hin_grad.reshape(2, -1, wide_count, rows, 6 * HS).transpose(0, 2, 1, 3, 4)
    hin_parts = hin_parts.reshape(2, wide_count, hin_rows, 6 * HS)
    hin_parts = jnp.pad(hin_parts, ((0, 0), (0, 0), (0, -hin_rows % 16), (0, 0)))
    mix_parts = mix_grad[:9].T.reshape(wide_count, 2, 1, own * 9).transpose(1, 0, 2, 3)
    mix_parts = jnp.where(place == 0, mix_parts, mix_parts[::-1]).astype(BF16)
    mix_parts = jnp.pad(mix_parts, ((0, 0), (0, 0), (0, 15), (0, 6 * HS - own * 9)))
    parts = jnp.concatenate([hin_parts, mix_parts], axis=2)
    slope = jax.vjp(jax.nn.silu, embedded)[1](jnp.ones_like(embedded))[0]
    blocks = jnp.concatenate([sums_one[:, 0:2], sums_two[:, 0:4]], axis=1).transpose(1, 0, 2).reshape(12, D)
    digits = jnp.stack([labels // 32, labels % 32], axis=1).astype(F32)
    digits = jnp.pad(digits, ((0, 14), (0, 126)))
    sent = jnp.concatenate([jnp.concatenate([blocks, cond_low.astype(F32), slope], axis=0), digits], axis=1)
    summed, everyone = reduce_gather(parts, sent.astype(BF16))
    everyone = everyone.transpose(1, 0, 2)
    all_modulation = everyone[:12, :, :D].reshape(6, 2, -1, D)
    mine_columns = lax.dynamic_slice_in_dim(everyone[12:, :, :D], cell * own, own, 2)
    all_cond = mine_columns[:2]
    all_slope = mine_columns[2:].astype(F32)
    all_digits = everyone[:2, :, D : D + 2].astype(jnp.int32)
    all_labels = (all_digits[..., 0] * 32 + all_digits[..., 1])[..., None]
    modulator_mine = jnp.einsum("fcd,kfcl->dkl", all_cond, all_modulation, preferred_element_type=F32).reshape(own, -1)
    modulator_rows = lax.dynamic_slice_in_dim(modulator, cell * own, own, 0).reshape(own, 6, D)
    all_embedded = all_slope * jnp.einsum(
        "kfcl,dkl->fcd", all_modulation, modulator_rows, preferred_element_type=F32
    )
    chosen = (all_labels == jnp.arange(class_table.shape[1], dtype=jnp.int32)).astype(F32)
    class_mine = jnp.einsum(
        "fcd,fck->dk", all_embedded, chosen, precision=lax.Precision.HIGHEST, preferred_element_type=F32
    )
    mix_mine = summed[-16, : own * 9].reshape(own, 9)
    hin_mine = summed[:hin_rows].reshape(-1, rows, 6 * HS)
    mine = mine.astype(F32)

    at = 2 * rows
    up_mine = jnp.concatenate([mine[:rows], mine[rows:at]], axis=1)
    down_mine = mine[at : at + half // wide_count]
    at += half // wide_count
    hout_mine = mine[at : at + D // 2 // wide_count]
    at += D // 2 // wide_count
    hidden = half // wide_count
    taps_mine = mine[at:].reshape(-1)[: hidden * 9].reshape(hidden, 9)
    shards = (
        modulator_mine, class_mine, mix_mine, head_columns(hin_mine),
        hout_mine, up_mine, taps_mine, down_mine,
    )
    square = square_sum(wide_count, shards)
    grad_norm = jnp.sqrt(square[0, 0])
    step_rates = (
        D ** (-0.5), 1.0, 1.0 / 3.0, D ** (-0.5), (D // 32) ** (-0.5), D ** (-0.5), 1.0 / 3.0, FF ** (-0.5),
    )
    flat = adamw(square, shards, states, step_rates)
    return (output, input_grad, grad_norm, *flat, modulation_two_grad)


def solution(mesh):
    both = P(("wide", "narrow"), None)
    turned = P(("narrow", "wide"), None)
    grid = P("wide", "narrow")
    places = (both, both, both, grid, turned, grid, turned, turned)
    in_specs = (
        both, both, P("wide"), P(("wide", "narrow")), P(("wide", "narrow")),
        P(), P(), P(), P(None, "narrow"), P("narrow", None), P(None, "narrow"), P("narrow", None), P("narrow", None),
        *[place for place in places for _ in range(3)],
    )
    out_specs = (both, both, P(), *[place for place in places for _ in range(4)], both)
    return jax.shard_map(per_device, mesh=mesh, in_specs=in_specs, out_specs=out_specs, check_vma=False)
```

time: 2010 us -> 660 us (0.33)
  other arithmetic: 656 us -> 28.7 us
  matrix products: 519 us -> 8.07 us
  Pallas kernels: 0 us -> 510 us
  waiting for transfers between devices: 447 us -> 19.6 us
  local copies, waits for them, and re-layouts: 194 us -> 61.5 us
  blocking collectives: 123 us -> 0 us
  loops' own time: 35.6 us -> 0 us
    dot_general x45 -> x4, matrix products: 519 us -> 8.07 us  [the longest x1 4.02 us: per_device(): jnp.dot(cond_low, modulator, preferred_element_type=F32).reshape(-1, 6, D)]
    pallas_call x0 -> x11, Pallas kernels: none -> 510 us  [the longest x1 175 us: feed_forward(): pl.pallas_call(ffn_kernel, grid=(steps,), out_shape=(body, body, jax.Shap...]
    psum x2 -> x0, waiting for transfers between devices: 372 us -> none  [the longest x1 263 us: per_device(): lax.psum(shared_grads + (square_sum(local_part),), ('wide', 'narrow'))]
    reduce_sum x23 -> x0, other arithmetic: 243 us -> none  [the longest x4 139 us: conv_taps(): jnp.sum(padded[:, offset // 3:offset // 3 + row_count, offset % 3:offset...]
    add x5 -> x3, other arithmetic: 235 us -> 0.02 us  [the longest x1 0.01 us: per_device(): all_labels = (all_digits[..., 0] * 32 + all_digits[..., 1])[..., None]]
    convert_element_type x22 -> x6, other arithmetic: 158 us -> 3.19 us  [the longest x2 1.46 us: one_hot_rows(): return hit.astype(BF16)]
    psum x3 -> x0, blocking collectives: 123 us -> none  [the longest x1 81.1 us: per_device(): lax.psum((split_grads[0], split_grads[1], split_grads[2], split_grads[3],...]
    reshape x9 -> x14, local copies, waits for them, and re-layouts: 92 us -> 16.9 us  [the longest x1 4.61 us: reduce_gather(): return (result[0], result[1].reshape(-1, *row))]
  transfers between devices with their start and end apart: 10 -> 16, of which waited for: 7 -> 5; matrix products, arithmetic and copies ran while one was open for 20% -> 11% of each run, Pallas kernels for 0% -> 44%
where the time goes in v1:
time: 660 us; the launch traced here: 651 us
  Pallas kernels  510 us (77%)
  local copies, waits for them, and re-layouts  61.5 us (9%)
  other arithmetic  28.7 us (4%)
  waiting for transfers between devices  19.6 us (3%)
  between operations  17.6 us (3%)
  matrix products  8.07 us (1%)
    pallas_call x1, Pallas kernels, feed_forward(): pl.pallas_call(ffn_kernel, grid=(steps,), out_shape=(body, body, jax.Shap...  175 us
    pallas_call x1, Pallas kernels, attention_back(): pl.pallas_call(attend_back_kernel, grid=(pairs, 4), out_shape=(jax.ShapeD...  90.3 us
    pallas_call x1, Pallas kernels, attention(): pl.pallas_call(attend_kernel, grid=(pairs, 4), out_shape=(jax.ShapeDtypeS...  46.1 us
    pallas_call x1, Pallas kernels, reduce_gather(): pl.pallas_call(functools.partial(reduce_gather_kernel, grid), out_shape=(...  41.6 us
    pallas_call x1, Pallas kernels, front(): pl.pallas_call(front_kernel, grid=(pairs,), out_shape=(body, body, plane,...  32 us
    pallas_call x1, Pallas kernels, turn(): pl.pallas_call(turn_kernel, grid=(8,), out_shape=(jax.ShapeDtypeStruct((2...  31.1 us
    pallas_call x1, Pallas kernels, back(): pl.pallas_call(back_kernel, out_shape=(jax.ShapeDtypeStruct((2048, D), BF...  30.9 us
    pallas_call x1, Pallas kernels, project_back(): pl.pallas_call(project_back_kernel, grid=(pairs,), out_shape=(jax.ShapeDt...  28.9 us
  transfers between devices with their start and end apart: 16, of which 5 were waited for; matrix products, arithmetic and copies ran while one was open for 11% of the time, Pallas kernels for 44%

profile of v1, /device:TPU:0, one launch (start us, length us, event | category | flops | bytes accessed | tf_op | source)
XLA Modules:
  0.0 650.6 jit_solution(18393514656200534522)
XLA Ops:
  7.3 1.2 slice_select_fusion.3
  9.0 2.6 copy.96
  11.6 1.3 copy.97
  12.9 2.8 copy.99
  16.6 4.0 fusion.41
  25.9 3.7 pad_maximum_fusion.1.weight_ref
  29.5 32.0 %front.1 = (bf16[4,512,768]{2,1,0:T(8,128)(2,1)}, bf16[4,512,768]{2,1,0:T(8,128)(2,1)}, bf16[4,592,768]{2,1,0:T(8,128)(2,1)}, bf16[4,592,768]{2,1,0:T(8,128)(2,1...) custom-call(s32[4]{0:T(128)} %pad_add_fusion.scal_ref, bf16[2048,768]{1,0:T(8,128)(2,1)} %x_ref.1, ...), custom_call_target="tpu_custom_call" | custom-call | tf_op jit(solution)/shard_map/front/pallas_call | solution.py:204
  62.6 1.1 constant_dynamic-update-slice_fusion.1
  63.7 12.2 %collective-permute-done.3 = bf16[384,768]{1,0:T(8,128)(2,1)S(1)} collective-permute-done((bf16[384,768]{1,0:T(8,128)(2,1)}, bf16[384,768]{1,0:T(8,128)(2,1)S(1)}, u32[]{:S(2)}, u32[]{:S(2)}) %collective-permute-start.3) | collective-permute-done | bytes 589856 | tf_op jit(solution)/shard_map/ppermute | solution.py:1151
  76.4 46.1 %attention.1 = (bf16[4,512,768]{2,1,0:T(8,128)(2,1)}, bf16[6,4,512,128]{3,2,1,0:T(8,128)(2,1)}) custom-call(s32[4]{0:T(128)} %pad_add_fusion.scal_ref, bf16[6,4,512,128]{3,2,1,0:T(8,128)(2,1)} %get-tuple-element.103.q_ref, bf16[6,2,4,512,128]{4,3,2,1,0:T(8,128)(2,1)} %get-tuple-element.104.own_ref, bf16[6,2,4,512,128]{4,3,2,1,0:T(8,128)(2,1)} %collective-permute-done.2.other_ref), custom_call_target="tpu_custom_call" | custom-call | tf_op jit(solution)/shard_map/attention/pallas_call | solution.py:301
  122.5 15.6 %middle.1 = (bf16[4,512,768]{2,1,0:T(8,128)(2,1)}, bf16[4,512,768]{2,1,0:T(8,128)(2,1)}, bf16[4,512,768]{2,1,0:T(8,128)(2,1)}, bf16[4,512,768]{2,1,0:T(8,128)(2,1)}) custom-call(bf16[4,512,768]{2,1,0:T(8,128)(2,1)} %get-tuple-element.102.x_ref, bf16[4,512,768]{2,1,0:T(8,128)(2,1)} %get-tuple-element.105.mix_ref, bf16[2048,768]{1,0:T(8,128)(2,1)} %cot_ref.1, ...), custom_call_target="tpu_custom_call" | custom-call | tf_op jit(solution)/shard_map/middle/pallas_call | solution.py:429
  138.1 1.0 slice_select_fusion.2
  139.6 1.0 slice_select_fusion.1
  143.6 174.6 %feed_forward.1 = (bf16[4,512,768]{2,1,0:T(8,128)(2,1)}, bf16[4,512,768]{2,1,0:T(8,128)(2,1)}, bf16[4,768,768]{2,1,0:T(8,128)(2,1)}, bf16[3072,768]{1,0:T(8,128)(2,1)}, f32[12,16,256]{2,1,0:T(8,128)}) custom-call(s32[4]{0:T(128)} %pad_add_fusion.scal_ref, bf16[16,1536]{1,0:T(8,128)(2,1)} %copy-done.9, bf16[16,1536]{1,0:T(8,128)(2,1)} %copy-done.11, ...), custom_call_target="tpu_custom_call" | custom-call | tf_op jit(solution)/shard_map/feed_forward/pallas_call | solution.py:617
  318.2 3.4 slice.130
  321.9 1.6 slice.132
  323.7 31.1 %turn.1 = (bf16[2048,768]{1,0:T(8,128)(2,1)}, bf16[4,512,768]{2,1,0:T(8,128)(2,1)}, bf16[4,512,768]{2,1,0:T(8,128)(2,1)}, f32[2,8,768]{2,1,0:T(8,128)}, bf16[768,768]{1,0:T(8,128)(2,1)}) custom-call(bf16[4,512,768]{2,1,0:T(8,128)(2,1)} %get-tuple-element.102.x_ref, bf16[4,512,768]{2,1,0:T(8,128)(2,1)} %get-tuple-element.106.attn_ref, ...), custom_call_target="tpu_custom_call" | custom-call | tf_op jit(solution)/shard_map/turn/pallas_call | solution.py:699
  354.9 1.1 slice.134
  356.6 1.6 collective-permute-done.12
  359.0 1.4 add_convert_fusion.2
  360.4 3.0 add_convert_fusion.1
  363.7 2.3 add_convert_fusion
  365.9 3.0 fusion.6
  369.1 90.3 %attention_back.1 = (bf16[6,4,512,128]{3,2,1,0:T(8,128)(2,1)}, bf16[6,2,4,512,128]{4,3,2,1,0:T(8,128)(2,1)}, bf16[6,2,4,512,128]{4,3,2,1,0:T(8,128)(2,1)}) custom-call(s32[4]{0:T(128)} %pad_add_fusion.scal_ref, bf16[6,4,512,128]{3,2,1,0:T(8,128)(2,1)} %get-tuple-element.103.q_ref, bf16[6,2,4,512,128]{4,3,2,1,0:T(8,128)(2,1)} %get-tuple-element.104.own_ref, ...), custom_call_target="tpu_custom_call" | custom-call | tf_op jit(solution)/shard_map/attention_back/pallas_call | solution.py:393
  465.5 4.5 collective-permute-done.13.gother_ref
  469.9 28.9 %project_back.1 = (bf16[4,512,768]{2,1,0:T(8,128)(2,1)}, bf16[6,768,384]{2,1,0:T(8,128)(2,1)}) custom-call(bf16[6,4,512,128]{3,2,1,0:T(8,128)(2,1)} %get-tuple-element.120.gq_ref, bf16[6,2,4,512,128]{4,3,2,1,0:T(8,128)(2,1)} %get-tuple-element.121.gown_ref, bf16[6,2,4,512,128]{4,3,2,1,0:T(8,128)(2,1)} %collective-permute-done.13.gother_ref, ...), custom_call_target="tpu_custom_call" | custom-call | tf_op jit(solution)/shard_map/project_back/pallas_call | solution.py:750
  498.9 1.1 slice_select_fusion
  500.9 4.1 copy.102
  505.8 30.9 %back.1 = (bf16[2048,768]{1,0:T(8,128)(2,1)}, f32[2,8,768]{2,1,0:T(8,128)}, f32[16,768]{1,0:T(8,128)}) custom-call(s32[4]{0:T(128)} %pad_add_fusion.scal_ref, bf16[4,512,768]{2,1,0:T(8,128)(2,1)} %get-tuple-element.102.x_ref, bf16[4,512,768]{2,1,0:T(8,128)(2,1)} %get-tuple-element.124.gmixed_ref, bf16[4,32,768]{2,1,0:T(8,128)(2,1)} %copy-done.8, ...), custom_call_target="tpu_custom_call" | custom-call | tf_op jit(solution)/shard_map/back/pallas_call | solution.py:823
  539.6 4.5 pad_maximum_fusion.parts_ref
  544.1 41.6 %reduce_gather.1 = (f32[160,384]{1,0:T(8,128)}, bf16[2,2,2,4,16,896]{5,4,3,2,1,0:T(8,128)(2,1)}) custom-call(bf16[2,4,2,2,160,384]{5,4,3,2,1,0:T(8,128)(2,1)} %pad_maximum_fusion.parts_ref, bf16[16,896]{1,0:T(8,128)(2,1)} %fusion.17.sent_ref), custom_call_target="tpu_custom_call" | custom-call | tf_op jit(solution)/shard_map/reduce_gather/pallas_call | solution.py:962
  585.7 4.6 copy.108
  590.3 3.3 slice.168
  593.6 1.2 slice.167
  594.8 2.4 copy.109
  600.9 2.1 fusion.7
  603.9 1.0 convolution_bitcast_fusion.refs_0_
  609.6 13.2 %square_sum.1.square_ref = f32[8,128]{1,0:T(8,128)} custom-call(f32[24,4608]{1,0:T(8,128)} %convolution_bitcast_fusion.refs_0_, f32[24,1000]{1,0:T(8,128)} %convolution_bitcast_fusion.1.refs_1_.refs_4_, f32[24,9]{1,0:T(8,128)} %reshape_squeeze.3.refs_2_.refs_8_, f32[48,1152]{1,0:T(8,128)} %reshape.446.refs_3_.refs_12_, ...), custom_call_target="tpu_custom_call" | custom-call | tf_op jit(solution)/shard_map/square_sum/pallas_call | solution.py:1040
  622.8 1.3 slice.161
  624.1 6.1 adamw.1
  630.2 1.4 copy.117
  631.5 1.4 copy.118
  632.9 1.4 copy.119
  634.3 1.5 copy.121
  635.8 1.5 copy.122
  637.2 1.5 copy.123
  638.7 1.4 copy.120
  640.1 1.4 copy.124
  (156 shorter events, 32.8 us)
Async XLA Ops:
  7.2 8.7 %copy-start = (bf16[768,1000]{0,1:T(8,128)(2,1)S(1)}, bf16[768,1000]{0,1:T(8,128)(2,1)}, u32[]{:S(2)}) copy-start(bf16[768,1000]{0,1:T(8,128)(2,1)} %param.43) | copy-start | bytes 4608004
  7.2 597.7 %reduce-scatter.2.cloned.1.call-start = ((), (), s32[]{:S(2)}) async-start(), calls=%async_computation.1 | async-start | bytes 5849088 | tf_op jit(solution)/shard_map/reduce_scatter | solution.py:1213
  8.4 21.1 %collective-permute-start = (bf16[128,768]{1,0:T(8,128)(2,1)S(1)}, bf16[128,768]{1,0:T(8,128)(2,1)}, u32[]{:S(2)}, u32[]{:S(2)}) collective-permute-start(bf16[128,768]{1,0:T(8,128)(2,1)S(1)} %slice_select_fusion.3), channel_id=1, source_target_pairs={{0,1},{1,0},{2,3},{3,2},{4,5},{5,4},{6,7},{7,6},{8,9},{9,8},{10,11... | collective-permute-start | bytes 589832 | tf_op jit(solution)/shard_map/ppermute | solution.py:1151
  11.6 4.3 copy-start.21
  11.6 4.3 copy-start.22
  15.7 10.2 %collective-permute-start.1 = (bf16[3,768,384]{2,1,0:T(8,128)(2,1)S(1)}, bf16[3,768,384]{2,1,0:T(8,128)(2,1)}, u32[]{:S(2)}, u32[]{:S(2)}) collective-permute-start(bf16[3,768,384]{2,1,0:T(8,128)(2,1)S(1)} %copy.99), channel_id=1, source_target_pairs={{0,1},{1,0},{2,3},{3,2},{4,5},{5,4},{6,7},{7,6},{8,9},{9,8},{10,11... | collective-permute-start | bytes 5308424 | tf_op jit(solution)/shard_map/ppermute | solution.py:1151
  16.6 5.4 copy-start.13
  29.5 32.5 %copy-start.4 = (bf16[768,1536]{1,0:T(8,128)(2,1)S(1)}, bf16[768,1536]{1,0:T(8,128)(2,1)}, u32[]{:S(2)}) copy-start(bf16[768,1536]{1,0:T(8,128)(2,1)} %up_own.1) | copy-start | bytes 7077892
  61.5 14.9 %collective-permute-start.2 = (bf16[6,2,4,512,128]{4,3,2,1,0:T(8,128)(2,1)}, bf16[6,2,4,512,128]{4,3,2,1,0:T(8,128)(2,1)}, u32[]{:S(2)}, u32[]{:S(2)}) collective-permute-start(bf16[6,2,4,512,128]{4,3,2,1,0:T(8,128)(2,1)} %get-tuple-element.104.own_ref), channel_id=1, source_target_pairs={{0,1},{1,0},{2,3},{3,2},{4,5},{5,4},{6,7},{7,6},{8,9},{9,8},{10,11... | collective-permute-start | bytes 18874376 | tf_op jit(solution)/shard_map/ppermute | solution.py:1151
  62.0 80.2 %collective-permute-start.7 = (bf16[768,1536]{1,0:T(8,128)(2,1)S(1)}, bf16[768,1536]{1,0:T(8,128)(2,1)}, u32[]{:S(2)}, u32[]{:S(2)}) collective-permute-start(bf16[768,1536]{1,0:T(8,128)(2,1)S(1)} %copy-done.4), channel_id=1, source_target_pairs={{0,1},{1,0},{2,3},{3,2},{4,5},{5,4},{6,7},{7,6},{8,9},{9,8},{10,11... | collective-permute-start | bytes 7077896 | tf_op jit(solution)/shard_map/ppermute | solution.py:1151
  62.1 80.1 %collective-permute-start.8 = (bf16[1536,768]{1,0:T(8,128)(2,1)}, bf16[1536,768]{1,0:T(8,128)(2,1)}, u32[]{:S(2)}, u32[]{:S(2)}) collective-permute-start(bf16[1536,768]{1,0:T(8,128)(2,1)} %down_own.1), channel_id=1, source_target_pairs={{0,1},{1,0},{2,3},{3,2},{4,5},{5,4},{6,7},{7,6},{8,9},{9,8},{10,11... | collective-permute-start | bytes 7077896 | tf_op jit(solution)/shard_map/ppermute | solution.py:1151
  62.5 13.4 %collective-permute-start.3 = (bf16[384,768]{1,0:T(8,128)(2,1)}, bf16[384,768]{1,0:T(8,128)(2,1)S(1)}, u32[]{:S(2)}, u32[]{:S(2)}) collective-permute-start(bf16[384,768]{1,0:T(8,128)(2,1)} %param.46), channel_id=1, source_target_pairs={{0,1},{1,0},{2,3},{3,2},{4,5},{5,4},{6,7},{7,6},{8,9},{9,8},{10,11... | collective-permute-start | bytes 1769480 | tf_op jit(solution)/shard_map/ppermute | solution.py:1151
  76.0 46.5 %copy-start.2 = (bf16[768,768]{1,0:T(8,128)(2,1)}, bf16[768,768]{1,0:T(8,128)(2,1)S(1)}, u32[]{:S(2)}) copy-start(bf16[768,768]{1,0:T(8,128)(2,1)S(1)} %constant_dynamic-update-slice_fusion.weight_ref) | copy-start | bytes 3538948
  122.5 18.4 %copy-start.12 = (bf16[1536,9]{0,1:T(8,128)(2,1)S(1)}, bf16[1536,9]{0,1:T(8,128)(2,1)}, u32[]{:S(2)}) copy-start(bf16[1536,9]{0,1:T(8,128)(2,1)} %param.48) | copy-start | bytes 82948
  139.1 3.1 collective-permute-start.5
  140.6 1.6 collective-permute-start.6
  140.8 1.4 copy-start.9
  140.9 1.4 collective-permute-start.4
  142.2 0.6 copy-start.11
  142.2 0.7 copy-start.6
  142.9 0.7 copy-start.7
  318.2 3.7 copy-start.3
  321.6 38.8 %collective-permute-start.9 = (bf16[2,768,768]{2,1,0:T(8,128)(2,1)}, bf16[2,768,768]{2,1,0:T(8,128)(2,1)}, u32[]{:S(2)}, u32[]{:S(2)}) collective-permute-start(bf16[2,768,768]{2,1,0:T(8,128)(2,1)} %slice.130), channel_id=1, source_target_pairs={{0,1},{1,0},{2,3},{3,2},{4,5},{5,4},{6,7},{7,6},{8,9},{9,8},{10,11... | collective-permute-start | bytes 7077896 | tf_op jit(solution)/shard_map/ppermute | solution.py:1151
  323.5 40.1 %collective-permute-start.10 = (bf16[1536,768]{1,0:T(8,128)(2,1)}, bf16[1536,768]{1,0:T(8,128)(2,1)}, u32[]{:S(2)}, u32[]{:S(2)}) collective-permute-start(bf16[1536,768]{1,0:T(8,128)(2,1)} %slice.132), channel_id=1, source_target_pairs={{0,1},{1,0},{2,3},{3,2},{4,5},{5,4},{6,7},{7,6},{8,9},{9,8},{10,11... | collective-permute-start | bytes 7077896 | tf_op jit(solution)/shard_map/ppermute | solution.py:1151
  323.7 32.7 %copy-start.10 = (f32[12,16,256]{2,1,0:T(8,128)S(1)}, f32[12,16,256]{2,1,0:T(8,128)}, u32[]{:S(2)}) copy-start(f32[12,16,256]{2,1,0:T(8,128)} %get-tuple-element.116) | copy-start | bytes 589828
  356.0 3.0 collective-permute-start.11
  356.4 1.8 collective-permute-start.12
  359.0 4.7 slice-start
  360.3 3.3 slice-start.1
  369.0 92.2 %copy-start.15 = (f32[96,9]{0,1:T(8,128)S(1)}, f32[96,9]{0,1:T(8,128)}, u32[]{:S(2)}) copy-start(f32[96,9]{0,1:T(8,128)} %param.68) | copy-start | bytes 10372
  369.0 92.9 %copy-start.16 = (f32[96,9]{0,1:T(8,128)S(1)}, f32[96,9]{0,1:T(8,128)}, u32[]{:S(2)}) copy-start(f32[96,9]{0,1:T(8,128)} %param.69) | copy-start | bytes 10372
  369.0 93.6 %copy-start.17 = (f32[96,9]{0,1:T(8,128)S(1)}, f32[96,9]{0,1:T(8,128)}, u32[]{:S(2)}) copy-start(f32[96,9]{0,1:T(8,128)} %param.70) | copy-start | bytes 10372
  369.1 94.3 %copy-start.18 = (f32[24,9]{0,1:T(8,128)S(1)}, f32[24,9]{0,1:T(8,128)}, u32[]{:S(2)}) copy-start(f32[24,9]{0,1:T(8,128)} %param.56) | copy-start | bytes 2596
  369.1 95.0 %copy-start.19 = (f32[24,9]{0,1:T(8,128)S(1)}, f32[24,9]{0,1:T(8,128)}, u32[]{:S(2)}) copy-start(f32[24,9]{0,1:T(8,128)} %param.57) | copy-start | bytes 2596
  369.1 95.6 %copy-start.20 = (f32[24,9]{0,1:T(8,128)S(1)}, f32[24,9]{0,1:T(8,128)}, u32[]{:S(2)}) copy-start(f32[24,9]{0,1:T(8,128)} %param.58) | copy-start | bytes 2596
  369.1 96.4 %copy-start.14 = (f32[2,8,768]{2,1,0:T(8,128)S(1)}, f32[2,8,768]{2,1,0:T(8,128)}, u32[]{:S(2)}) copy-start(f32[2,8,768]{2,1,0:T(8,128)} %get-tuple-element.132) | copy-start | bytes 147460
  459.4 10.5 %collective-permute-start.13 = (bf16[6,2,4,512,128]{4,3,2,1,0:T(8,128)(2,1)}, bf16[6,2,4,512,128]{4,3,2,1,0:T(8,128)(2,1)}, u32[]{:S(2)}, u32[]{:S(2)}) collective-permute-start(bf16[6,2,4,512,128]{4,3,2,1,0:T(8,128)(2,1)} %get-tuple-element.122), channel_id=1, source_target_pairs={{0,1},{1,0},{2,3},{3,2},{4,5},{5,4},{6,7},{7,6},{8,9},{9,8},{10,11... | collective-permute-start | bytes 18874376 | tf_op jit(solution)/shard_map/ppermute | solution.py:1151
  499.9 5.1 collective-permute-start.14
  505.1 0.7 copy-start.8
  593.6 4.4 copy-start.5
  622.8 19.4 %copy-start.1 = (bf16[768,1000]{0,1:T(8,128)(2,1)S(1)}, bf16[768,1000]{0,1:T(8,128)(2,1)}, u32[]{:S(2)}) copy-start(bf16[768,1000]{0,1:T(8,128)(2,1)} %param.43) | copy-start | bytes 4608004
Sparse Core Ops, SparseCore 0:
  369.1 144.1 reduce-scatter.1

commit v2 on v1

v2 whole, which is shorter than its diff:
```python
import functools

import jax
import jax.numpy as jnp
from jax import lax
from jax.experimental import pallas as pl
from jax.experimental.pallas import tpu as pltpu
from jax.sharding import PartitionSpec as P

D = 768
HS = 64
FF = 3072
SIDE = 32
STEP = 10
PARAMS = 11419392

NORM_EPS = 1e-06
BETA_ONE = 0.5
BETA_TWO = 0.5
ADAM_EPS = 1e-08
WEIGHT_DECAY = 0.01

F32 = jnp.float32
BF16 = jnp.bfloat16

BODY = 512
HALF = 256
EDGE = 32
PLANE = 592
CHUNK = 256
VMEM_BYTES = 60 * 1024 * 1024


def params(*semantics):
    return pltpu.CompilerParams(
        dimension_semantics=semantics or None, vmem_limit_bytes=VMEM_BYTES
    )


def nn(left, right):
    return lax.dot_general(left, right, (((1,), (0,)), ((), ())), preferred_element_type=F32)


def nt(left, right):
    return lax.dot_general(left, right, (((1,), (1,)), ((), ())), preferred_element_type=F32)


def tn(left, right):
    return lax.dot_general(left, right, (((0,), (0,)), ((), ())), preferred_element_type=F32)


def whole(shape):
    return pl.BlockSpec(shape, lambda *_: (0,) * len(shape), pipeline_mode=pl.Buffered(1))


def scalars():
    return pl.BlockSpec(memory_space=pltpu.SMEM)


def geometry(scal_ref):
    return scal_ref[0], scal_ref[1], scal_ref[2] == 1, scal_ref[3]


def body_offset(half, gap):
    return pl.multiple_of(EDGE + half * (HALF + gap), 16)


def edge_offset(place):
    return pl.multiple_of(jnp.where(place == 0, EDGE + BODY, 0), 16)


def normalize(fields):
    center = fields - jnp.mean(fields, -1, keepdims=True)
    inverse = lax.rsqrt(jnp.mean(center * center, -1, keepdims=True) + NORM_EPS)
    return center * inverse, inverse


def norm_back(grad_hat, normed, inverse):
    return inverse * (
        grad_hat
        - jnp.mean(grad_hat, -1, keepdims=True)
        - normed * jnp.mean(grad_hat * normed, -1, keepdims=True)
    )


def variants(base, shifted, offset, width, rows, lanes):
    up = pl.multiple_of(offset - width, 16)
    down = pl.multiple_of(offset + width, 16)
    found = {}
    for part, shift, where in ((0, 0, offset), (0, 1, down), (1, 0, offset), (1, -1, up)):
        for column in (0, 1):
            at = (2 * part + column, pl.ds(where, rows), lanes)
            found[part, shift, column, 0] = base[at].astype(F32)
            found[part, shift, column, 1] = shifted[at].astype(F32)
    return found


def tap(found, p, q, a, b):
    part, shift = ((1, -1), (0, 0), (1, 0))[a + 1] if p == 0 else ((0, 0), (1, 0), (0, 1))[a + 1]
    column, moved = ((1, 1), (0, 0), (1, 0))[b + 1] if q == 0 else ((0, 0), (1, 0), (0, 1))[b + 1]
    return found[part, shift, column, moved]


def conv_at(found, kernel, p, q, flip=False):
    total = None
    for a in (-1, 0, 1):
        for b in (-1, 0, 1):
            index = 3 * (a + 1) + (b + 1)
            term = tap(found, p, q, a, b) * kernel[8 - index if flip else index]
            total = term if total is None else total + term
    return total


def kernel_rows(kernel_ref, lanes, rows):
    return [
        jnp.broadcast_to(kernel_ref[index : index + 1, lanes].astype(F32), (rows, lanes.size)) for index in range(9)
    ]


def clear_borders(plane, wide_gap=True):
    zeros = jnp.zeros((4, EDGE, plane.shape[2]), plane.dtype)
    plane[:, 0:EDGE, :] = zeros
    plane[:, EDGE + HALF : EDGE + HALF + EDGE, :] = zeros
    plane[:, EDGE + BODY : EDGE + BODY + EDGE, :] = zeros
    plane[:, PLANE - EDGE : PLANE, :] = zeros


def column_masks(rows, width):
    column = lax.broadcasted_iota(jnp.int32, (rows, 128), 0) & (width - 1)
    return column != width - 1, column != 0


def moved_rows(value, column, masks):
    rows, lanes = value.shape
    moved = pltpu.roll(value, rows - 1 if column == 0 else 1, 0)
    parts = [jnp.where(masks[column], moved[:, at : at + 128], 0.0) for at in range(0, lanes, 128)]
    return parts[0] if len(parts) == 1 else jnp.concatenate(parts, axis=1)


def own_half(half):
    return lambda i: jnp.minimum(i, half - 1)


def other_half(half):
    return lambda i: jnp.maximum(i - half, 0)


def front_kernel(
    scal_ref, x_ref, edge_ref, perm_ref, edge_perm_ref, mod_ref, taps_ref, order_ref, weight_ref,
    x_out, mixed_out, base_out, shifted_out, q_out, kv_out,
):
    width, gap, long_latent, place = geometry(scal_ref)
    @pl.when(pl.program_id(0) == 0)
    def _():
        clear_borders(base_out)
        clear_borders(shifted_out)
        masks = column_masks(64, width)
        edge_masks = column_masks(EDGE, width)

        @pl.loop(0, 8, unroll=2)
        def _(block):
            half = block // 4
            rows = x_ref[pl.ds(pl.multiple_of(block * 256, 256), 256), :]
            shift = mod_ref[half, 0:1, :]
            scale = mod_ref[half, 1:2, :]
            place_in = pl.ds(pl.multiple_of(block * 64, 64), 64)
            place_out = pl.ds(pl.multiple_of(body_offset(half, gap) + (block % 4) * 64, 16), 64)
            for group in range(4):
                picked = nn(perm_ref[64 * group : 64 * group + 64, :], rows)
                x_out[group, place_in, :] = picked.astype(BF16)
                normed = normalize(picked)[0]
                value = normed * (1.0 + scale) + shift
                base_out[group, place_out, :] = value.astype(BF16)
                shifted_out[group, place_out, :] = moved_rows(value, group % 2, masks).astype(BF16)

        @pl.when(long_latent)
        def _():
            at = pl.ds(edge_offset(place), EDGE)
            for group in range(4):
                picked = nn(edge_perm_ref[32 * group : 32 * group + 32, :], edge_ref[...])
                normed = normalize(picked)[0]
                value = normed * (1.0 + mod_ref[0, 1:2, :]) + mod_ref[0, 0:1, :]
                base_out[group, at, :] = value.astype(BF16)
                shifted_out[group, at, :] = moved_rows(value, group % 2, edge_masks).astype(BF16)

        for lane in range(D // 128):
            lanes = pl.ds(lane * 128, 128)
            kernel = kernel_rows(taps_ref, lanes, 16)

            @pl.loop(0, 32, unroll=4)
            def _(tile, lanes=lanes, kernel=kernel):
                offset = body_offset(tile // 16, gap) + (tile % 16) * 16
                found = variants(base_out, shifted_out, pl.multiple_of(offset, 16), width, 16, lanes)
                for p in (0, 1):
                    for q in (0, 1):
                        at = (2 * p + q, pl.ds(pl.multiple_of(tile * 16, 16), 16), lanes)
                        mixed_out[at] = conv_at(found, kernel, p, q).astype(BF16)

    project_kernel(mixed_out, order_ref, weight_ref, q_out, kv_out)


def project_kernel(mixed_ref, order_ref, weight_ref, q_out, kv_out):
    weight = nn(weight_ref[...], order_ref[...]).astype(BF16)
    for group in range(4):
        triple = nn(mixed_ref[group], weight)
        q_out[0, group] = (triple[:, 0:128] * (HS**-0.5)).astype(BF16)
        kv_out[0, 0, group] = triple[:, 128:256].astype(BF16)
        kv_out[0, 1, group] = triple[:, 256:384].astype(BF16)


def project_specs(pairs):
    shapes = (
        jax.ShapeDtypeStruct((pairs, 4, BODY, 128), BF16),
        jax.ShapeDtypeStruct((pairs, 2, 4, BODY, 128), BF16),
    )
    blocks = (
        pl.BlockSpec((1, 4, BODY, 128), lambda i: (i, 0, 0, 0)),
        pl.BlockSpec((1, 2, 4, BODY, 128), lambda i: (i, 0, 0, 0, 0)),
    )
    return shapes, blocks, pl.BlockSpec((D, 384), lambda i: (0, i))


def front(scal, x, edge, perm, edge_perm, mod, taps, order, weight):
    pairs = weight.shape[1] // 384
    shapes, blocks, weight_block = project_specs(pairs)
    plane = jax.ShapeDtypeStruct((4, PLANE, D), BF16)
    body = jax.ShapeDtypeStruct((4, BODY, D), BF16)
    return pl.pallas_call(
        front_kernel,
        grid=(pairs,),
        out_shape=(body, body, plane, plane, *shapes),
        in_specs=[
            scalars(), whole(x.shape), whole(edge.shape), whole(perm.shape), whole(edge_perm.shape),
            whole(mod.shape), whole(taps.shape), whole(order.shape), weight_block,
        ],
        out_specs=(whole(body.shape), whole(body.shape), whole(plane.shape), whole(plane.shape), *blocks),
        compiler_params=params("arbitrary"),
        name="front",
    )(scal, x, edge, perm, edge_perm, mod, taps, order, weight)


def project(mixed, order, weight):
    pairs = weight.shape[1] // 384
    shapes, blocks, weight_block = project_specs(pairs)
    return pl.pallas_call(
        project_kernel,
        grid=(pairs,),
        out_shape=shapes,
        in_specs=[whole(mixed.shape), whole(order.shape), weight_block],
        out_specs=blocks,
        compiler_params=params("arbitrary"),
        name="project",
    )(mixed, order, weight)


def head_mask(rows, head):
    lane = lax.broadcasted_iota(jnp.int32, (rows, 128), 1)
    return (lane < HS) if head == 0 else (lane >= HS)


def pieces(first, second, rows):
    lane = lax.broadcasted_iota(jnp.int32, (rows, 128), 1)
    value = jnp.where(lane < HS, first, second)
    one = value.astype(BF16).astype(F32)
    two = (value - one).astype(BF16).astype(F32)
    three = value - one - two
    turn = lane % HS
    picked = jnp.where(turn == 0, one, jnp.where(turn == 1, two, jnp.where(turn == 2, three, 0.0)))
    return picked.astype(BF16)


def unit_pieces(rows):
    lane = lax.broadcasted_iota(jnp.int32, (rows, 128), 1)
    return jnp.where(lane % HS < 3, 1.0, 0.0).astype(BF16)


def attend_kernel(scal_ref, q_ref, own_ref, other_ref, out_ref, log_ref):
    long_latent = scal_ref[2] == 1

    def attend(query, keys, values, rows):
        mixes, logs = [], []
        for head in (0, 1):
            masked = jnp.where(head_mask(rows, head), query, jnp.zeros_like(query))
            scores = [nt(masked, key) for key in keys]
            highest = jnp.max(scores[0], -1, keepdims=True)
            for other in scores[1:]:
                highest = jnp.maximum(highest, jnp.max(other, -1, keepdims=True))
            mix = None
            for score, value in zip(scores, values):
                share = jnp.exp(score - highest).astype(BF16)
                part = nn(share, value)
                mix = part if mix is None else mix + part
            total = mix[:, 128:256]
            mixes.append(mix[:, 0:128] / total)
            logs.append(highest + jnp.log(total))
        mix = jnp.where(head_mask(rows, 0), mixes[0], mixes[1])
        return mix.astype(BF16), pieces(-logs[0], -logs[1], rows)

    def with_ones(value):
        return jnp.concatenate([value, jnp.ones_like(value)], axis=1)

    @pl.when(long_latent)
    def _():
        for tile in range(2):
            at = pl.ds(tile * 256, 256)
            out_ref[0, at, :], log_ref[0, 0, at, :] = attend(
                q_ref[0, 0, at, :],
                [own_ref[0, 0, 0], other_ref[0, 0, 0]],
                [with_ones(own_ref[0, 1, 0]), with_ones(other_ref[0, 1, 0])],
                256,
            )

    @pl.when(jnp.logical_not(long_latent))
    def _():
        for tile in range(2):
            at = pl.ds(tile * 256, 256)
            out_ref[0, at, :], log_ref[0, 0, at, :] = attend(
                q_ref[0, 0, at, :],
                [own_ref[0, 0, 0, at, :]],
                [with_ones(own_ref[0, 1, 0, at, :])],
                256,
            )


def attention(scal, q, own, other):
    pairs = q.shape[0]
    pair_spec = pl.BlockSpec((1, 1, BODY, 128), lambda p, g: (p, g, 0, 0))
    kv_spec = pl.BlockSpec((1, 2, 1, BODY, 128), lambda p, g: (p, 0, g, 0, 0))
    return pl.pallas_call(
        attend_kernel,
        grid=(pairs, 4),
        out_shape=(
            jax.ShapeDtypeStruct((4, BODY, 128 * pairs), BF16),
            jax.ShapeDtypeStruct((pairs, 4, BODY, 128), BF16),
        ),
        in_specs=[scalars(), pair_spec, kv_spec, kv_spec],
        out_specs=(pl.BlockSpec((1, BODY, 128), lambda p, g: (g, 0, p)), pair_spec),
        compiler_params=params("arbitrary", "arbitrary"),
        name="attention",
    )(scal, q, own, other)


def attend_back_kernel(
    scal_ref, q_ref, own_ref, other_ref, mix_ref, grad_ref, log_ref, gq_ref, gown_ref, gother_ref
):
    long_latent = scal_ref[2] == 1

    def side(query, mix, grad, log):
        rows = query.shape[0]
        product = mix.astype(F32) * grad.astype(F32)
        deltas = [
            jnp.sum(jnp.where(head_mask(rows, head), product, 0.0), -1, keepdims=True) for head in (0, 1)
        ]
        delta = pieces(-deltas[0], -deltas[1], rows)
        result = []
        for head in (0, 1):
            mask = head_mask(rows, head)
            zero = jnp.zeros_like(query)
            q_head = jnp.where(mask, query, zero)
            g_head = jnp.where(mask, grad, zero)
            q_more = jnp.concatenate([q_head, jnp.where(mask, log, zero)], axis=1)
            g_more = jnp.concatenate([g_head, jnp.where(mask, delta, zero)], axis=1)
            result.append((q_head, g_head, q_more, g_more))
        return result

    def keys_part(heads, key, value):
        rows = key.shape[0]
        ones = unit_pieces(rows)
        key_more = jnp.concatenate([key, ones], axis=1)
        value_more = jnp.concatenate([value, ones], axis=1)
        key_turned = key.astype(F32).T.astype(BF16)
        gk = gv = None
        turned = []
        for q_head, g_head, q_more, g_more in heads:
            share = jnp.exp(nt(key_more, q_more))
            slope = (share * nt(value_more, g_more)).astype(BF16)
            share = share.astype(BF16)
            gv_part = nn(share, g_head)
            gk_part = nn(slope, q_head)
            gv = gv_part if gv is None else gv + gv_part
            gk = gk_part if gk is None else gk + gk_part
            turned.append(nn(key_turned, slope))
        return gk, gv, turned

    def query_grad(turned):
        row = lax.broadcasted_iota(jnp.int32, turned[0].shape, 0)
        both = jnp.where(row < HS, turned[0], turned[1]) * (HS**-0.5)
        return both.T.astype(BF16)

    @pl.when(long_latent)
    def _():
        heads = side(q_ref[0, 0], mix_ref[0], grad_ref[0], log_ref[0, 0])
        totals = None
        for source, target in ((own_ref, gown_ref), (other_ref, gother_ref)):
            for tile in range(2):
                at = pl.ds(tile * 256, 256)
                gk, gv, turned = keys_part(heads, source[0, 0, 0, at, :], source[0, 1, 0, at, :])
                target[0, 0, 0, at, :] = gk.astype(BF16)
                target[0, 1, 0, at, :] = gv.astype(BF16)
                totals = turned if totals is None else [a + b for a, b in zip(totals, turned)]
        gq_ref[0, 0] = query_grad(totals)

    @pl.when(jnp.logical_not(long_latent))
    def _():
        for tile in range(2):
            at = pl.ds(tile * 256, 256)
            heads = side(q_ref[0, 0, at, :], mix_ref[0, at, :], grad_ref[0, at, :], log_ref[0, 0, at, :])
            gk, gv, turned = keys_part(heads, own_ref[0, 0, 0, at, :], own_ref[0, 1, 0, at, :])
            gown_ref[0, 0, 0, at, :] = gk.astype(BF16)
            gown_ref[0, 1, 0, at, :] = gv.astype(BF16)
            gq_ref[0, 0, at, :] = query_grad(turned)
        gother_ref[...] = jnp.zeros_like(gother_ref)


def attention_back(scal, q, own, other, mix, grad, log):
    pairs = q.shape[0]
    pair_spec = pl.BlockSpec((1, 1, BODY, 128), lambda p, g: (p, g, 0, 0))
    kv_spec = pl.BlockSpec((1, 2, 1, BODY, 128), lambda p, g: (p, 0, g, 0, 0))
    lane_spec = pl.BlockSpec((1, BODY, 128), lambda p, g: (g, 0, p))
    return pl.pallas_call(
        attend_back_kernel,
        grid=(pairs, 4),
        out_shape=(
            jax.ShapeDtypeStruct(q.shape, BF16),
            jax.ShapeDtypeStruct(own.shape, BF16),
            jax.ShapeDtypeStruct(own.shape, BF16),
        ),
        in_specs=[scalars(), pair_spec, kv_spec, kv_spec, lane_spec, lane_spec, pair_spec],
        out_specs=(pair_spec, kv_spec, kv_spec),
        compiler_params=params("arbitrary", "arbitrary"),
        name="attention_back",
    )(scal, q, own, other, mix, grad, log)


def middle_kernel(
    x_ref, mix_own, mix_other, cot_ref, perm_ref, mod_ref, own_ref, other_ref, attn_out, norm_out, cot_out, grad_out
):
    gate_one = mod_ref[0, 2:3, :]
    shift = mod_ref[0, 3:4, :]
    scale = mod_ref[0, 4:5, :]
    gate_two = mod_ref[0, 5:6, :]
    for group in range(4):
        attn = nn(mix_own[group], own_ref[...]) + nn(mix_other[group], other_ref[...])
        attn_low = attn.astype(BF16)
        attn_out[group] = attn_low
        residual = x_ref[group].astype(F32) + gate_one * attn_low.astype(F32)
        norm_out[group] = (normalize(residual)[0] * (1.0 + scale) + shift).astype(BF16)
        cot = nn(perm_ref[64 * group : 64 * group + 64, :], cot_ref[...])
        cot_out[group] = cot.astype(BF16)
        grad_out[group] = (cot * gate_two).astype(BF16)


def middle(x, mix, mix_other, cot, perm, mod, weight, weight_other):
    part = pl.BlockSpec((4, 64, D // 2), lambda i: (0, i, 0))
    block = pl.BlockSpec((4, 64, D), lambda i: (0, i, 0))
    body = jax.ShapeDtypeStruct((4, BODY, D), BF16)
    return pl.pallas_call(
        middle_kernel,
        grid=(8,),
        out_shape=(body,) * 4,
        in_specs=[
            block, part, part, pl.BlockSpec((256, D), lambda i: (i, 0)), whole(perm.shape),
            pl.BlockSpec((1, 8, D), lambda i: (i // 4, 0, 0)), whole(weight.shape), whole(weight.shape),
        ],
        out_specs=(block,) * 4,
        compiler_params=params("arbitrary"),
        name="middle",
    )(x, mix, mix_other, cot, perm, mod, weight, weight_other)


def gelu_both(value):
    root = 0.7978845608028654
    square = value * value
    angle = value * (root + (root * 0.044715) * square)
    bent = jnp.tanh(angle)
    half = 0.5 + 0.5 * bent
    inner = (0.5 * root) + (1.5 * root * 0.044715) * square
    return value * half, half + value * (1.0 - bent * bent) * inner


def ffn_kernel(
    scal_ref, taps_own, taps_other, norm_ref, norm_edge, grad_ref, grad_edge,
    up_own, up_other, down_own, down_other,
    ffn_out, back_out, up_grad_own, up_grad_other, down_grad_own, down_grad_other, taps_grad,
    hid, hid_moved, gc, gc_moved, act, gh, da, da_edge, ffn_sum, back_sum, up, down, taps, norm_turned, grad_turned, tap_sums,
):
    width, gap, long_latent, place = geometry(scal_ref)
    step = pl.program_id(0)
    steps = pl.num_programs(0)

    @pl.when(step < steps // 2)
    def _():
        up[...] = up_own[...]
        down[...] = down_own[...]
        taps[...] = taps_own[...].astype(F32)

    @pl.when(step >= steps // 2)
    def _():
        up[...] = up_other[...]
        down[...] = down_other[...]
        taps[...] = taps_other[...].astype(F32)

    @pl.when(step == 0)
    def _():
        for plane in (hid, hid_moved, gc, gc_moved):
            clear_borders(plane)

        @pl.loop(0, 8)
        def _(tile):
            rows = pl.ds(pl.multiple_of((tile % 2) * HALF, HALF), HALF)
            cols = pl.ds(pl.multiple_of(tile * HALF, HALF), HALF)
            norm_turned[:, cols] = norm_ref[tile // 2, rows, :].T
            grad_turned[:, cols] = grad_ref[tile // 2, rows, :].T
            ffn_sum[tile // 2, rows, :] = jnp.zeros((HALF, D), F32)
            back_sum[tile // 2, rows, :] = jnp.zeros((HALF, D), F32)

    masks = column_masks(BODY, width)
    edge_masks = column_masks(EDGE, width)

    for group in range(4):
        value = nn(norm_ref[group], up[...])
        moved = moved_rows(value, group % 2, masks)
        for half in (0, 1):
            at = (group, pl.ds(body_offset(half, gap), HALF), slice(None))
            hid[at] = value[half * HALF : (half + 1) * HALF]
            hid_moved[at] = moved[half * HALF : (half + 1) * HALF]
        da[group] = nt(grad_ref[group], down[...]).astype(BF16)

    @pl.when(long_latent)
    def _():
        for group in range(4):
            at = (group, pl.ds(edge_offset(place), EDGE), slice(None))
            value = nn(norm_edge[group], up[...])
            hid[at] = value
            hid_moved[at] = moved_rows(value, group % 2, edge_masks)
            da_edge[group] = nt(grad_edge[group], down[...]).astype(BF16)

    def plane_rows(block, row):
        return pl.multiple_of(body_offset(block // 4, gap) + (block % 4) * 64 + row, 16)

    def accumulate(total, left, right, block):
        rows = slice(64 * block, 64 * block + 64)
        part = nn(left[:, rows, :].reshape(256, CHUNK), right)
        total[:, rows, :] += part.reshape(4, 64, D)

    down_now = down[...]
    up_turned = up[...].T

    for block in range(8):
        for lane in range(CHUNK // 128):
            lanes = pl.ds(lane * 128, 128)
            kernel = kernel_rows(taps, lanes, 16)
            for tile in (0, 32):
                grads = [[] for _ in range(4)]
                for part in (0, 16):
                    offset = plane_rows(block, tile + part)
                    rows = pl.ds(block * 64 + tile + part, 16)
                    found = variants(hid, hid_moved, offset, width, 16, lanes)
                    for p in (0, 1):
                        for q in (0, 1):
                            group = 2 * p + q
                            value, slope = gelu_both(conv_at(found, kernel, p, q))
                            act[group, rows, lanes] = value.astype(BF16)
                            grads[group].append(slope * da[group, rows, lanes].astype(F32))
                at = pl.ds(plane_rows(block, tile), 32)
                for group in range(4):
                    grad = jnp.concatenate(grads[group], axis=0)
                    gc[group, at, lanes] = grad
                    gc_moved[group, at, lanes] = moved_rows(grad, group % 2, edge_masks)
        if block > 0:
            accumulate(ffn_sum, act, down_now, block - 1)
    accumulate(ffn_sum, act, down_now, 7)

    for side in (0, 1):

        @pl.when(jnp.logical_and(long_latent, place == side))
        def _(side=side):
            for lane in range(CHUNK // 128):
                lanes = pl.ds(lane * 128, 128)
                kernel = kernel_rows(taps, lanes, 32)
                offset = EDGE + BODY if side == 0 else 0
                found = {}
                for part, shift, where in ((0, 0, offset), (0, 1, offset + EDGE), (1, 0, offset), (1, -1, offset - EDGE)):
                    if where < 0 or where + 32 > PLANE:
                        continue
                    for column in (0, 1):
                        at = (2 * part + column, slice(where, where + 32), lanes)
                        found[part, shift, column, 0] = hid[at]
                        found[part, shift, column, 1] = hid_moved[at]
                for q in (0, 1):
                    group = 2 * side + q
                    slope = gelu_both(conv_at(found, kernel, side, q))[1]
                    grad = slope * da_edge[group, :, lanes].astype(F32)
                    gc[group, offset : offset + 32, lanes] = grad
                    gc_moved[group, offset : offset + 32, lanes] = moved_rows(grad, q, edge_masks)

    tap_sums[...] = jnp.zeros_like(tap_sums)
    for block in range(8):
        for lane in range(CHUNK // 128):
            lanes = pl.ds(lane * 128, 128)
            kernel = kernel_rows(taps, lanes, 16)
            totals = None
            for tile in range(0, 64, 16):
                offset = plane_rows(block, tile)
                rows = pl.ds(block * 64 + tile, 16)
                found = variants(gc, gc_moved, offset, width, 16, lanes)
                for p in (0, 1):
                    for q in (0, 1):
                        gh[2 * p + q, rows, lanes] = conv_at(found, kernel, p, q, flip=True).astype(BF16)
                parts = taps_at(found, variants(hid, hid_moved, offset, width, 16, lanes))
                totals = parts if totals is None else [total + more for total, more in zip(totals, parts)]
            for index, total in enumerate(totals):
                tap_sums[lane, index] += total
        if block > 0:
            accumulate(back_sum, gh, up_turned, block - 1)
    accumulate(back_sum, gh, up_turned, 7)
    for lane in range(CHUNK // 128):
        for index in range(9):
            taps_grad[0, index : index + 1, lane * 128 : (lane + 1) * 128] = jnp.sum(tap_sums[lane, index], 0, keepdims=True)

    def weight_grads(up_grad, down_grad):
        down_grad[...] = nn(grad_turned[...], act[...].reshape(4 * BODY, CHUNK)).T.astype(BF16)
        up_grad[0] = nn(norm_turned[...], gh[...].reshape(4 * BODY, CHUNK)).astype(BF16)

    @pl.when(step < steps // 2)
    def _():
        weight_grads(up_grad_own, down_grad_own)

    @pl.when(step >= steps // 2)
    def _():
        weight_grads(up_grad_other, down_grad_other)

    @pl.when(step == steps - 1)
    def _():
        ffn_out[...] = ffn_sum[...].astype(BF16)
        back_out[...] = back_sum[...].astype(BF16)


def taps_at(grads, fields):
    sums = []
    for a in (-1, 0, 1):
        for b in (-1, 0, 1):
            total = None
            for p in (0, 1):
                for q in (0, 1):
                    term = grads[p, 0, q, 0] * tap(fields, p, q, a, b)
                    total = term if total is None else total + term
            sums.append(sum(total[at : at + 8] for at in range(0, total.shape[0], 8)))
    return sums


def feed_forward(scal, taps_own, taps_other, norm, norm_edge, grad, grad_edge, up_own, up_other, down_own, down_other):
    half = up_own.shape[1] // CHUNK
    steps = 2 * half
    body = jax.ShapeDtypeStruct((4, BODY, D), BF16)

    own, other = own_half(half), other_half(half)
    per = D // CHUNK
    plane = pltpu.VMEM((4, PLANE, CHUNK), F32)
    small = pltpu.VMEM((4, BODY, CHUNK), BF16)
    return pl.pallas_call(
        ffn_kernel,
        grid=(steps,),
        out_shape=(
            body, body,
            *[jax.ShapeDtypeStruct((half // per, D, D), BF16)] * 2,
            *[jax.ShapeDtypeStruct((half * CHUNK, D), BF16)] * 2,
            jax.ShapeDtypeStruct((steps, 16, CHUNK), F32),
        ),
        in_specs=[
            scalars(),
            pl.BlockSpec((16, CHUNK), lambda i: (0, own(i))),
            pl.BlockSpec((16, CHUNK), lambda i: (0, other(i))),
            whole(norm.shape), whole(norm_edge.shape), whole(grad.shape), whole(grad_edge.shape),
            pl.BlockSpec((D, CHUNK), lambda i: (0, own(i))),
            pl.BlockSpec((D, CHUNK), lambda i: (0, other(i))),
            pl.BlockSpec((CHUNK, D), lambda i: (own(i), 0)),
            pl.BlockSpec((CHUNK, D), lambda i: (other(i), 0)),
        ],
        out_specs=(
            whole(body.shape), whole(body.shape),
            pl.BlockSpec((1, D, CHUNK), lambda i: (own(i) // per, 0, own(i) % per)),
            pl.BlockSpec((1, D, CHUNK), lambda i: (other(i) // per, 0, other(i) % per)),
            pl.BlockSpec((CHUNK, D), lambda i: (own(i), 0)),
            pl.BlockSpec((CHUNK, D), lambda i: (other(i), 0)),
            pl.BlockSpec((1, 16, CHUNK), lambda i: (i, 0, 0)),
        ),
        scratch_shapes=[
            plane, plane, plane, plane, small, small, small, pltpu.VMEM((4, EDGE, CHUNK), BF16),
            pltpu.VMEM((4, BODY, D), F32), pltpu.VMEM((4, BODY, D), F32),
            pltpu.VMEM((D, CHUNK), BF16), pltpu.VMEM((CHUNK, D), BF16), pltpu.VMEM((16, CHUNK), F32),
            pltpu.VMEM((D, 4 * BODY), BF16), pltpu.VMEM((D, 4 * BODY), BF16),
            pltpu.VMEM((CHUNK // 128, 9, 8, 128), F32),
        ],
        compiler_params=params("arbitrary"),
        name="feed_forward",
    )(scal, taps_own, taps_other, norm, norm_edge, grad, grad_edge, up_own, up_other, down_own, down_other)


def turn_kernel(
    x_ref, attn_ref, ffn_ref, cot_ref, back_ref, mix_own, mix_other, perm_ref, mod_ref, own_ref, other_ref,
    out_ref, grad_ref, gmix_own, gmix_other, sums_ref, wgrad_own, wgrad_other,
    wsum,
):
    step = pl.program_id(0)
    gate_one = mod_ref[0, 2:3, :]
    scale = mod_ref[0, 4:5, :]
    gate_two = mod_ref[0, 5:6, :]

    @pl.when(step % 4 == 0)
    def _():
        sums_ref[...] = jnp.zeros_like(sums_ref)

    @pl.when(step == 0)
    def _():
        wsum[...] = jnp.zeros_like(wsum)

    result = None
    gattns = []
    for group in range(4):
        attn = attn_ref[group].astype(F32)
        ffn = ffn_ref[group].astype(F32)
        cot = cot_ref[group].astype(F32)
        back = back_ref[group].astype(F32)
        residual = x_ref[group].astype(F32) + gate_one * attn
        low = (residual + gate_two * ffn).astype(BF16)
        part = nn(perm_ref[:, 64 * group : 64 * group + 64], low)
        result = part if result is None else result + part
        normed, inverse = normalize(residual)
        grad = cot + norm_back(back * (1.0 + scale), normed, inverse)
        grad_ref[group] = grad.astype(BF16)
        for row, value in ((0, grad * attn), (1, back), (2, back * normed), (3, cot * ffn)):
            sums_ref[0, row : row + 1, :] += jnp.sum(value, 0, keepdims=True)
        gattn = (grad * gate_one).astype(BF16)
        gattns.append(gattn)
    gattn = jnp.concatenate(gattns, axis=0)
    for index, (mix, weight, gmix) in enumerate(((mix_own, own_ref, gmix_own), (mix_other, other_ref, gmix_other))):
        gmix[...] = nt(gattn, weight[...]).astype(BF16).reshape(4, 64, D // 2)
        wsum[index] += tn(mix[...].reshape(256, D // 2), gattn)
    out_ref[...] = result.astype(BF16)

    @pl.when(step == 7)
    def _():
        wgrad_own[...] = wsum[0].astype(BF16)
        wgrad_other[...] = wsum[1].astype(BF16)


def turn(x, attn, ffn, cot, back, mix, mix_other, perm, mod, weight, weight_other):
    block = pl.BlockSpec((4, 64, D), lambda i: (0, i, 0))
    part = pl.BlockSpec((4, 64, D // 2), lambda i: (0, i, 0))
    body = jax.ShapeDtypeStruct((4, BODY, D), BF16)
    half_body = jax.ShapeDtypeStruct((4, BODY, D // 2), BF16)
    half_weight = jax.ShapeDtypeStruct((D // 2, D), BF16)
    return pl.pallas_call(
        turn_kernel,
        grid=(8,),
        out_shape=(
            jax.ShapeDtypeStruct((2048, D), BF16), body, half_body, half_body,
            jax.ShapeDtypeStruct((2, 8, D), F32), half_weight, half_weight,
        ),
        in_specs=[block] * 5 + [part] * 2 + [
            whole(perm.shape), pl.BlockSpec((1, 8, D), lambda i: (i // 4, 0, 0)), whole(weight.shape), whole(weight.shape),
        ],
        out_specs=(
            pl.BlockSpec((256, D), lambda i: (i, 0)), block, part, part,
            pl.BlockSpec((1, 8, D), lambda i: (i // 4, 0, 0)), whole(weight.shape), whole(weight.shape),
        ),
        scratch_shapes=[pltpu.VMEM((2, D // 2, D), F32)],
        compiler_params=params("arbitrary"),
        name="turn",
    )(x, attn, ffn, cot, back, mix, mix_other, perm, mod, weight, weight_other)


def project_back_kernel(
    gq_own, gkv_own, add_own, gq_other, gkv_other, add_other, mixed_ref, order_ref, own_ref, other_ref,
    gmixed_ref, wgrad_own, wgrad_other,
    gsum, turned, triples, weights,
):
    step = pl.program_id(0)
    half_steps = pl.num_programs(0) // 2

    @pl.when(step == 0)
    def _():
        for tile in range(8):
            rows = slice((tile % 2) * HALF, (tile % 2 + 1) * HALF)
            turned[:, tile * HALF : (tile + 1) * HALF] = mixed_ref[tile // 2, rows, :].T

    def gather(gq_ref, gkv_ref, add_ref, weight_ref, pair):
        at = 384 * pair
        weights[:, at : at + 384] = nn(weight_ref[...], order_ref[...]).astype(BF16)
        for group in range(4):
            triples[group, :, at : at + 128] = gq_ref[0, group]
            for part in (0, 1):
                total = gkv_ref[0, part, group].astype(F32) + add_ref[0, part, group].astype(F32)
                triples[group, :, at + 128 * (part + 1) : at + 128 * (part + 2)] = total.astype(BF16)

    def finish(wgrad_ref, last):
        width = weights.shape[1]
        for group in range(4):
            part = nt(triples[group], weights[...])
            if last:
                gmixed_ref[group] = (gsum[group] + part).astype(BF16)
            else:
                gsum[group] = part
        wgrad = nn(turned[...], triples[...].reshape(4 * BODY, width)).astype(BF16)
        for at in range(0, width, 384):
            wgrad_ref[:, at : at + 384] = nt(wgrad[:, at : at + 384], order_ref[...]).astype(BF16)

    for half, refs in enumerate(((gq_own, gkv_own, add_own, own_ref), (gq_other, gkv_other, add_other, other_ref))):
        for pair in range(weights.shape[1] // 384):

            @pl.when(step == half * half_steps + pair)
            def _(refs=refs, pair=pair):
                gather(*refs, pair)

    @pl.when(step == half_steps - 1)
    def _():
        finish(wgrad_own, False)

    @pl.when(step == 2 * half_steps - 1)
    def _():
        finish(wgrad_other, True)


def project_back(own_grads, other_grads, mixed, order, weight, weight_other):
    half = own_grads[0].shape[0]
    own, other = own_half(half), other_half(half)

    def specs(at):
        kv_spec = pl.BlockSpec((1, 2, 4, BODY, 128), lambda i: (at(i), 0, 0, 0, 0))
        return [pl.BlockSpec((1, 4, BODY, 128), lambda i: (at(i), 0, 0, 0)), kv_spec, kv_spec]

    weight_specs = [pl.BlockSpec((D, 384), lambda i: (0, own(i))), pl.BlockSpec((D, 384), lambda i: (0, other(i)))]
    weight_shape = jax.ShapeDtypeStruct(weight.shape, BF16)
    return pl.pallas_call(
        project_back_kernel,
        grid=(2 * half,),
        out_shape=(jax.ShapeDtypeStruct((4, BODY, D), BF16), weight_shape, weight_shape),
        in_specs=[*specs(own), *specs(other), whole(mixed.shape), whole(order.shape), *weight_specs],
        out_specs=(whole((4, BODY, D)), whole(weight.shape), whole(weight.shape)),
        scratch_shapes=[
            pltpu.VMEM((4, BODY, D), F32), pltpu.VMEM((D, 4 * BODY), BF16),
            pltpu.VMEM((4, BODY, weight.shape[1]), BF16), pltpu.VMEM(weight.shape, BF16),
        ],
        compiler_params=params("arbitrary"),
        name="project_back",
    )(*own_grads, *other_grads, mixed, order, weight, weight_other)


def back_kernel(
    scal_ref, x_ref, gmixed_ref, gedge_ref, base_ref, shifted_ref, gres_ref, perm_ref, mod_ref, taps_ref,
    out_ref, sums_ref, taps_grad,
    gm, gm_moved, gnorm,
):
    width, gap, long_latent, place = geometry(scal_ref)
    clear_borders(gm)
    clear_borders(gm_moved)
    masks = column_masks(64, width)
    edge_masks = column_masks(EDGE, width)

    @pl.loop(0, 8)
    def _(block):
        place_in = pl.ds(pl.multiple_of(block * 64, 64), 64)
        place_out = pl.ds(pl.multiple_of(body_offset(block // 4, gap) + (block % 4) * 64, 16), 64)
        for group in range(4):
            value = gmixed_ref[group, place_in, :].astype(F32)
            gm[group, place_out, :] = value
            gm_moved[group, place_out, :] = moved_rows(value, group % 2, masks)

    @pl.when(long_latent)
    def _():
        at = pl.ds(edge_offset(place), EDGE)
        for group in range(4):
            value = gedge_ref[group].astype(F32)
            gm[group, at, :] = value
            gm_moved[group, at, :] = moved_rows(value, group % 2, edge_masks)

    for lane in range(D // 128):
        lanes = pl.ds(lane * 128, 128)
        kernel = kernel_rows(taps_ref, lanes, 16)

        def back_tile(tile, sums, lanes=lanes, kernel=kernel):
            offset = pl.multiple_of(body_offset(tile // 16, gap) + (tile % 16) * 16, 16)
            rows = pl.ds(pl.multiple_of(tile * 16, 16), 16)
            found = variants(gm, gm_moved, offset, width, 16, lanes)
            for p in (0, 1):
                for q in (0, 1):
                    gnorm[2 * p + q, rows, lanes] = conv_at(found, kernel, p, q, flip=True).astype(BF16)
            totals = taps_at(found, variants(base_ref, shifted_ref, offset, width, 16, lanes))
            return tuple(total + more for total, more in zip(sums, totals))

        sums = lax.fori_loop(0, 32, back_tile, (jnp.zeros((8, 128), F32),) * 9, unroll=2)
        for index in range(9):
            taps_grad[index : index + 1, lanes] = jnp.sum(sums[index], 0, keepdims=True)

    sums_ref[...] = jnp.zeros_like(sums_ref)

    @pl.loop(0, 8, unroll=2)
    def _(block):
        half = block // 4
        scale = mod_ref[half, 1:2, :]
        rows = pl.ds(pl.multiple_of(block * 64, 64), 64)
        result = None
        for group in range(4):
            normed, inverse = normalize(x_ref[group, rows, :].astype(F32))
            back = gnorm[group, rows, :].astype(F32)
            grad = gres_ref[group, rows, :].astype(F32) + norm_back(back * (1.0 + scale), normed, inverse)
            sums_ref[half, 0:1, :] += jnp.sum(back, 0, keepdims=True)
            sums_ref[half, 1:2, :] += jnp.sum(back * normed, 0, keepdims=True)
            part = nn(perm_ref[:, 64 * group : 64 * group + 64], grad.astype(BF16))
            result = part if result is None else result + part
        out_ref[pl.ds(pl.multiple_of(block * 256, 256), 256), :] = result.astype(BF16)


def back(scal, x, gmixed, gedge, base, shifted, gres, perm, mod, taps):
    arrays = (x, gmixed, gedge, base, shifted, gres, perm, mod, taps)
    plane = pltpu.VMEM((4, PLANE, D), F32)
    return pl.pallas_call(
        back_kernel,
        out_shape=(
            jax.ShapeDtypeStruct((2048, D), BF16),
            jax.ShapeDtypeStruct((2, 8, D), F32),
            jax.ShapeDtypeStruct((16, D), F32),
        ),
        in_specs=[scalars()] + [pl.BlockSpec(memory_space=pltpu.VMEM)] * len(arrays),
        out_specs=(pl.BlockSpec(memory_space=pltpu.VMEM),) * 3,
        scratch_shapes=[plane, plane, pltpu.VMEM((4, BODY, D), BF16)],
        compiler_params=params(),
        name="back",
    )(scal, *arrays)


MESH = pl.DeviceIdType.MESH


def chip_grid(count):
    return {16: (4, 2, 2), 64: (4, 4, 4)}.get(count, (count, 1, 1))


def reduce_gather_kernel(grid, units, *refs):
    own_refs, other_refs, sent_ref = refs[:units], refs[units : 2 * units], refs[2 * units]
    sum_refs, all_ref = refs[2 * units + 1 : 3 * units + 1], refs[3 * units + 1]
    scratch = refs[3 * units + 2 :]
    buffers = [scratch[10 * unit : 10 * unit + 10] for unit in range(units)]
    gz, gx, gy, sends, recvs = scratch[10 * units :]
    deep, tall, broad = grid
    low = deep // 2
    wide = lax.axis_index("wide")
    place = lax.axis_index("narrow")
    z, y, x = wide // (tall * broad), (wide // broad) % tall, wide % broad

    def chip(zz, yy, xx):
        return {"wide": (zz * tall + yy) * broad + xx, "narrow": place}

    def along_x(step):
        return chip(z, y, (x + step) % broad)

    def along_y(step):
        return chip(z, (y + step) % tall, x)

    def along_z(step):
        return chip((z + step) % deep, y, x)

    sibling = {"wide": wide, "narrow": 1 - place}
    partners = (
        [sibling]
        + [along_x(step) for step in range(1, broad)]
        + [along_y(step) for step in range(1, tall)]
        + [along_z(step) for step in range(1, deep)]
    )
    barrier = pltpu.get_barrier_semaphore()
    for partner in partners:
        pl.semaphore_signal(barrier, inc=1, device_id=partner, device_id_type=MESH)
    pl.semaphore_wait(barrier, len(partners))

    count = [0]

    def send(source, target, partner):
        copy = pltpu.make_async_remote_copy(
            src_ref=source, dst_ref=target, send_sem=sends.at[count[0]], recv_sem=recvs.at[count[0]],
            device_id=partner, device_id_type=MESH,
        )
        count[0] += 1
        copy.start()
        return copy

    def wait(copies):
        for copy in copies:
            copy.wait()

    def add(target, *sources):
        total = sources[0].astype(F32)
        for source in sources[1:]:
            total = total + source.astype(F32)
        return total.astype(target.dtype)

    gz[z] = sent_ref[...]
    halves = ((0, low), (low, deep))
    swaps = [
        [send(other.at[start:stop], buffer[0].at[start:stop], sibling) for other, buffer in zip(other_refs, buffers)]
        for start, stop in halves
    ]
    gathers = [send(sent_ref, gz.at[z], along_z(step)) for step in range(1, deep)]

    def add_first(start, stop):
        for own, (first, work, *_) in zip(own_refs, buffers):
            for zz in range(start, stop):

                @pl.loop(0, tall * broad)
                def _(at, zz=zz, own=own, first=first, work=work):
                    yy, xx = at // broad, at % broad
                    work[zz, yy, xx] = add(work, own[zz, yy, xx], first[zz, yy, xx])

    wait(swaps[0])
    add_first(0, low)
    one_a = [
        send(work.at[0:low, :, (x + s) % broad], r1a.at[s - 1], along_x(s))
        for _, work, r1a, *_ in buffers
        for s in range(1, broad)
    ]
    wait(swaps[1])
    add_first(low, deep)
    one_b = [
        send(work.at[low:deep, (y + s) % tall], r1b.at[s - 1], along_y(s))
        for _, work, _, r1b, *_ in buffers
        for s in range(1, tall)
    ]
    wait(gathers)
    gx[x] = gz[...]
    gathers = [send(gz, gx.at[x], along_x(step)) for step in range(1, broad)]

    wait(one_a)
    two_a = []
    for _, work, r1a, _, w1a, _, r2a, *_ in buffers:
        for zz in range(low):
            for yy in range(tall):
                w1a[zz, yy] = add(w1a, work[zz, yy, x], *[r1a[s, zz, yy] for s in range(broad - 1)])
        two_a += [send(w1a.at[:, (y + s) % tall], r2a.at[s - 1], along_y(s)) for s in range(1, tall)]
    wait(one_b)
    two_b = []
    for _, work, _, r1b, _, w1b, _, r2b, *_ in buffers:
        for zz in range(deep - low):
            for xx in range(broad):
                w1b[zz, xx] = add(w1b, work[low + zz, y, xx], *[r1b[s, zz, xx] for s in range(tall - 1)])
        two_b += [send(w1b.at[:, (x + s) % broad], r2b.at[s - 1], along_x(s)) for s in range(1, broad)]
    wait(gathers)
    gy[y] = gx[...]
    gathers = [send(gx, gy.at[y], along_y(step)) for step in range(1, tall)]

    wait(two_a)
    for _, _, _, _, w1a, _, r2a, _, w2, _ in buffers:
        for zz in range(low):
            w2[zz] = add(w2, w1a[zz, y], *[r2a[s, zz] for s in range(tall - 1)])
    wait(two_b)
    three = []
    for _, _, _, _, _, w1b, _, r2b, w2, r3 in buffers:
        for zz in range(deep - low):
            w2[low + zz] = add(w2, w1b[zz, x], *[r2b[s, zz] for s in range(broad - 1)])
        three += [send(w2.at[(z + s) % deep], r3.at[s - 1], along_z(s)) for s in range(1, deep)]
    wait(gathers)
    all_ref[place] = gy[...]
    gathers = [send(gy, all_ref.at[place], sibling)]
    wait(three)
    for sum_ref, buffer in zip(sum_refs, buffers):
        w2, r3 = buffer[8:]
        sum_ref[...] = add(sum_ref, w2[z], *[r3[s] for s in range(deep - 1)])
    wait(gathers)


def reduce_gather(own, other, sent):
    deep, tall, broad = grid = chip_grid(own[0].shape[0])
    low = deep // 2
    shapes = [array.shape[1:] for array in own]
    copies = len(own) * (2 + 2 * (broad - 1 + tall - 1) + (deep - 1)) + (deep - 1) + (broad - 1) + (tall - 1) + 1

    def buffers(unit):
        def slots(count, *shape):
            return pltpu.VMEM((max(count, 1), *shape, *unit), BF16)

        return [
            pltpu.VMEM((*grid, *unit), BF16), pltpu.VMEM((*grid, *unit), BF16),
            slots(broad - 1, low, tall), slots(tall - 1, deep - low, broad),
            pltpu.VMEM((low, tall, *unit), BF16), pltpu.VMEM((deep - low, broad, *unit), BF16),
            slots(tall - 1, low), slots(broad - 1, deep - low),
            pltpu.VMEM((deep, *unit), BF16), slots(deep - 1),
        ]

    row = sent.shape
    space = pl.BlockSpec(memory_space=pltpu.VMEM)
    result = pl.pallas_call(
        functools.partial(reduce_gather_kernel, grid, len(own)),
        out_shape=(
            *[jax.ShapeDtypeStruct(unit, F32) for unit in shapes],
            jax.ShapeDtypeStruct((2, tall, broad, deep, *row), BF16),
        ),
        in_specs=[space] * (2 * len(own) + 1),
        out_specs=(space,) * (len(own) + 1),
        scratch_shapes=[
            *[buffer for unit in shapes for buffer in buffers(unit)],
            pltpu.VMEM((deep, *row), BF16), pltpu.VMEM((broad, deep, *row), BF16),
            pltpu.VMEM((tall, broad, deep, *row), BF16),
            pltpu.SemaphoreType.DMA((copies,)), pltpu.SemaphoreType.DMA((copies,)),
        ],
        compiler_params=pltpu.CompilerParams(
            collective_id=1, has_side_effects=True, vmem_limit_bytes=VMEM_BYTES
        ),
        name="reduce_gather",
    )(*[array.reshape(*grid, *array.shape[1:]) for array in (*own, *other)], sent)
    return result[:-1], result[-1].reshape(-1, *row)


def square_sum_kernel(grid, *refs):
    count = len(refs) - 6
    grads = refs[:count]
    out_ref, mine, near, far, sends, recvs = refs[count:]
    deep, tall, broad = grid
    wide = lax.axis_index("wide")
    place = lax.axis_index("narrow")
    z, across = wide // (tall * broad), wide % (tall * broad)
    line = z * 2 + place

    def near_device(step):
        other = (line + step) % (2 * deep)
        return {"wide": (other // 2) * (tall * broad) + across, "narrow": other % 2}

    def far_device(step):
        return {"wide": z * (tall * broad) + (across + step) % (tall * broad), "narrow": place}

    nears = [near_device(step) for step in range(1, 2 * deep)]
    fars = [far_device(step) for step in range(1, tall * broad)]
    barrier = pltpu.get_barrier_semaphore()
    for partner in nears + fars:
        pl.semaphore_signal(barrier, inc=1, device_id=partner, device_id_type=MESH)

    total = jnp.zeros((), F32)
    for grad in grads:
        value = grad[...].astype(F32)
        total = total + jnp.sum(value * value)
    mine[...] = jnp.full((8, 128), total, F32)
    pl.semaphore_wait(barrier, len(nears + fars))

    def exchange(slots, partners, first):
        copies = []
        for step, partner in enumerate(partners):
            copy = pltpu.make_async_remote_copy(
                src_ref=mine, dst_ref=slots.at[step], send_sem=sends.at[first + step],
                recv_sem=recvs.at[first + step], device_id=partner, device_id_type=MESH,
            )
            copy.start()
            copies.append(copy)
        for copy in copies:
            copy.wait()
        value = mine[...]
        for step in range(len(partners)):
            value = value + slots[step]
        return value

    mine[...] = exchange(near, nears, 0)
    out_ref[...] = exchange(far, fars, len(nears))


def square_sum(wide_count, grads):
    deep, tall, broad = grid = chip_grid(wide_count)
    near, far = 2 * deep - 1, tall * broad - 1
    return pl.pallas_call(
        functools.partial(square_sum_kernel, grid),
        out_shape=jax.ShapeDtypeStruct((8, 128), F32),
        in_specs=[pl.BlockSpec(memory_space=pltpu.VMEM)] * len(grads),
        out_specs=pl.BlockSpec(memory_space=pltpu.VMEM),
        scratch_shapes=[
            pltpu.VMEM((8, 128), F32), pltpu.VMEM((near, 8, 128), F32), pltpu.VMEM((max(far, 1), 8, 128), F32),
            pltpu.SemaphoreType.DMA((near + far,)), pltpu.SemaphoreType.DMA((near + far,)),
        ],
        compiler_params=pltpu.CompilerParams(
            collective_id=2, has_side_effects=True, vmem_limit_bytes=VMEM_BYTES
        ),
        name="square_sum",
    )(*grads)


def shared_rows(shared_ref, rows):
    half = FF // 2 * rows // D
    shared = shared_ref[...].astype(F32)
    up = [shared[at : at + rows] for at in (0, rows)]
    down = shared[2 * rows : 2 * rows + half]
    out = shared[2 * rows + half : 2 * rows + half + rows // 2]
    return [[out], up, [down]]


def adamw_kernel(rates, square_ref, shared_ref, *refs):
    clip_limit = PARAMS**0.5
    norm = jnp.sqrt(square_ref[0:1, 0:1])
    factor = clip_limit / jnp.maximum(norm, clip_limit)
    plain = (len(refs) - 3 * 7) // 8
    count = plain + 3
    grads = [[ref[...]] for ref in refs[:plain]]
    states, outs = refs[plain : plain + 3 * count], refs[plain + 3 * count :]
    grads += shared_rows(shared_ref, states[3 * (plain + 1)].shape[0])
    for index, rate in enumerate(rates):
        master_ref, first_ref, second_ref = states[3 * index : 3 * index + 3]
        first_out, second_out, master_out, copy_out = outs[4 * index : 4 * index + 4]
        start = 0
        for grad in grads[index]:
            at = (slice(None), slice(start, start + grad.shape[1]))
            start += grad.shape[1]
            scaled = grad * factor
            first_new = BETA_ONE * first_ref[at] + (1.0 - BETA_ONE) * scaled
            second_new = BETA_TWO * second_ref[at] + (1.0 - BETA_TWO) * scaled * scaled
            ratio = (first_new * (1.0 / (1.0 - BETA_ONE**STEP))) / (
                jnp.sqrt(second_new * (1.0 / (1.0 - BETA_TWO**STEP))) + ADAM_EPS
            )
            master = master_ref[at]
            master_new = master - rate * (ratio + WEIGHT_DECAY * master)
            first_out[at] = first_new
            second_out[at] = second_new
            master_out[at] = master_new
            copy_out[at] = master_new.astype(BF16)


def adamw(square, shared, grads, states, rates):
    arrays = [array for state in states for array in state]
    shapes = [
        jax.ShapeDtypeStruct(state[0].shape, dtype) for state in states for dtype in (F32, F32, F32, BF16)
    ]
    space = pl.BlockSpec(memory_space=pltpu.VMEM)
    return pl.pallas_call(
        functools.partial(adamw_kernel, rates),
        out_shape=shapes,
        in_specs=[space] * (2 + len(grads) + len(arrays)),
        out_specs=[space] * len(shapes),
        compiler_params=params(),
        name="adamw",
    )(square, shared, *grads, *arrays)


def timestep_code(stamps, channels):
    half_dim = channels // 2
    scales = jnp.exp(-jnp.log(10000.0) * jnp.arange(half_dim, dtype=F32) / half_dim)
    angles = stamps.astype(F32)[:, None] * scales[None, :]
    return jnp.concatenate([jnp.cos(angles), jnp.sin(angles)], axis=1)


def one_hot_rows(source, columns, valid=None):
    hit = source[:, None] == jnp.arange(columns, dtype=jnp.int32)[None, :]
    if valid is not None:
        hit = jnp.logical_and(hit, valid[:, None])
    return hit.astype(BF16)


def permutation(long_latent):
    row = jnp.arange(256, dtype=jnp.int32)
    p, q, s = row // 128, (row // 64) % 2, row % 64
    big = (2 * (s // 32) + p) * 64 + 2 * (s % 32) + q
    small = (2 * (s // 16) + p) * 32 + 2 * (s % 16) + q
    return one_hot_rows(jnp.where(long_latent, big, small), 256)


def edge_permutation():
    row = jnp.arange(128, dtype=jnp.int32)
    return one_hot_rows((row // 64) * 64 + 2 * (row % 32) + (row // 32) % 2, 128)


def pair_order():
    row = jnp.arange(6 * HS, dtype=jnp.int32)
    return one_hot_rows((row % 192) // HS * 128 + row // 192 * HS + row % HS, 6 * HS)


def tap_rows(kernel):
    return jnp.pad(kernel.T, ((0, 7), (0, 0)))


def per_device(tokens, cotangent, size_tags, timesteps, labels, *weights_and_states):
    modulator, class_table, mix_kernel, heads_in, heads_out, up_weight, hidden_kernel, down_weight = weights_and_states[:8]
    states = [weights_and_states[8 + 3 * i : 11 + 3 * i] for i in range(8)]
    wide_count = lax.axis_size("wide")
    wide = lax.axis_index("wide")
    place = lax.axis_index("narrow")
    cell = wide * 2 + place
    cells = wide_count * 2

    def swap(value):
        return lax.ppermute(value, "narrow", [(0, 1), (1, 0)])

    def boundary(body):
        return jnp.where(place == 0, body[:, BODY - EDGE :], body[:, :EDGE])

    edge = swap(jnp.where(place == 0, tokens[-4 * EDGE :], tokens[: 4 * EDGE]))
    hin_other = swap(heads_in)
    hout_other = swap(heads_out)
    up_other = swap(up_weight)
    down_other = swap(down_weight)
    taps_own = tap_rows(hidden_kernel)
    taps_other = swap(taps_own)
    mix_taps = tap_rows(mix_kernel)

    long_latent = size_tags[0] > SIDE * SIDE
    width = jnp.where(long_latent, SIDE, SIDE // 2)
    gap = jnp.where(long_latent, 0, 16)
    scal = jnp.stack([width, gap, long_latent.astype(jnp.int32), place]).astype(jnp.int32)
    perm = permutation(long_latent)
    perm_back = perm.T
    order = pair_order()
    embedded = timestep_code(timesteps, D) + class_table[:, labels].astype(F32).T
    cond_low = jax.nn.silu(embedded).astype(BF16)
    modulation = jnp.dot(cond_low, modulator, preferred_element_type=F32).reshape(-1, 6, D)
    mod = jnp.pad(modulation, ((0, 0), (0, 2), (0, 0)))

    x, mixed, base, shifted, q, kv = front(
        scal, tokens, edge, perm, edge_permutation(), mod, mix_taps, order, heads_in
    )
    kv_far_other = swap(kv)
    q_other, kv_other = project(mixed, order, hin_other)
    kv_far = swap(kv_other)
    attended_other, logs_other = attention(scal, q_other, kv_other, kv_far_other)
    attended, logs = attention(scal, q, kv, kv_far)
    attn, norm, cot, grad_ffn = middle(x, attended, attended_other, cotangent, perm, mod, heads_out, hout_other)
    norm_edge, grad_edge = swap((boundary(norm), boundary(grad_ffn)))
    ffn, back_norm, up_grad, up_grad_other, down_grad, down_grad_other, taps_grad = feed_forward(
        scal, taps_own, taps_other, norm, norm_edge, grad_ffn, grad_edge, up_weight, up_other, down_weight, down_other
    )

    output, grad_residual, grad_attended, grad_attended_other, sums_two, hout_grad, hout_grad_other = turn(
        x, attn, ffn, cot, back_norm, attended, attended_other, perm_back, mod, heads_out, hout_other
    )
    rows = D // wide_count
    half = FF // 2
    up_sum = up_grad.astype(F32) + swap(up_grad_other).astype(F32)
    down_sum = down_grad.astype(F32) + swap(down_grad_other).astype(F32)
    hout_sum = hout_grad.astype(F32) + swap(hout_grad_other).astype(F32)
    tap_half = taps_grad.shape[0] // 2
    taps_sum = taps_grad[:tap_half, :9] + swap(taps_grad[tap_half:, :9])
    tap_part = taps_sum.transpose(0, 2, 1).reshape(wide_count, -1)
    tap_part = jnp.pad(tap_part, ((0, 0), (0, -tap_part.shape[1] % D)))
    grads = jnp.concatenate(
        [
            up_sum.reshape(2, wide_count, rows, D).transpose(1, 0, 2, 3).reshape(wide_count, 2 * rows, D),
            down_sum.reshape(wide_count, -1, D),
            hout_sum.reshape(wide_count, -1, D),
            tap_part.reshape(wide_count, -1, D),
        ],
        axis=1,
    )
    pad = -grads.shape[1] % 16
    grads = jnp.pad(grads, ((0, 0), (0, pad), (0, 0))).astype(BF16)
    grads, grad_attended_other = lax.optimization_barrier((grads, grad_attended_other))
    mine = lax.psum_scatter(grads, "wide", scatter_dimension=0, tiled=False)

    gq_other, gkv_other, gkv_far_other = attention_back(
        scal, q_other, kv_other, kv_far_other, attended_other, grad_attended_other, logs_other
    )
    gkv_add = swap(gkv_far_other)
    gq, gkv, gkv_far = attention_back(scal, q, kv, kv_far, attended, grad_attended, logs)
    gkv_add_other = swap(gkv_far)
    gmixed, hin_grad, hin_grad_other = project_back(
        (gq, gkv, gkv_add), (gq_other, gkv_other, gkv_add_other), mixed, order, heads_in, hin_other
    )
    gmixed_edge = swap(boundary(gmixed))
    input_grad, sums_one, mix_grad = back(
        scal, x, gmixed, gmixed_edge, base, shifted, grad_residual, perm_back, mod, mix_taps
    )

    modulation_two_grad = sums_two[:, 1:3].reshape(-1, 2 * D)
    own = D // cells
    mix_parts = mix_grad[:9].T.reshape(wide_count, 2, 1, own * 9).transpose(1, 0, 2, 3).astype(BF16)
    mix_parts = jnp.pad(mix_parts, ((0, 0), (0, 0), (0, 15), (0, -own * 9 % 128)))
    mix_own = jnp.where(place == 0, mix_parts[0], mix_parts[1])
    mix_other = jnp.where(place == 0, mix_parts[1], mix_parts[0])

    def by_chip(grad):
        split = grad.reshape(wide_count, rows, -1)
        return jnp.pad(split, ((0, 0), (0, -rows % 16), (0, 0)))

    slope = jax.vjp(jax.nn.silu, embedded)[1](jnp.ones_like(embedded))[0]
    blocks = jnp.concatenate([sums_one[:, 0:2], sums_two[:, 0:4]], axis=1).transpose(1, 0, 2).reshape(12, D)
    digits = jnp.stack([labels // 32, labels % 32], axis=1).astype(F32)
    digits = jnp.pad(digits, ((0, 14), (0, 126)))
    sent = jnp.concatenate([jnp.concatenate([blocks, cond_low.astype(F32), slope], axis=0), digits], axis=1)
    (hin_mine, mix_mine), everyone = reduce_gather(
        [by_chip(hin_grad), mix_own], [by_chip(hin_grad_other), mix_other], sent.astype(BF16)
    )
    row = jnp.arange(16, dtype=jnp.int32)
    block_row = 2 * jnp.arange(6, dtype=jnp.int32)[:, None] + jnp.arange(2, dtype=jnp.int32)
    picks = (block_row[:, :, None] == row).astype(F32)
    columns = lax.dynamic_slice_in_dim(everyone[:, 12:], cell * own, own, 2).astype(F32)
    all_cond, all_slope = columns[:, :2], columns[:, 2:]
    flat = everyone.reshape(cells * 16, -1)
    left = jnp.einsum("cfd,kfr->kdcr", all_cond, picks).astype(BF16).reshape(6 * own, cells * 16)
    modulator_mine = jnp.dot(left, flat, preferred_element_type=F32)[:, :D]
    modulator_mine = modulator_mine.reshape(6, own, D).transpose(1, 0, 2).reshape(own, 6 * D)
    modulator_rows = lax.dynamic_slice_in_dim(modulator, cell * own, own, 0).reshape(own, 6, D)
    modulator_rows = modulator_rows.transpose(1, 0, 2).reshape(6 * own, D)
    products = lax.dot_general(
        flat[:, :D], modulator_rows, (((1,), (1,)), ((), ())), preferred_element_type=F32
    ).reshape(cells, 16, 6, own)
    all_embedded = all_slope * jnp.stack(
        [sum(products[:, 2 * block + frame, block] for block in range(6)) for frame in range(2)], axis=1
    )
    all_digits = everyone[:, :2, D : D + 2].astype(jnp.int32)
    all_labels = (all_digits[..., 0] * 32 + all_digits[..., 1])[..., None]
    chosen = (all_labels == jnp.arange(class_table.shape[1], dtype=jnp.int32)).astype(F32)
    class_mine = jnp.dot(
        all_embedded.reshape(cells * 2, own).T, chosen.reshape(cells * 2, -1),
        precision=lax.Precision.HIGHEST, preferred_element_type=F32,
    )
    mix_mine = mix_mine[0, : own * 9].reshape(own, 9).T
    hin_mine = hin_mine[:rows]

    shared = 2 * rows + half // wide_count + rows // 2
    hidden = half // wide_count
    taps_mine = mine[shared:].reshape(-1)[: hidden * 9].reshape(hidden, 9).T.astype(F32)
    shards = (modulator_mine, class_mine, mix_mine, hin_mine, taps_mine)
    square = square_sum(wide_count, (*shards[:4], mine))
    grad_norm = jnp.sqrt(square[0, 0])
    order = (0, 1, 2, 3, 6, 4, 5, 7)
    step_rates = (
        D ** (-0.5), 1.0, 1.0 / 3.0, D ** (-0.5), 1.0 / 3.0, (D // 32) ** (-0.5), D ** (-0.5), FF ** (-0.5),
    )
    turned = (2, 6)
    given = [tuple(array.T for array in states[i]) if i in turned else states[i] for i in order]
    updated = adamw(square, mine, shards, given, step_rates)
    flat = [None] * 32
    for at, i in enumerate(order):
        for j in range(4):
            array = updated[4 * at + j]
            flat[4 * i + j] = array.T if i in turned else array
    return (output, input_grad, grad_norm, *flat, modulation_two_grad)


def solution(mesh):
    both = P(("wide", "narrow"), None)
    turned = P(("narrow", "wide"), None)
    grid = P("wide", "narrow")
    places = (both, both, both, grid, turned, grid, turned, turned)
    in_specs = (
        both, both, P("wide"), P(("wide", "narrow")), P(("wide", "narrow")),
        P(), P(), P(), P(None, "narrow"), P("narrow", None), P(None, "narrow"), P("narrow", None), P("narrow", None),
        *[place for place in places for _ in range(3)],
    )
    out_specs = (both, both, P(), *[place for place in places for _ in range(4)], both)
    return jax.shard_map(per_device, mesh=mesh, in_specs=in_specs, out_specs=out_specs, check_vma=False)
```

time: 660 us -> 587 us (0.89)
  local copies, waits for them, and re-layouts: 61.5 us -> 26.1 us
  Pallas kernels: 510 us -> 495 us
  waiting for transfers between devices: 19.6 us -> 7.04 us
  other arithmetic: 28.7 us -> 18.6 us
    reshape x9 -> x2, local copies, waits for them, and re-layouts: 16.2 us -> 0.61 us  [the longest x1 0.58 us: per_device(): jnp.einsum('cfd,kfr->kdcr', all_cond, picks).astype(BF16)]
    unnamed x69 -> x41, local copies, waits for them, and re-layouts: 22 us -> 7.44 us
    ppermute x15 -> x17, waiting for transfers between devices: 19.5 us -> 7.02 us  [swap(): return lax.ppermute(value, 'narrow', [(0, 1), (1, 0)])]
    pallas_call x1, Pallas kernels: 31.1 us -> 19 us  [turn(): pl.pallas_call(turn_kernel, grid=(8,), out_shape=(jax.ShapeDtypeStruct((2...]
    pallas_call x3 -> x4, Pallas kernels: 245 us -> 256 us  [the longest x1 167 us: feed_forward(): pl.pallas_call(ffn_kernel, grid=(steps,), out_shape=(body, body, *[jax.Sh...]
    pallas_call x1, Pallas kernels: 32 us -> 22.8 us  [front(): pl.pallas_call(front_kernel, grid=(pairs,), out_shape=(body, body, plane,...]
    concatenate x3 -> x0, other arithmetic: 8.88 us -> none  [the longest x1 4.48 us: per_device(): parts = jnp.concatenate([hin_parts, mix_parts], axis=2)]
    slice x12 -> x7, local copies, waits for them, and re-layouts: 12.7 us -> 4.9 us  [the longest x1 1.22 us: per_device(): everyone[:, 12:]]
  transfers between devices with their start and end apart: 16 -> 18, of which waited for: 5 -> 4; matrix products, arithmetic and copies ran while one was open for 11% -> 6% of each run, Pallas kernels for 44% -> 54%
where the time goes in v2:
time: 587 us; the launch traced here: 575 us
  Pallas kernels  495 us (84%)
  local copies, waits for them, and re-layouts  26.1 us (4%)
  other arithmetic  18.6 us (3%)
  between operations  17.2 us (3%)
  waiting for transfers between devices  7.04 us (1%)
  matrix products  6.41 us (1%)
    pallas_call x1, Pallas kernels, feed_forward(): pl.pallas_call(ffn_kernel, grid=(steps,), out_shape=(body, body, *[jax.Sh...  167 us
    pallas_call x2, Pallas kernels, attention_back(): pl.pallas_call(attend_back_kernel, grid=(pairs, 4), out_shape=(jax.ShapeD...  91.2 us
    pallas_call x2, Pallas kernels, attention(): pl.pallas_call(attend_kernel, grid=(pairs, 4), out_shape=(jax.ShapeDtypeS...  47.6 us
    pallas_call x1, Pallas kernels, reduce_gather(): pl.pallas_call(functools.partial(reduce_gather_kernel, grid, len(own)), o...  43.9 us
    pallas_call x1, Pallas kernels, project_back(): pl.pallas_call(project_back_kernel, grid=(2 * half,), out_shape=(jax.Shap...  34.7 us
    pallas_call x1, Pallas kernels, back(): pl.pallas_call(back_kernel, out_shape=(jax.ShapeDtypeStruct((2048, D), BF...  26.5 us
    pallas_call x1, Pallas kernels, front(): pl.pallas_call(front_kernel, grid=(pairs,), out_shape=(body, body, plane,...  22.8 us
    pallas_call x1, Pallas kernels, turn(): pl.pallas_call(turn_kernel, grid=(8,), out_shape=(jax.ShapeDtypeStruct((2...  19 us
  transfers between devices with their start and end apart: 18, of which 4 were waited for; matrix products, arithmetic and copies ran while one was open for 6% of the time, Pallas kernels for 54%

profile of v2, /device:TPU:0, one launch (start us, length us, event | category | flops | bytes accessed | tf_op | source)
XLA Modules:
  0.0 575.3 jit_solution(13464110151148466555)
XLA Ops:
  7.3 1.2 slice_select_fusion.3
  11.8 4.0 fusion.73
  17.7 0.8 fusion.12
  18.5 0.8 fusion.10.order_ref
  19.3 0.7 fusion.15.edge_perm_ref
  20.7 22.8 %front.1 = (bf16[4,512,768]{2,1,0:T(8,128)(2,1)}, bf16[4,512,768]{2,1,0:T(8,128)(2,1)}, bf16[4,592,768]{2,1,0:T(8,128)(2,1)}, bf16[4,592,768]{2,1,0:T(8,128)(2,1...) custom-call(s32[4]{0:T(128)} %pad_add_fusion.scal_ref, bf16[2048,768]{1,0:T(8,128)(2,1)} %x_ref.1, ...), custom_call_target="tpu_custom_call" | custom-call | tf_op jit(solution)/shard_map/front/pallas_call | solution.py:228
  44.0 10.0 %project.1 = (bf16[3,4,512,128]{3,2,1,0:T(8,128)(2,1)}, bf16[3,2,4,512,128]{4,3,2,1,0:T(8,128)(2,1)}) custom-call(bf16[4,512,768]{2,1,0:T(8,128)(2,1)} %get-tuple-element.118.mixed_ref, bf16[384,384]{1,0:T(8,128)(2,1)} %fusion.10.order_ref, bf16[768,1152]{1,0:T(8,128)(2,1)} %collective-permute-done.1.weight_ref.other_ref), custom_call_target="tpu_custom_call" | custom-call | tf_op jit(solution)/shard_map/project/pallas_call | solution.py:245
  55.0 1.7 copy-done.2
  56.7 23.8 %attention.3 = (bf16[4,512,384]{2,1,0:T(8,128)(2,1)}, bf16[3,4,512,128]{3,2,1,0:T(8,128)(2,1)}) custom-call(s32[4]{0:T(128)} %pad_add_fusion.scal_ref, bf16[3,4,512,128]{3,2,1,0:T(8,128)(2,1)} %get-tuple-element.121.q_ref, bf16[3,2,4,512,128]{4,3,2,1,0:T(8,128)(2,1)} %get-tuple-element.119.own_ref, bf16[3,2,4,512,128]{4,3,2,1,0:T(8,128)(2,1)} %copy-done.2), custom_call_target="tpu_custom_call" | custom-call | tf_op jit(solution)/shard_map/attention/pallas_call | solution.py:329
  80.4 23.8 %attention.2 = (bf16[4,512,384]{2,1,0:T(8,128)(2,1)}, bf16[3,4,512,128]{3,2,1,0:T(8,128)(2,1)}) custom-call(s32[4]{0:T(128)} %pad_add_fusion.scal_ref, bf16[3,4,512,128]{3,2,1,0:T(8,128)(2,1)} %get-tuple-element.116.q_ref, bf16[3,2,4,512,128]{4,3,2,1,0:T(8,128)(2,1)} %get-tuple-element.117.own_ref, bf16[3,2,4,512,128]{4,3,2,1,0:T(8,128)(2,1)} %collective-permute-done.2.other_ref), custom_call_target="tpu_custom_call" | custom-call | tf_op jit(solution)/shard_map/attention/pallas_call | solution.py:329
  104.2 15.2 %middle.1 = (bf16[4,512,768]{2,1,0:T(8,128)(2,1)}, bf16[4,512,768]{2,1,0:T(8,128)(2,1)}, bf16[4,512,768]{2,1,0:T(8,128)(2,1)}, bf16[4,512,768]{2,1,0:T(8,128)(2,1)}) custom-call(bf16[4,512,768]{2,1,0:T(8,128)(2,1)} %get-tuple-element.115.x_ref, bf16[4,512,384]{2,1,0:T(8,128)(2,1)} %get-tuple-element.120.mix_own.mix_ref, ...), custom_call_target="tpu_custom_call" | custom-call | tf_op jit(solution)/shard_map/middle/pallas_call | solution.py:457
  119.5 1.0 slice_select_fusion.2
  120.7 1.0 slice_select_fusion.1
  122.4 1.1 collective-permute-done.5.taps_other
  124.9 167.4 %feed_forward.1 = (bf16[4,512,768]{2,1,0:T(8,128)(2,1)}, bf16[4,512,768]{2,1,0:T(8,128)(2,1)}, bf16[2,768,768]{2,1,0:T(8,128)(2,1)}, bf16[2,768,768]{2,1,0:T(8,1...) custom-call(s32[4]{0:T(128)} %pad_add_fusion.scal_ref, ...), custom_call_target="tpu_custom_call" | custom-call | tf_op jit(solution)/shard_map/feed_forward/pallas_call | solution.py:661
  292.9 19.0 %turn.1 = (bf16[2048,768]{1,0:T(8,128)(2,1)}, bf16[4,512,768]{2,1,0:T(8,128)(2,1)}, bf16[4,512,384]{2,1,0:T(8,128)(2,1)}, bf16[4,512,384]{2,1,0:T(8,128)(2,1)}, ...) custom-call(bf16[4,512,768]{2,1,0:T(8,128)(2,1)} %get-tuple-element.115.x_ref, ...), custom_call_target="tpu_custom_call" | custom-call | tf_op jit(solution)/shard_map/turn/pallas_call | solution.py:754
  312.5 1.6 collective-permute-done.13
  314.9 1.2 add_convert_fusion.2
  316.1 2.2 add_convert_fusion.1
  318.6 1.4 copy-done.5
  320.0 2.2 add_convert_fusion
  322.2 2.9 fusion.6
  325.2 45.7 %attention_back.2 = (bf16[3,4,512,128]{3,2,1,0:T(8,128)(2,1)}, bf16[3,2,4,512,128]{4,3,2,1,0:T(8,128)(2,1)}, bf16[3,2,4,512,128]{4,3,2,1,0:T(8,128)(2,1)}) custom-call(s32[4]{0:T(128)} %pad_add_fusion.scal_ref, bf16[3,4,512,128]{3,2,1,0:T(8,128)(2,1)} %get-tuple-element.116.q_ref, bf16[3,2,4,512,128]{4,3,2,1,0:T(8,128)(2,1)} %get-tuple-element.117.own_ref, ...), custom_call_target="tpu_custom_call" | custom-call | tf_op jit(solution)/shard_map/attention_back/pallas_call | solution.py:420
  371.1 45.6 %attention_back.3 = (bf16[3,4,512,128]{3,2,1,0:T(8,128)(2,1)}, bf16[3,2,4,512,128]{4,3,2,1,0:T(8,128)(2,1)}, bf16[3,2,4,512,128]{4,3,2,1,0:T(8,128)(2,1)}) custom-call(s32[4]{0:T(128)} %pad_add_fusion.scal_ref, bf16[3,4,512,128]{3,2,1,0:T(8,128)(2,1)} %get-tuple-element.121.q_ref, bf16[3,2,4,512,128]{4,3,2,1,0:T(8,128)(2,1)} %get-tuple-element.119.own_ref, ...), custom_call_target="tpu_custom_call" | custom-call | tf_op jit(solution)/shard_map/attention_back/pallas_call | solution.py:420
  417.3 1.6 constant_dynamic-slice_fusion.1
  419.0 3.7 collective-permute-done.14.add_own
  422.7 34.7 %project_back.1 = (bf16[4,512,768]{2,1,0:T(8,128)(2,1)}, bf16[768,1152]{1,0:T(8,128)(2,1)}, bf16[768,1152]{1,0:T(8,128)(2,1)}) custom-call(bf16[3,4,512,128]{3,2,1,0:T(8,128)(2,1)} %get-tuple-element.132.gq_own, bf16[3,2,4,512,128]{4,3,2,1,0:T(8,128)(2,1)} %get-tuple-element.133.gkv_own, bf16[3,2,4,512,128]{4,3,2,1,0:T(8,128)(2,1)} %collective-permute-done.14.add_own, ...), custom_call_target="tpu_custom_call" | custom-call | tf_op jit(solution)/shard_map/project_back/pallas_call | solution.py:835
  457.4 1.1 slice_select_fusion
  460.7 26.5 %back.1 = (bf16[2048,768]{1,0:T(8,128)(2,1)}, f32[2,8,768]{2,1,0:T(8,128)}, f32[16,768]{1,0:T(8,128)}) custom-call(s32[4]{0:T(128)} %pad_add_fusion.scal_ref, bf16[4,512,768]{2,1,0:T(8,128)(2,1)} %get-tuple-element.115.x_ref, bf16[4,512,768]{2,1,0:T(8,128)(2,1)} %get-tuple-element.148.gmixed_ref, bf16[4,32,768]{2,1,0:T(8,128)(2,1)} %copy-done.10, ...), custom_call_target="tpu_custom_call" | custom-call | tf_op jit(solution)/shard_map/back/pallas_call | solution.py:918
  487.2 0.8 slice.269
  488.0 0.8 fusion.19
  489.7 0.8 copy.124
  490.5 0.8 copy.125
  491.9 43.9 %reduce_gather.1 = (f32[48,1152]{1,0:T(8,128)}, f32[16,256]{1,0:T(8,128)}, bf16[2,2,2,4,16,896]{5,4,3,2,1,0:T(8,128)(2,1)}) custom-call(bf16[4,2,2,48,1152]{4,3,2,1,0:T(8,128)(2,1)} %bitcast.101, bf16[4,2,2,16,256]{4,3,2,1,0:T(8,128)(2,1)} %bitcast.107, bf16[4,2,2,48,1152]{4,3,2,1,0:T(8,128)(2,1)} %bitcast.102, bf16[4,2,2,16,256]{4,3,2,1,0:T(8,128)(2,1)} %bitcast.108, ...), custom_call_target="tpu_custom_call" | custom-call | tf_op jit(solution)/shard_map/reduce_gather/pallas_call | solution.py:1090
  535.9 1.2 slice.176
  537.1 0.9 slice.190
  538.0 1.2 slice.177
  540.1 2.1 copy.131
  543.1 0.8 copy.159
  543.9 0.7 slice_reduce_fusion
  544.7 0.7 copy.147
  545.4 0.7 fusion.8
  546.1 0.9 convolution_bitcast_fusion.refs_1_
  547.0 0.7 slice.193
  547.9 0.7 copy.148
  548.6 10.6 %square_sum.1.square_ref = f32[8,128]{1,0:T(8,128)} custom-call(f32[24,4608]{1,0:T(8,128)} %bitcast.94, f32[24,1000]{1,0:T(8,128)} %convolution_bitcast_fusion.refs_1_, f32[9,24]{1,0:T(8,128)} %bitcast.110, f32[48,1152]{1,0:T(8,128)} %get-tuple-element.160.refs_3_, bf16[224,768]{1,0:T(8,128)(2,1)} %bitcast.104), custom_call_target="tpu_custom_call" | custom-call | tf_op jit(solution)/shard_map/square_sum/pallas_call | solution.py:1165
  559.3 1.2 slice.166
  561.1 6.0 %adamw.1 = (f32[24,4608]{1,0:T(8,128)}, f32[24,4608]{1,0:T(8,128)}, f32[24,4608]{1,0:T(8,128)}, bf16[24,4608]{1,0:T(8,128)(2,1)}, f32[24,1000]{1,0:T(8,128)}, /*...) custom-call(f32[8,128]{1,0:T(8,128)} %square_sum.1.square_ref, ...), custom_call_target="tpu_custom_call" | custom-call | tf_op jit(solution)/shard_map/adamw/pallas_call | solution.py:1226
  (119 shorter events, 17.9 us)
Async XLA Ops:
  7.2 3.8 copy-start
  7.2 539.8 %reduce-scatter.2.cloned.1.call-start = ((), (), s32[]{:S(2)}) async-start(), calls=%async_computation.1 | async-start | bytes 5849088 | tf_op jit(solution)/shard_map/reduce_scatter | solution.py:1346
  8.4 11.6 %collective-permute-start = (bf16[128,768]{1,0:T(8,128)(2,1)S(1)}, bf16[128,768]{1,0:T(8,128)(2,1)S(1)}, u32[]{:S(2)}, u32[]{:S(2)}) collective-permute-start(bf16[128,768]{1,0:T(8,128)(2,1)S(1)} %slice_select_fusion.3), channel_id=1, source_target_pairs={{0,1},{1,0},{2,3},{3,2},{4,5},{5,4},{6,7},{7,6},{8,9},{9,8},{10,11... | collective-permute-start | bytes 589832 | tf_op jit(solution)/shard_map/ppermute | solution.py:1282
  9.0 35.0 %collective-permute-start.1 = (bf16[768,1152]{1,0:T(8,128)(2,1)}, bf16[768,1152]{1,0:T(8,128)(2,1)}, u32[]{:S(2)}, u32[]{:S(2)}) collective-permute-start(bf16[768,1152]{1,0:T(8,128)(2,1)} %own_ref.5), channel_id=1, source_target_pairs={{0,1},{1,0},{2,3},{3,2},{4,5},{5,4},{6,7},{7,6},{8,9},{9,8},{10,11... | collective-permute-start | bytes 5308424 | tf_op jit(solution)/shard_map/ppermute | solution.py:1282
  11.8 4.7 copy-start.16
  20.0 0.7 copy-start.12
  43.6 11.4 %collective-permute-start.3 = (bf16[3,2,4,512,128]{4,3,2,1,0:T(8,128)(2,1)}, bf16[3,2,4,512,128]{4,3,2,1,0:T(8,128)(2,1)S(1)}, u32[]{:S(2)}, u32[]{:S(2)}) collective-permute-start(bf16[3,2,4,512,128]{4,3,2,1,0:T(8,128)(2,1)} %get-tuple-element.117.own_ref), channel_id=1, source_target_pairs={{0,1},{1,0},{2,3},{3,2},{4,5},{5,4},{6,7},{7,6},{8,9},{9,8},{10,11... | collective-permute-start | bytes 9437192 | tf_op jit(solution)/shard_map/ppermute | solution.py:1282
  53.9 26.5 %collective-permute-start.2 = (bf16[3,2,4,512,128]{4,3,2,1,0:T(8,128)(2,1)}, bf16[3,2,4,512,128]{4,3,2,1,0:T(8,128)(2,1)}, u32[]{:S(2)}, u32[]{:S(2)}) collective-permute-start(bf16[3,2,4,512,128]{4,3,2,1,0:T(8,128)(2,1)} %get-tuple-element.119.own_ref), channel_id=1, source_target_pairs={{0,1},{1,0},{2,3},{3,2},{4,5},{5,4},{6,7},{7,6},{8,9},{9,8},{10,11... | collective-permute-start | bytes 9437192 | tf_op jit(solution)/shard_map/ppermute | solution.py:1282
  54.0 69.5 %collective-permute-start.8 = (bf16[768,1536]{1,0:T(8,128)(2,1)}, bf16[768,1536]{1,0:T(8,128)(2,1)}, u32[]{:S(2)}, u32[]{:S(2)}) collective-permute-start(bf16[768,1536]{1,0:T(8,128)(2,1)} %up_own.1), channel_id=1, source_target_pairs={{0,1},{1,0},{2,3},{3,2},{4,5},{5,4},{6,7},{7,6},{8,9},{9,8},{10,11... | collective-permute-start | bytes 7077896 | tf_op jit(solution)/shard_map/ppermute | solution.py:1282
  54.5 69.1 %collective-permute-start.9 = (bf16[1536,768]{1,0:T(8,128)(2,1)}, bf16[1536,768]{1,0:T(8,128)(2,1)}, u32[]{:S(2)}, u32[]{:S(2)}) collective-permute-start(bf16[1536,768]{1,0:T(8,128)(2,1)} %down_own.1), channel_id=1, source_target_pairs={{0,1},{1,0},{2,3},{3,2},{4,5},{5,4},{6,7},{7,6},{8,9},{9,8},{10,11... | collective-permute-start | bytes 7077896 | tf_op jit(solution)/shard_map/ppermute | solution.py:1282
  54.5 49.7 %collective-permute-start.4 = (bf16[384,768]{1,0:T(8,128)(2,1)}, bf16[384,768]{1,0:T(8,128)(2,1)}, u32[]{:S(2)}, u32[]{:S(2)}) collective-permute-start(bf16[384,768]{1,0:T(8,128)(2,1)} %own_ref.4), channel_id=1, source_target_pairs={{0,1},{1,0},{2,3},{3,2},{4,5},{5,4},{6,7},{7,6},{8,9},{9,8},{10,11... | collective-permute-start | bytes 1769480 | tf_op jit(solution)/shard_map/ppermute | solution.py:1282
  55.0 1.7 copy-start.2
  104.2 18.0 %copy-start.15 = (bf16[1536,9]{0,1:T(8,128)(2,1)S(1)}, bf16[1536,9]{0,1:T(8,128)(2,1)}, u32[]{:S(2)}) copy-start(bf16[1536,9]{0,1:T(8,128)(2,1)} %param.48) | copy-start | bytes 82948
  120.5 3.0 collective-permute-start.6
  121.7 1.9 collective-permute-start.7
  122.2 1.4 copy-start.11
  122.2 1.3 collective-permute-start.5
  123.5 0.6 copy-start.14
  123.5 0.7 copy-start.8
  124.2 0.7 copy-start.9
  292.3 23.8 %collective-permute-start.10 = (bf16[2,768,768]{2,1,0:T(8,128)(2,1)}, bf16[2,768,768]{2,1,0:T(8,128)(2,1)}, u32[]{:S(2)}, u32[]{:S(2)}) collective-permute-start(bf16[2,768,768]{2,1,0:T(8,128)(2,1)} %get-tuple-element.135), channel_id=1, source_target_pairs={{0,1},{1,0},{2,3},{3,2},{4,5},{5,4},{6,7},{7,6},{8,9},{9,8},{10,11... | collective-permute-start | bytes 7077896 | tf_op jit(solution)/shard_map/ppermute | solution.py:1282
  292.7 25.9 %collective-permute-start.11 = (bf16[1536,768]{1,0:T(8,128)(2,1)}, bf16[1536,768]{1,0:T(8,128)(2,1)}, u32[]{:S(2)}, u32[]{:S(2)}) collective-permute-start(bf16[1536,768]{1,0:T(8,128)(2,1)} %get-tuple-element.137), channel_id=1, source_target_pairs={{0,1},{1,0},{2,3},{3,2},{4,5},{5,4},{6,7},{7,6},{8,9},{9,8},{10,11... | collective-permute-start | bytes 7077896 | tf_op jit(solution)/shard_map/ppermute | solution.py:1282
  292.9 19.4 %copy-start.13 = (f32[12,16,256]{2,1,0:T(8,128)S(1)}, f32[12,16,256]{2,1,0:T(8,128)}, u32[]{:S(2)}) copy-start(f32[12,16,256]{2,1,0:T(8,128)} %get-tuple-element.140) | copy-start | bytes 589828
  311.9 4.2 copy-start.6
  311.9 3.0 collective-permute-start.12
  312.3 1.8 collective-permute-start.13
  318.3 1.7 copy-start.5
  370.8 48.1 %collective-permute-start.15 = (bf16[3,2,4,512,128]{4,3,2,1,0:T(8,128)(2,1)}, bf16[3,2,4,512,128]{4,3,2,1,0:T(8,128)(2,1)S(1)}, u32[]{:S(2)}, u32[]{:S(2)}) collective-permute-start(bf16[3,2,4,512,128]{4,3,2,1,0:T(8,128)(2,1)} %get-tuple-element.147), channel_id=1, source_target_pairs={{0,1},{1,0},{2,3},{3,2},{4,5},{5,4},{6,7},{7,6},{8,9},{9,8},{10,11... | collective-permute-start | bytes 9437192 | tf_op jit(solution)/shard_map/ppermute | solution.py:1282
  371.1 47.8 %copy-start.17 = (f32[2,8,768]{2,1,0:T(8,128)S(1)}, f32[2,8,768]{2,1,0:T(8,128)}, u32[]{:S(2)}) copy-start(f32[2,8,768]{2,1,0:T(8,128)} %get-tuple-element.157) | copy-start | bytes 147460
  416.7 6.0 %collective-permute-start.14 = (bf16[3,2,4,512,128]{4,3,2,1,0:T(8,128)(2,1)}, bf16[3,2,4,512,128]{4,3,2,1,0:T(8,128)(2,1)}, u32[]{:S(2)}, u32[]{:S(2)}) collective-permute-start(bf16[3,2,4,512,128]{4,3,2,1,0:T(8,128)(2,1)} %get-tuple-element.144), channel_id=1, source_target_pairs={{0,1},{1,0},{2,3},{3,2},{4,5},{5,4},{6,7},{7,6},{8,9},{9,8},{10,11... | collective-permute-start | bytes 9437192 | tf_op jit(solution)/shard_map/ppermute | solution.py:1282
  419.0 3.7 copy-start.4
  458.5 1.5 collective-permute-start.16
  460.0 0.7 copy-start.10
  535.9 6.8 %copy-start.3 = (bf16[2,2,2,4,16,896]{5,4,3,2,1,0:T(8,128)(2,1)S(1)}, bf16[2,2,2,4,16,896]{5,4,3,2,1,0:T(8,128)(2,1)}, u32[]{:S(2)}) copy-start(bf16[2,2,2,4,16,896]{5,4,3,2,1,0:T(8,128)(2,1)} %get-tuple-element.158) | copy-start | bytes 2752516
  542.1 3.2 copy-start.7
  548.6 18.5 %copy-start.1 = (bf16[768,1000]{0,1:T(8,128)(2,1)S(1)}, bf16[768,1000]{0,1:T(8,128)(2,1)}, u32[]{:S(2)}) copy-start(bf16[768,1000]{0,1:T(8,128)(2,1)} %param.43) | copy-start | bytes 4608004
Sparse Core Ops, SparseCore 0:
  325.3 143.8 reduce-scatter.1
